TPU v7x, 32 devices: a whole 2x2x4 slice. The times are simulated.
32 devices in a mesh: dp: 4 (over y, core), ctx: 2 (over x), tp: 4 (over z).
Axes of the slice: x: 2, y: 2, z: 4, core: 2. Of those that a mesh axis runs over, the one named last changes fastest.
Arguments:
- hidden_in: bfloat16 [4, 5120, 1024], P('dp', ('ctx', 'tp')), may hold values from -6 to 6
- cotangent: bfloat16 [4, 5120, 1024], P('dp', ('ctx', 'tp')), may hold values from -6 to 6
- pic_starts: int32 [4, 4], P('dp'), may hold values from 0 to 4864, as said below
- norm_mixer: bfloat16 [1024], replicated, may hold values from 0.5 to 1.5
- w_query: bfloat16 [1024, 512], P(('dp', 'ctx'), 'tp'), may hold values from -0.1875 to 0.1875
- w_key: bfloat16 [1024, 512], P(('dp', 'ctx'), 'tp'), may hold values from -0.1875 to 0.1875
- w_value: bfloat16 [1024, 1024], P(('dp', 'ctx'), 'tp'), may hold values from -0.1875 to 0.1875
- w_outgate: bfloat16 [1024, 1024], P(('dp', 'ctx'), 'tp'), may hold values from -0.1875 to 0.1875
- w_rank_in: bfloat16 [1024, 16], replicated, may hold values from -0.1875 to 0.1875
- w_rank_out: bfloat16 [16, 512], replicated, may hold values from -1.5 to 1.5
- gate_bias: bfloat16 [512], replicated, may hold values from -2 to 6
- group_gain: bfloat16 [256], replicated, may hold values from 0.5 to 1.5
- w_output: bfloat16 [1024, 1024], P('tp', ('dp', 'ctx')), may hold values from -0.1875 to 0.1875
- norm_ffn: bfloat16 [1024], replicated, may hold values from 0.5 to 1.5
- w_gate: bfloat16 [1024, 2816], P(('dp', 'ctx'), 'tp'), may hold values from -0.1875 to 0.1875
- w_up: bfloat16 [1024, 2816], P(('dp', 'ctx'), 'tp'), may hold values from -0.1875 to 0.1875
- w_down: bfloat16 [2816, 1024], P('tp', ('dp', 'ctx')), may hold values from -0.109375 to 0.109375
Outputs:
- hidden_out: bfloat16 [4, 5120, 1024], P('dp', ('ctx', 'tp'))
- grad_in: float32 [4, 5120, 1024], P('dp', ('ctx', 'tp'))
- grad_norm_mixer: float32 [1024], replicated
- grad_query: float32 [1024, 512], P(('dp', 'ctx'), 'tp')
- grad_key: float32 [1024, 512], P(('dp', 'ctx'), 'tp')
- grad_value: float32 [1024, 1024], P(('dp', 'ctx'), 'tp')
- grad_outgate: float32 [1024, 1024], P(('dp', 'ctx'), 'tp')
- grad_rank_in: float32 [1024, 16], replicated
- grad_rank_out: float32 [16, 512], replicated
- grad_gate_bias: float32 [512], replicated
- grad_group_gain: float32 [256], replicated
- grad_output: float32 [1024, 1024], P('tp', ('dp', 'ctx'))
- grad_norm_ffn: float32 [1024], replicated
- grad_gate: float32 [1024, 2816], P(('dp', 'ctx'), 'tp')
- grad_up: float32 [1024, 2816], P(('dp', 'ctx'), 'tp')
- grad_down: float32 [2816, 1024], P('tp', ('dp', 'ctx'))
Inputs may be any that keep to these rules, and one draw needn't show every extreme that they name: `pic_starts`: each row holds 4 different multiples of 256; a picture piece is the 256 tokens from its start on.
All inputs are finite; a program needn't handle non-finite values.
Results may differ from a plain program's by a relative error of at most 0.025.
Values may be sent and summed in bfloat16 or wider, within the bound.
No kernel may reach another device: no remote copies, remote signals or barrier semaphores. Data moves between devices by JAX's collectives and lax.ppermute only.
A program may use at most 256 MiB of HBM per device.

v0:
```python
import jax
import jax.numpy as jnp
from jax import lax
from jax.sharding import PartitionSpec as P

DK = 128
DV = 256
RANK = 16
SPAN = 64
PIECE = 256


EPSILON = 1e-06
MIXER_PRECISION = lax.Precision.HIGH
GATE_NORM = 16.0


def entering(array, axis, join, neutral):
    place = lax.axis_index(axis)
    gathered = jax.tree.map(
        lambda a, kind: lax.all_gather(a.astype(kind), axis), array, (jnp.bfloat16, jnp.bfloat16)
    )
    state = jax.tree.map(lambda a, e: jnp.zeros_like(a) + jnp.asarray(e, a.dtype), array, neutral)

    def one(turn, state):
        return join(
            state,
            jax.tree.map(
                lambda a, own: lax.dynamic_index_in_dim(a, turn, 0, False).astype(own.dtype),
                gathered,
                array,
            ),
        )

    return lax.fori_loop(0, place, one, state)


def entering_2(array, axis, join, neutral):
    count = lax.axis_size(axis)
    place = lax.axis_index(axis)
    ahead = count - 1 - place
    gathered = jax.tree.map(
        lambda a, kind: lax.all_gather(a.astype(kind), axis),
        array,
        jax.tree.map(lambda a: jnp.bfloat16 if a.dtype == jnp.float32 else a.dtype, array),
    )
    state = jax.tree.map(lambda a, e: jnp.zeros_like(a) + jnp.asarray(e, a.dtype), array, neutral)

    def one(turn, state):
        source = count - 1 - turn
        return join(
            state,
            jax.tree.map(
                lambda a, own: lax.dynamic_index_in_dim(a, source, 0, False).astype(own.dtype),
                gathered,
                array,
            ),
        )

    return lax.fori_loop(0, ahead, one, state)


def block_causal(carried, inputs):
    queries, key_rows, value_rows, decays = inputs
    block_end = decays[-1]
    block_size = queries.shape[0]
    causal = (jnp.arange(block_size)[:, None] >= jnp.arange(block_size)[None, :]).astype(
        queries.dtype
    )
    query_decayed = queries * jnp.exp(decays)
    key_decayed = key_rows * jnp.exp(-decays)
    scores = (
        jnp.einsum("thd,shd->hts", query_decayed, key_decayed, precision=MIXER_PRECISION) * causal
    )
    within = jnp.einsum("hts,she->the", scores, value_rows, precision=MIXER_PRECISION)
    earlier = jnp.einsum("thd,hde->the", query_decayed, carried, precision=MIXER_PRECISION)
    key_final = key_rows * jnp.exp(block_end - decays)
    updated = jnp.exp(block_end)[:, :, None] * carried + jnp.einsum(
        "thd,the->hde", key_final, value_rows, precision=MIXER_PRECISION
    )
    return (updated, within + earlier)


def block_future(carried, inputs):
    queries, key_rows, value_rows, decays, picture = inputs
    block_end = decays[-1]
    block_size = queries.shape[0]
    above = (jnp.arange(block_size)[:, None] < jnp.arange(block_size)[None, :]).astype(
        queries.dtype
    )
    query_decayed = queries * jnp.exp(-decays)
    key_decayed = key_rows * jnp.exp(decays)
    scores = (
        jnp.einsum("thd,shd->hts", query_decayed, key_decayed, precision=MIXER_PRECISION) * above
    )
    within = jnp.einsum("hts,she->the", scores, value_rows, precision=MIXER_PRECISION)
    later = jnp.einsum(
        "thd,hde->the", queries * jnp.exp(block_end - decays), carried, precision=MIXER_PRECISION
    )
    updated = jnp.exp(block_end)[:, :, None] * carried + jnp.einsum(
        "thd,the->hde", key_decayed, value_rows, precision=MIXER_PRECISION
    )
    return (updated, picture * (within + later))


def split_blocks(values):
    return values.reshape(values.shape[0] // SPAN, SPAN, *values.shape[1:])


def by_piece(values):
    group = PIECE // SPAN
    return values.reshape(values.shape[0] // group, group, *values.shape[1:])


def piece_future(start_state, scaled, key_blocks, value_blocks, decays, picture):

    def one_piece(piece_queries, piece_keys, piece_values, piece_decays, piece_mask):
        return lax.scan(
            jax.checkpoint(block_future),
            start_state,
            (piece_queries, piece_keys, piece_values, piece_decays, piece_mask),
            reverse=True,
        )[1]

    future_out = jax.vmap(one_piece)(
        by_piece(scaled),
        by_piece(key_blocks),
        by_piece(value_blocks),
        by_piece(decays),
        by_piece(picture),
    )
    return future_out.reshape(scaled.shape[0], *future_out.shape[2:])


def sequence_mixer(queries, key_rows, value_rows, gate_log, picture):
    scaled = split_blocks(queries * DK ** (-0.5))
    key_blocks = split_blocks(key_rows)
    value_blocks = split_blocks(value_rows)
    decays = jnp.cumsum(split_blocks(gate_log), axis=1)
    start_state = jnp.zeros(
        (queries.shape[1], queries.shape[2], value_rows.shape[2]), queries.dtype
    )
    final_state, causal_out = lax.scan(
        jax.checkpoint(block_causal), start_state, (scaled, key_blocks, value_blocks, decays)
    )
    future_out = piece_future(start_state, scaled, key_blocks, value_blocks, decays, picture)
    mixed = (causal_out + future_out).reshape(value_rows.shape)
    return (mixed, final_state, scaled, decays)


def shard_mixer(queries, key_rows, value_rows, gate_log, picture):
    mixed, final_state, scaled, decays = sequence_mixer(
        queries, key_rows, value_rows, gate_log, picture
    )
    block_ends = decays[:, -1]
    shifted = jnp.concatenate([jnp.zeros_like(block_ends[:1]), block_ends[:-1]], axis=0)
    before = jnp.cumsum(shifted, axis=0)
    query_decay = (scaled * jnp.exp(before[:, None] + decays)).reshape(queries.shape)
    total_log = jnp.sum(block_ends, axis=0)
    return (mixed, final_state, query_decay, total_log)


def chain_states(earlier, later):
    return (earlier[0] * later[0], earlier[1] * later[0][..., None] + later[1])


def rms_scale(values):
    return lax.rsqrt(jnp.mean(values * values, axis=-1, keepdims=True) + EPSILON)


def norm_back(upstream, values, scale, gain):
    weighted = upstream * gain
    return scale * weighted - values * scale**3 * jnp.mean(
        weighted * values, axis=-1, keepdims=True
    )


def swish_slope(gate_value, sigmoid_value):
    return sigmoid_value * (1.0 + gate_value * (1.0 - sigmoid_value))


def times_transposed(left, right):
    return lax.dot_general(
        left, right, (((1,), (1,)), ((), ())), preferred_element_type=jnp.float32
    )


def transposed_times(left, right):
    return lax.dot_general(
        left, right, (((0,), (0,)), ((), ())), preferred_element_type=jnp.float32
    )


def on_device(
    hidden_in,
    cotangent,
    pic_starts,
    norm_mixer,
    w_query,
    w_key,
    w_value,
    w_outgate,
    w_rank_in,
    w_rank_out,
    gate_bias,
    group_gain,
    w_output,
    norm_ffn,
    w_gate,
    w_up,
    w_down,
):
    seq_count, part_rows, model_width = hidden_in.shape
    head_devices = lax.axis_size("tp")
    full_rows = part_rows * head_devices
    row_count = seq_count * full_rows
    head_slot = lax.axis_index("tp")
    key_width = w_query.shape[1]
    value_width = w_value.shape[1]
    heads_here = key_width // DK
    gathered = (
        lax.all_gather(w_query, ("dp", "ctx"), axis=0, tiled=True),
        lax.all_gather(w_key, ("dp", "ctx"), axis=0, tiled=True),
        lax.all_gather(w_value, ("dp", "ctx"), axis=0, tiled=True),
        lax.all_gather(w_outgate, ("dp", "ctx"), axis=0, tiled=True),
        lax.all_gather(w_gate, ("dp", "ctx"), axis=0, tiled=True),
        lax.all_gather(w_up, ("dp", "ctx"), axis=0, tiled=True),
        lax.all_gather(w_output, ("dp", "ctx"), axis=1, tiled=True),
        lax.all_gather(w_down, ("dp", "ctx"), axis=1, tiled=True),
    )
    full_query, full_key, full_value, full_outgate, full_gate, full_up, full_output, full_down = (
        gathered
    )
    rank_out = lax.dynamic_slice_in_dim(w_rank_out, head_slot * key_width, key_width, 1)
    bias_here = lax.dynamic_slice_in_dim(gate_bias, head_slot * key_width, key_width, 0).astype(
        jnp.float32
    )
    inputs = hidden_in.astype(jnp.float32)
    scale_one = rms_scale(inputs)
    gain_one = norm_mixer.astype(jnp.float32)
    normed = (inputs * scale_one * gain_one).astype(jnp.bfloat16)
    normed_whole, upstream_whole = (
        lax.all_gather(normed, "tp", axis=1, tiled=True),
        lax.all_gather(cotangent, "tp", axis=1, tiled=True),
    )
    normed_all = normed_whole.reshape(row_count, model_width)
    upstream = upstream_whole.reshape(row_count, model_width)

    def project(weight):
        return jnp.dot(normed_all, weight, preferred_element_type=jnp.float32)

    queries = project(full_query).astype(jnp.bfloat16)
    key_rows = project(full_key).astype(jnp.bfloat16)
    value_rows = project(full_value).astype(jnp.bfloat16)
    outgate = project(full_outgate)
    rank_low = project(w_rank_in).astype(jnp.bfloat16)
    gate_in = jnp.dot(rank_low, rank_out, preferred_element_type=jnp.float32) + bias_here
    gate_log = jax.nn.log_sigmoid(gate_in) / GATE_NORM

    def per_head(values, inner_size):
        return values.astype(jnp.float32).reshape(seq_count, full_rows, heads_here, inner_size)

    block_count = full_rows // SPAN
    positions = lax.axis_index("ctx") * full_rows + jnp.arange(block_count, dtype=jnp.int32) * SPAN
    in_piece = (positions[None, :, None] >= pic_starts[:, None, :]) & (
        positions[None, :, None] < pic_starts[:, None, :] + PIECE
    )
    picture = jnp.any(in_piece, axis=2).astype(jnp.float32)

    def local_mix(queries_in, keys_in, values_in, gates_in):
        return jax.vmap(shard_mixer, in_axes=(0, 0, 0, 0, 0))(
            queries_in, keys_in, values_in, gates_in, picture
        )

    mix_parts, mix_back = jax.vjp(
        local_mix,
        per_head(queries, DK),
        per_head(key_rows, DK),
        per_head(value_rows, DV),
        per_head(gate_log, DK),
    )
    mixed_local, final_state, query_decay, total_log = mix_parts
    decay_total = jnp.exp(total_log)
    identity = (jnp.ones_like(decay_total), jnp.zeros_like(final_state))
    incoming = entering((decay_total, final_state), "ctx", chain_states, identity)[1]
    mixed = mixed_local + jnp.einsum(
        "sthd,shde->sthe", query_decay, incoming, precision=MIXER_PRECISION
    )
    gate_out = outgate.reshape(seq_count, full_rows, heads_here, DV)
    scale_group = rms_scale(mixed)
    group_weight = group_gain.astype(jnp.float32)
    grouped = mixed * scale_group * group_weight
    gate_sigma = jax.nn.sigmoid(gate_out)
    gated = (grouped * gate_out * gate_sigma).astype(jnp.bfloat16).reshape(row_count, value_width)
    branch = jnp.dot(gated, full_output, preferred_element_type=jnp.float32).reshape(
        seq_count, full_rows, model_width
    )
    mixer_sum = lax.psum_scatter(
        branch.astype(jnp.bfloat16), "tp", scatter_dimension=1, tiled=True
    ).astype(jnp.float32)
    residual = inputs + mixer_sum
    scale_two = rms_scale(residual)
    gain_two = norm_ffn.astype(jnp.float32)
    normed_two = (residual * scale_two * gain_two).astype(jnp.bfloat16)
    feed_rows = lax.all_gather(normed_two, "tp", axis=1, tiled=True).reshape(row_count, model_width)
    gate_pre = jnp.dot(feed_rows, full_gate, preferred_element_type=jnp.float32)
    up_pre = jnp.dot(feed_rows, full_up, preferred_element_type=jnp.float32)
    sigma_pre = jax.nn.sigmoid(gate_pre)
    silu_gate = gate_pre * sigma_pre
    activation = (silu_gate * up_pre).astype(jnp.bfloat16)
    feed_part = jnp.dot(activation, full_down, preferred_element_type=jnp.float32).reshape(
        seq_count, full_rows, model_width
    )
    feed_sum = lax.psum_scatter(
        feed_part.astype(jnp.bfloat16), "tp", scatter_dimension=1, tiled=True
    ).astype(jnp.float32)
    hidden_out = (residual + feed_sum).astype(jnp.bfloat16)
    d_activation = times_transposed(upstream, full_down)
    grad_down = transposed_times(activation, upstream)
    d_gate = (d_activation * up_pre * swish_slope(gate_pre, sigma_pre)).astype(jnp.bfloat16)
    d_up = (d_activation * silu_gate).astype(jnp.bfloat16)
    grad_gate = transposed_times(feed_rows, d_gate)
    grad_up = transposed_times(feed_rows, d_up)
    d_normed_two = (times_transposed(d_gate, full_gate) + times_transposed(d_up, full_up)).reshape(
        seq_count, full_rows, model_width
    )
    d_norm_two = lax.psum_scatter(
        d_normed_two.astype(jnp.bfloat16), "tp", scatter_dimension=1, tiled=True
    ).astype(jnp.float32)
    grad_ffn_term = jnp.sum(d_norm_two * residual * scale_two, axis=(0, 1))
    d_resid = cotangent.astype(jnp.float32) + norm_back(d_norm_two, residual, scale_two, gain_two)
    d_branch = lax.all_gather(d_resid.astype(jnp.bfloat16), "tp", axis=1, tiled=True).reshape(
        row_count, model_width
    )
    grad_output = transposed_times(gated, d_branch)
    d_gated = times_transposed(d_branch, full_output).reshape(seq_count, full_rows, heads_here, DV)
    d_grouped = d_gated * gate_out * gate_sigma
    d_outgate = (
        (d_gated * grouped * swish_slope(gate_out, gate_sigma))
        .astype(jnp.bfloat16)
        .reshape(row_count, value_width)
    )
    grad_group_term = jnp.sum(d_grouped * mixed * scale_group, axis=(0, 1, 2))
    d_mixed = norm_back(d_grouped, mixed, scale_group, group_weight)
    d_query_decay = jnp.einsum("sthe,shde->sthd", d_mixed, incoming, precision=MIXER_PRECISION)
    d_incoming = jnp.einsum("sthd,sthe->shde", query_decay, d_mixed, precision=MIXER_PRECISION)
    d_final = entering_2((decay_total, d_incoming), "ctx", chain_states, identity)[1]
    d_total = jnp.sum(incoming * d_final, axis=-1) * decay_total
    d_queries, d_keys, d_values, d_gates = mix_back((d_mixed, d_final, d_query_decay, d_total))
    d_queries = d_queries.astype(jnp.bfloat16).reshape(row_count, key_width)
    d_keys = d_keys.astype(jnp.bfloat16).reshape(row_count, key_width)
    d_values = d_values.astype(jnp.bfloat16).reshape(row_count, value_width)
    d_gate_in = (
        d_gates.reshape(row_count, key_width) * jax.nn.sigmoid(-gate_in) / GATE_NORM
    ).astype(jnp.bfloat16)
    grad_bias_here = jnp.sum(d_gate_in.astype(jnp.float32), axis=0)
    grad_rank_here = transposed_times(rank_low, d_gate_in)
    d_rank_part = times_transposed(d_gate_in, rank_out).reshape(seq_count, full_rows, RANK)
    grad_query = transposed_times(normed_all, d_queries)
    grad_key = transposed_times(normed_all, d_keys)
    grad_value = transposed_times(normed_all, d_values)
    grad_outgate = transposed_times(normed_all, d_outgate)
    d_normed = (
        times_transposed(d_queries, full_query)
        + times_transposed(d_keys, full_key)
        + times_transposed(d_values, full_value)
        + times_transposed(d_outgate, full_outgate)
    )
    d_normed = d_normed.reshape(seq_count, full_rows, model_width)
    d_norm_one, d_rank_sum = (
        lax.psum_scatter(
            d_normed.astype(jnp.bfloat16), "tp", scatter_dimension=1, tiled=True
        ).astype(jnp.float32),
        lax.psum_scatter(
            d_rank_part.astype(jnp.bfloat16), "tp", scatter_dimension=1, tiled=True
        ).astype(jnp.float32),
    )
    d_rank_low = d_rank_sum.astype(jnp.bfloat16).reshape(seq_count * part_rows, RANK)
    d_norm_one = d_norm_one + times_transposed(d_rank_low, w_rank_in).reshape(d_norm_one.shape)
    grad_rank_in_term = transposed_times(
        normed.reshape(seq_count * part_rows, model_width), d_rank_low
    )
    grad_mixer_term = jnp.sum(d_norm_one * inputs * scale_one, axis=(0, 1))
    grad_in = d_resid + norm_back(d_norm_one, inputs, scale_one, gain_one)
    rank_out_full = lax.dynamic_update_slice_in_dim(
        jnp.zeros(w_rank_out.shape, jnp.float32), grad_rank_here, head_slot * key_width, 1
    )
    bias_full = lax.dynamic_update_slice_in_dim(
        jnp.zeros(gate_bias.shape, jnp.float32), grad_bias_here, head_slot * key_width, 0
    )
    shared = lax.psum(
        (
            grad_mixer_term,
            grad_rank_in_term,
            rank_out_full,
            bias_full,
            grad_group_term,
            grad_ffn_term,
        ),
        ("dp", "ctx", "tp"),
    )
    owned = (
        lax.psum_scatter(grad_query, ("dp", "ctx"), scatter_dimension=0, tiled=True),
        lax.psum_scatter(grad_key, ("dp", "ctx"), scatter_dimension=0, tiled=True),
        lax.psum_scatter(grad_value, ("dp", "ctx"), scatter_dimension=0, tiled=True),
        lax.psum_scatter(grad_outgate, ("dp", "ctx"), scatter_dimension=0, tiled=True),
        lax.psum_scatter(grad_gate, ("dp", "ctx"), scatter_dimension=0, tiled=True),
        lax.psum_scatter(grad_up, ("dp", "ctx"), scatter_dimension=0, tiled=True),
        lax.psum_scatter(grad_output, ("dp", "ctx"), scatter_dimension=1, tiled=True),
        lax.psum_scatter(grad_down, ("dp", "ctx"), scatter_dimension=1, tiled=True),
    )
    return (
        hidden_out,
        grad_in,
        shared[0],
        owned[0],
        owned[1],
        owned[2],
        owned[3],
        shared[1],
        shared[2],
        shared[3],
        shared[4],
        owned[6],
        shared[5],
        owned[4],
        owned[5],
        owned[7],
    )


def solution(mesh):
    return jax.shard_map(
        on_device,
        mesh=mesh,
        in_specs=(
            P("dp", ("ctx", "tp"), None),
            P("dp", ("ctx", "tp"), None),
            P("dp", None),
            P(),
            P(("dp", "ctx"), "tp"),
            P(("dp", "ctx"), "tp"),
            P(("dp", "ctx"), "tp"),
            P(("dp", "ctx"), "tp"),
            P(),
            P(),
            P(),
            P(),
            P("tp", ("dp", "ctx")),
            P(),
            P(("dp", "ctx"), "tp"),
            P(("dp", "ctx"), "tp"),
            P("tp", ("dp", "ctx")),
        ),
        out_specs=(
            P("dp", ("ctx", "tp"), None),
            P("dp", ("ctx", "tp"), None),
            P(),
            P(("dp", "ctx"), "tp"),
            P(("dp", "ctx"), "tp"),
            P(("dp", "ctx"), "tp"),
            P(("dp", "ctx"), "tp"),
            P(),
            P(),
            P(),
            P(),
            P("tp", ("dp", "ctx")),
            P(),
            P(("dp", "ctx"), "tp"),
            P(("dp", "ctx"), "tp"),
            P("tp", ("dp", "ctx")),
        ),
        check_vma=False,
    )
```

profile of v0, /device:TPU:12, one launch (start us, length us, event | category | flops | bytes accessed | tf_op | source)
XLA Modules:
  0.0 2083.4 jit_solution(13579970238931190562)
XLA Ops:
  14.9 16.4 all_gather.57
  31.3 16.9 all_gather.55
  48.3 19.5 all_gather.56
  67.8 19.0 all_gather.61
  86.7 19.4 all_gather.62
  106.2 5.0 all-gather.12.cloned.1.call-done
  111.2 3.9 fusion.212
  120.2 4.4 all-gather.3
  129.2 4.1 copy.209
  133.4 5.2 fusion.200
  138.6 5.5 fusion.256
  145.9 246.6 %while.104 = (s32[]{:T(128)}, f32[1,1,128,256]{3,2,1,0:T(8,128)S(1)}, f32[40,1,64,1,256]{4,2,3,1,0:T(8,128)}, f32[40,1,1,128,256]{4,3,2,1,0:T(8,128)}, f32[40,1,...) while((s32[]{:T(128)}, ...), condition=%wide.region_3.4_spmd.clone, body=%wide.region_2.3_spmd.clone.sunk | while | flops 34844672 | bytes 1480328 | solution.py:143
  392.6 4.9 all-gather.1
  397.8 3.3 copy.217
  412.0 35.5 %while.105 = (s32[]{:T(128)}, f32[1,10,1,128,256]{4,3,1,2,0:T(8,128)S(1)}, f32[4,1,10,64,1,256]{5,3,0,2,4,1:T(8,128)}, f32[4,1,10,1,128,256]{5,4,2,3,1,0:T(8,128...) while((s32[]{:T(128)}, ...), condition=%wide.region_6.7_spmd.clone, body=%wide.region_5.6_spmd.clone.sunk | while | flops 348536832 | bytes 24182032 | solution.py:118
  447.5 3.8 copy.218
  451.3 4.6 multiply_reduce_fusion.3
  456.0 3.7 fusion.241
  459.7 3.9 fusion.187
  464.3 94.3 %reduce-scatter.16.cloned.1.call-done = bf16[1,640,1024]{2,1,0:T(8,128)(2,1)} async-done(((bf16[1,2560,1024]{2,1,0:T(8,128)(2,1)}), bf16[1,640,1024]{2,1,0:T(8,128)(2,1)}) %reduce-scatter.16.cloned.1.call-update) | async-done | bytes 1310736 | tf_op jit(solution)/shard_map/reduce_scatter | solution.py:298
  564.8 93.3 %all-gather.14.cloned.1.call-done = bf16[1,2560,1024]{2,1,0:T(8,128)(2,1)} async-done(((bf16[1,640,1024]{2,1,0:T(8,128)(2,1)}), bf16[1,2560,1024]{2,1,0:T(8,128)(2,1)}) %all-gather.14.cloned.1.call-update) | async-done | bytes 5242896 | tf_op jit(solution)/shard_map/all_gather | solution.py:305
  658.1 9.7 fusion.166
  667.8 18.0 all-gather.18.cloned.1.call-done
  685.8 9.8 fusion.164
  695.6 17.2 all-gather.20.cloned.1.call-done
  712.8 97.1 %all-gather.22.cloned.1.call-done = bf16[1,2560,1024]{2,1,0:T(8,128)(2,1)} async-done(((bf16[1,640,1024]{2,1,0:T(8,128)(2,1)}), bf16[1,2560,1024]{2,1,0:T(8,128)(2,1)}) %all-gather.22.cloned.1.call-update) | async-done | bytes 5242896 | tf_op jit(solution)/shard_map/all_gather | solution.py:244
  809.9 13.8 multiply_convert_fusion
  823.8 4.3 fusion.281
  828.1 8.4 fusion.189
  836.6 94.8 %reduce-scatter.20.cloned.1.call-done = bf16[1,640,1024]{2,1,0:T(8,128)(2,1)} async-done(((bf16[1,2560,1024]{2,1,0:T(8,128)(2,1)}), bf16[1,640,1024]{2,1,0:T(8,128)(2,1)}) %reduce-scatter.20.cloned.1.call-update) | async-done | bytes 1310736 | tf_op jit(solution)/shard_map/reduce_scatter | solution.py:327
  931.5 3.1 fusion.222
  940.1 92.5 %all-gather.24.cloned.1.call-done = bf16[1,2560,1024]{2,1,0:T(8,128)(2,1)} async-done(((bf16[1,640,1024]{2,1,0:T(8,128)(2,1)}), bf16[1,2560,1024]{2,1,0:T(8,128)(2,1)}) %all-gather.24.cloned.1.call-update) | async-done | bytes 5242896 | tf_op jit(solution)/shard_map/all_gather | solution.py:332
  1032.7 9.6 fusion.234
  1049.0 4.9 all-gather.2
  1058.5 348.2 %while.103 = (s32[]{:T(128)}, f32[1,1,128,256]{2,3,1,0:T(8,128)S(1)}, f32[40,1,64,1,128]{4,2,3,1,0:T(8,128)}, f32[40,1,64,1,128]{4,2,3,1,0:T(8,128)}, f32[40,1,6...) while((s32[]{:T(128)}, ...), condition=%wide.region_27.28_spmd, body=%wide.region_24.27_spmd.sunk | while | flops 72785920 | bytes 3793089 | solution.py:143
  1409.1 68.5 %while.106 = (s32[]{:T(128)}, f32[1,10,1,128,256]{3,4,1,2,0:T(8,128)}, f32[4,1,10,64,1,128]{5,3,0,2,4,1:T(8,128)}, f32[4,1,10,64,1,128]{5,3,0,2,4,1:T(8,128)}, f...) while((s32[]{:T(128)}, ...), condition=%wide.region_21.22_spmd.clone, body=%wide.region_18.21_spmd.clone.sunk | while | flops 728768512 | bytes 38483380 | solution.py:118
  1477.7 3.4 copy.254
  1498.2 5.6 fusion.284
  1509.4 3.5 fusion.266
  1512.9 5.4 fusion.282
  1519.3 5.5 fusion.283
  1524.8 13.5 fusion.186
  1538.4 9.2 fusion.188
  1547.9 9.1 fusion.160
  1557.1 9.1 fusion.162
  1566.2 9.0 fusion.156
  1580.5 5.1 fusion.174
  1587.7 5.0 fusion.172
  1595.1 5.2 fusion.170
  1600.5 5.2 fusion.168
  1605.8 5.1 fusion.152
  1611.5 21.7 %reduce-scatter.22.cloned.1.call-done = bf16[1,640,1024]{2,1,0:T(8,128)(2,1)} async-done(((bf16[1,2560,1024]{2,1,0:T(8,128)(2,1)}), bf16[1,640,1024]{2,1,0:T(8,128)(2,1)}) %reduce-scatter.22.cloned.1.call-update) | async-done | bytes 1310736 | tf_op jit(solution)/shard_map/reduce_scatter | solution.py:371
  1633.2 3.8 fusion.231
  1637.0 44.8 %all-reduce.4 = (f32[1024]{0:T(1024)}, f32[16,512]{1,0:T(8,128)}, f32[512]{0:T(512)}, f32[256]{0:T(256)}, f32[1024]{0:T(1024)}) all-reduce(f32[1024]{0:T(1024)S(1)} %get-tuple-element.1054, f32[16,512]{1,0:T(8,128)S(1)} %convolution_dynamic-update-slice_fusion, ...), channel_id=1, replica_groups=mesh['dp'=4,'ctx'=2,'tp'=4] {'dp','ctx','tp'}, use_global_device_ids=true, to_apply=%region_36.37 | all-reduce | flops 11008 | bytes 88064 | tf_op jit(solution)/shard_map/psum | solution.py:391
  1681.8 49.0 %reduce-scatter.18.cloned.1.call-done = bf16[1,640,1024]{2,1,0:T(8,128)(2,1)} async-done(((bf16[1,2560,1024]{2,1,0:T(8,128)(2,1)}), bf16[1,640,1024]{2,1,0:T(8,128)(2,1)}) %reduce-scatter.18.cloned.1.call-update) | async-done | bytes 1310736 | tf_op jit(solution)/shard_map/reduce_scatter | solution.py:314
  1730.9 5.2 fusion.228
  1736.1 44.3 %reduce-scatter.34.cloned.1.call-done = f32[128,704]{0,1:T(8,128)} async-done(((f32[1024,704]{0,1:T(8,128)}), f32[128,704]{0,1:T(8,128)}) %reduce-scatter.34.cloned.1.call-update) | async-done | bytes 360464 | tf_op jit(solution)/shard_map/reduce_scatter | solution.py:407
  1780.4 49.2 %reduce-scatter.36.cloned.1.call-done = f32[128,704]{0,1:T(8,128)} async-done(((f32[1024,704]{0,1:T(8,128)}), f32[128,704]{0,1:T(8,128)}) %reduce-scatter.36.cloned.1.call-update) | async-done | bytes 360464 | tf_op jit(solution)/shard_map/reduce_scatter | solution.py:408
  1829.6 48.9 %reduce-scatter.38.cloned.1.call-done = f32[704,128]{1,0:T(8,128)} async-done(((f32[704,1024]{1,0:T(8,128)}), f32[704,128]{1,0:T(8,128)}) %reduce-scatter.38.cloned.1.call-update) | async-done | bytes 360464 | tf_op jit(solution)/shard_map/reduce_scatter | solution.py:410
  1878.5 37.9 %reduce-scatter.24.cloned.1.call-done = f32[128,128]{1,0:T(8,128)} async-done(((f32[1024,128]{1,0:T(8,128)}), f32[128,128]{1,0:T(8,128)}) %reduce-scatter.24.cloned.1.call-update) | async-done | bytes 65552 | tf_op jit(solution)/shard_map/reduce_scatter | solution.py:403
  1916.4 37.8 %reduce-scatter.26.cloned.1.call-done = f32[128,128]{1,0:T(8,128)} async-done(((f32[1024,128]{1,0:T(8,128)}), f32[128,128]{1,0:T(8,128)}) %reduce-scatter.26.cloned.1.call-update) | async-done | bytes 65552 | tf_op jit(solution)/shard_map/reduce_scatter | solution.py:404
  1954.2 40.0 %reduce-scatter.28.cloned.1.call-done = f32[128,256]{1,0:T(8,128)} async-done(((f32[1024,256]{1,0:T(8,128)}), f32[128,256]{1,0:T(8,128)}) %reduce-scatter.28.cloned.1.call-update) | async-done | bytes 131088 | tf_op jit(solution)/shard_map/reduce_scatter | solution.py:405
  1994.2 40.1 %reduce-scatter.30.cloned.1.call-done = f32[128,256]{1,0:T(8,128)} async-done(((f32[1024,256]{1,0:T(8,128)}), f32[128,256]{1,0:T(8,128)}) %reduce-scatter.30.cloned.1.call-update) | async-done | bytes 131088 | tf_op jit(solution)/shard_map/reduce_scatter | solution.py:406
  2034.4 40.0 %reduce-scatter.32.cloned.1.call-done = f32[256,128]{1,0:T(8,128)} async-done(((f32[256,1024]{1,0:T(8,128)}), f32[256,128]{1,0:T(8,128)}) %reduce-scatter.32.cloned.1.call-update) | async-done | bytes 131088 | tf_op jit(solution)/shard_map/reduce_scatter | solution.py:409
  (1639 shorter events, 784.2 us)
Async XLA Ops:
  8.0 103.2 %copy-start = (bf16[1024,16]{0,1:T(8,128)(2,1)S(1)}, bf16[1024,16]{0,1:T(8,128)(2,1)}, u32[]{:S(2)}) copy-start(bf16[1024,16]{0,1:T(8,128)(2,1)} %param.37) | copy-start | bytes 98308
  8.0 103.2 %all-gather.12.cloned.1.call-start = ((), (), s32[]{:S(2)}) async-start(), calls=%async_computation.13 | async-start | bytes 6553600 | tf_op jit(solution)/shard_map/all_gather | solution.py:243
  8.1 6.5 copy-start.66
  8.1 6.8 copy-start.72
  8.1 6.8 copy-start.60
  8.1 23.2 %copy-start.61 = (bf16[128,128]{1,0:T(8,128)(2,1)S(1)}, bf16[128,128]{1,0:T(8,128)(2,1)}, u32[]{:S(2)}) copy-start(bf16[128,128]{1,0:T(8,128)(2,1)} %param.34) | copy-start | bytes 98308
  9.8 38.4 %copy-start.71 = (bf16[512]{0:T(512)(128)(2,1)S(1)}, bf16[512]{0:T(512)(128)(2,1)}, u32[]{:S(2)}) copy-start(bf16[512]{0:T(512)(128)(2,1)} %param.39) | copy-start | bytes 3076
  9.8 38.5 %copy-start.49 = (bf16[128,256]{1,0:T(8,128)(2,1)S(1)}, bf16[128,256]{1,0:T(8,128)(2,1)}, u32[]{:S(2)}) copy-start(bf16[128,256]{1,0:T(8,128)(2,1)} %param.35) | copy-start | bytes 196612
  9.8 58.0 %copy-start.50 = (bf16[128,256]{1,0:T(8,128)(2,1)S(1)}, bf16[128,256]{1,0:T(8,128)(2,1)}, u32[]{:S(2)}) copy-start(bf16[128,256]{1,0:T(8,128)(2,1)} %param.36) | copy-start | bytes 196612
  11.7 75.1 %copy-start.51 = (bf16[256,128]{1,0:T(8,128)(2,1)S(1)}, bf16[256,128]{1,0:T(8,128)(2,1)}, u32[]{:S(2)}) copy-start(bf16[256,128]{1,0:T(8,128)(2,1)} %param.41) | copy-start | bytes 196612
  14.5 544.2 %reduce-scatter.16.cloned.1.call-start = ((), (), s32[]{:S(2)}) async-start(), calls=%async_computation.14 | async-start | bytes 6553600 | tf_op jit(solution)/shard_map/reduce_scatter | solution.py:298
  31.3 107.3 %copy-start.33 = (bf16[1024,128]{1,0:T(8,128)(2,1)}, bf16[1024,128]{1,0:T(8,128)(2,1)S(1)}, u32[]{:S(2)}) copy-start(bf16[1024,128]{1,0:T(8,128)(2,1)S(1)} %all_gather.57) | copy-start | bytes 786436
  48.2 85.2 %copy-start.31 = (bf16[1024,128]{1,0:T(8,128)(2,1)}, bf16[1024,128]{1,0:T(8,128)(2,1)S(1)}, u32[]{:S(2)}) copy-start(bf16[1024,128]{1,0:T(8,128)(2,1)S(1)} %all_gather.55) | copy-start | bytes 786436
  115.2 10.8 slice-start
  118.1 7.9 slice-start.1
  118.8 282.2 %copy-start.4 = (f32[1,40,64,1,128]{4,1,2,3,0:T(8,128)}, f32[1,40,64,1,128]{4,1,2,3,0:T(8,128)S(1)}, u32[]{:S(2)}) copy-start(f32[1,40,64,1,128]{4,1,2,3,0:T(8,128)S(1)} %fusion.258) | copy-start | bytes 3932164
  118.9 5.8 copy-start.67
  118.9 7.1 copy-start.37
  447.5 8.5 slice-start.2
  463.6 95.0 %copy-start.1 = (bf16[1,640,1024]{2,1,0:T(8,128)(2,1)S(1)}, bf16[1,640,1024]{2,1,0:T(8,128)(2,1)}, u32[]{:S(2)}) copy-start(bf16[1,640,1024]{2,1,0:T(8,128)(2,1)} %param.29) | copy-start | bytes 3932164
  463.6 101.1 %all-gather.16.cloned.1.call-start = ((), (), s32[]{:S(2)}) async-start(), calls=%async_computation.16 | async-start | bytes 1622016 | tf_op jit(solution)/shard_map/all_gather | solution.py:226
  464.2 193.9 %all-gather.14.cloned.1.call-start = ((), (), s32[]{:S(2)}) async-start(), calls=%async_computation.15 | async-start | bytes 6553600 | tf_op jit(solution)/shard_map/all_gather | solution.py:305
  464.3 470.3 %copy-start.45 = (f32[1024]{0:T(1024)}, f32[1024]{0:T(1024)S(1)}, u32[]{:S(2)}) copy-start(f32[1024]{0:T(1024)S(1)} %convert_element_type.293) | copy-start | bytes 12292
  560.6 374.0 %copy-start.47 = (f32[640]{0:T(1024)}, f32[640]{0:T(1024)S(1)}, u32[]{:S(2)}) copy-start(f32[640]{0:T(1024)S(1)} %get-tuple-element.1198) | copy-start | bytes 7684
  560.6 374.0 %copy-start.54 = (f32[640]{0:T(1024)}, f32[640]{0:T(1024)S(1)}, u32[]{:S(2)}) copy-start(f32[640]{0:T(1024)S(1)} %get-tuple-element.1197) | copy-start | bytes 7684
  562.2 123.6 %all-gather.18.cloned.1.call-start = ((), (), s32[]{:S(2)}) async-start(), calls=%async_computation.17 | async-start | bytes 1622016 | tf_op jit(solution)/shard_map/all_gather | solution.py:227
  562.8 150.1 %all-gather.20.cloned.1.call-start = ((), (), s32[]{:S(2)}) async-start(), calls=%async_computation.18 | async-start | bytes 1622016 | tf_op jit(solution)/shard_map/all_gather | solution.py:229
  563.5 246.4 %all-gather.22.cloned.1.call-start = ((), (), s32[]{:S(2)}) async-start(), calls=%async_computation.20 | async-start | bytes 6553600 | tf_op jit(solution)/shard_map/all_gather | solution.py:244
  564.2 367.2 %reduce-scatter.20.cloned.1.call-start = ((), (), s32[]{:S(2)}) async-start(), calls=%async_computation.21 | async-start | bytes 6553600 | tf_op jit(solution)/shard_map/reduce_scatter | solution.py:327
  809.9 13.9 copy-start.69
  836.6 196.1 %all-gather.24.cloned.1.call-start = ((), (), s32[]{:S(2)}) async-start(), calls=%async_computation.22 | async-start | bytes 6553600 | tf_op jit(solution)/shard_map/all_gather | solution.py:332
  936.7 638.6 %reduce-scatter.40.cloned.1.call-start = ((), (), s32[]{:S(2)}) async-start(), calls=%async_computation.33 | async-start | bytes 819200
  1032.6 9.7 copy-start.20
  1032.6 9.7 copy-start.30
  1477.7 6.2 copy-start.5
  1477.7 6.2 copy-start.12
  1490.3 5.8 copy-start.10
  1495.8 137.4 %reduce-scatter.22.cloned.1.call-start = ((), (), s32[]{:S(2)}) async-start(), calls=%async_computation.23 | async-start | bytes 6553600 | tf_op jit(solution)/shard_map/reduce_scatter | solution.py:371
  1512.9 5.5 copy-start.27
  1512.9 5.5 copy-start.13
  1519.3 5.5 copy-start.36
  1519.3 5.5 copy-start.40
  1538.3 192.5 %reduce-scatter.18.cloned.1.call-start = ((), (), s32[]{:S(2)}) async-start(), calls=%async_computation.19 | async-start | bytes 6553600 | tf_op jit(solution)/shard_map/reduce_scatter | solution.py:314
  1547.6 232.7 %reduce-scatter.34.cloned.1.call-start = ((), (), s32[]{:S(2)}) async-start(), calls=%async_computation.30 | async-start | bytes 3244032 | tf_op jit(solution)/shard_map/reduce_scatter | solution.py:407
  1557.0 272.6 %reduce-scatter.36.cloned.1.call-start = ((), (), s32[]{:S(2)}) async-start(), calls=%async_computation.31 | async-start | bytes 3244032 | tf_op jit(solution)/shard_map/reduce_scatter | solution.py:408
  1566.1 312.3 %reduce-scatter.38.cloned.1.call-start = ((), (), s32[]{:S(2)}) async-start(), calls=%async_computation.32 | async-start | bytes 3244032 | tf_op jit(solution)/shard_map/reduce_scatter | solution.py:410
  1575.2 303.3 %all-reduce.7.cloned.1.call-start = ((), (), s32[]{:S(2)}) async-start(), calls=%async_computation.28 | async-start | bytes 131072 | tf_op jit(solution)/shard_map/psum | solution.py:391
  1580.5 336.0 %reduce-scatter.24.cloned.1.call-start = ((), (), s32[]{:S(2)}) async-start(), calls=%async_computation.24 | async-start | bytes 589824 | tf_op jit(solution)/shard_map/reduce_scatter | solution.py:403
  1585.7 368.6 %reduce-scatter.26.cloned.1.call-start = ((), (), s32[]{:S(2)}) async-start(), calls=%async_computation.25 | async-start | bytes 589824 | tf_op jit(solution)/shard_map/reduce_scatter | solution.py:404
  1592.7 401.6 %reduce-scatter.28.cloned.1.call-start = ((), (), s32[]{:S(2)}) async-start(), calls=%async_computation.26 | async-start | bytes 1179648 | tf_op jit(solution)/shard_map/reduce_scatter | solution.py:405
  1600.4 434.0 %reduce-scatter.30.cloned.1.call-start = ((), (), s32[]{:S(2)}) async-start(), calls=%async_computation.27 | async-start | bytes 1179648 | tf_op jit(solution)/shard_map/reduce_scatter | solution.py:406
  1605.7 5.5 copy-start.44
  1605.7 27.5 %copy-start.2 = (bf16[1,640,1024]{2,1,0:T(8,128)(2,1)S(1)}, bf16[1,640,1024]{2,1,0:T(8,128)(2,1)}, u32[]{:S(2)}) copy-start(bf16[1,640,1024]{2,1,0:T(8,128)(2,1)} %param.29) | copy-start | bytes 3932164
  1605.7 27.5 %copy-start.53 = (f32[640]{0:T(1024)S(1)}, f32[640]{0:T(1024)}, u32[]{:S(2)}) copy-start(f32[640]{0:T(1024)} %copy-done.52) | copy-start | bytes 7684
  1605.7 27.5 %copy-start.57 = (f32[1024]{0:T(1024)S(1)}, f32[1024]{0:T(1024)}, u32[]{:S(2)}) copy-start(f32[1024]{0:T(1024)} %copy-done.56) | copy-start | bytes 12292
  1605.7 468.6 %reduce-scatter.32.cloned.1.call-start = ((), (), s32[]{:S(2)}) async-start(), calls=%async_computation.29 | async-start | bytes 1179648 | tf_op jit(solution)/shard_map/reduce_scatter | solution.py:409
  1611.4 25.6 %copy-start.63 = (f32[1024]{0:T(1024)S(1)}, f32[1024]{0:T(1024)}, u32[]{:S(2)}) copy-start(f32[1024]{0:T(1024)} %get-tuple-element.1052) | copy-start | bytes 12292
  1611.4 25.6 %copy-start.65 = (f32[256]{0:T(256)S(1)}, f32[256]{0:T(256)}, u32[]{:S(2)}) copy-start(f32[256]{0:T(256)} %get-tuple-element.1050) | copy-start | bytes 3076
  1611.4 119.4 %copy-start.7 = (bf16[1,640,1024]{2,1,0:T(8,128)(2,1)S(1)}, bf16[1,640,1024]{2,1,0:T(8,128)(2,1)}, u32[]{:S(2)}) copy-start(bf16[1,640,1024]{2,1,0:T(8,128)(2,1)} %reduce-scatter.16.cloned.1.call-done) | copy-start | bytes 3932164
  1611.4 119.4 %copy-start.46 = (f32[1024]{0:T(1024)S(1)}, f32[1024]{0:T(1024)}, u32[]{:S(2)}) copy-start(f32[1024]{0:T(1024)} %copy-done.45) | copy-start | bytes 12292
  1611.4 119.4 %copy-start.48 = (f32[640]{0:T(1024)S(1)}, f32[640]{0:T(1024)}, u32[]{:S(2)}) copy-start(f32[640]{0:T(1024)} %copy-done.47) | copy-start | bytes 7684
  1611.5 119.4 %copy-start.55 = (f32[640]{0:T(1024)S(1)}, f32[640]{0:T(1024)}, u32[]{:S(2)}) copy-start(f32[640]{0:T(1024)} %copy-done.54) | copy-start | bytes 7684
  1611.5 119.4 %copy-start.59 = (f32[640]{0:T(1024)S(1)}, f32[640]{0:T(1024)}, u32[]{:S(2)}) copy-start(f32[640]{0:T(1024)} %copy-done.58) | copy-start | bytes 7684
  1611.5 119.4 %copy-start.62 = (f32[640]{0:T(1024)S(1)}, f32[640]{0:T(1024)}, u32[]{:S(2)}) copy-start(f32[640]{0:T(1024)} %get-tuple-element.1195) | copy-start | bytes 7684
  (38 other events, 117.5 us)
Sparse Core Ops, SparseCore 0:
  14.6 96.5 all-gather.11
  463.8 94.8 reduce-scatter.15
  836.7 94.7 reduce-scatter.19
  1496.0 20.8 reduce-scatter.39
  1538.4 94.7 reduce-scatter.21
  1635.4 95.4 reduce-scatter.17
  1734.8 45.5 reduce-scatter.33
  1784.7 44.8 reduce-scatter.35
  1833.5 44.9 reduce-scatter.37
  1882.3 34.0 reduce-scatter.23
  1920.1 34.1 reduce-scatter.25
  1958.2 36.0 reduce-scatter.27
  1998.3 36.0 reduce-scatter.29
  2038.3 36.0 reduce-scatter.31
Sparse Core Ops, SparseCore 1:
  466.0 26.0 all-gather.15
  562.3 95.8 all-gather.13
  659.8 25.9 all-gather.17
  687.7 25.1 all-gather.19
  714.4 95.4 all-gather.21
  936.8 95.8 all-gather.23
  1582.8 235.9 all-reduce.6
where the time goes:
time: 2120 us; the launch traced here: 2080 us
  waiting for transfers between devices  924 us (44%)
  matrix products  501 us (24%)
  local copies, waits for them, and re-layouts  401 us (19%)
  blocking collectives  150 us (7%)
  other arithmetic  81.2 us (4%)
    dynamic_slice x200, local copies, waits for them, and re-layouts, sequence_mixer(): lax.scan(jax.checkpoint(block_causal), start_state, (scaled, key_blocks,...  138 us
    squeeze x120, local copies, waits for them, and re-layouts, sequence_mixer(): lax.scan(jax.checkpoint(block_causal), start_state, (scaled, key_blocks,...  98.2 us
    all_gather x1, waiting for transfers between devices, on_device(): lax.all_gather(cotangent, 'tp', axis=1, tiled=True)  97.1 us
    reduce_scatter x1, waiting for transfers between devices, on_device(): lax.psum_scatter(d_normed_two.astype(jnp.bfloat16), 'tp', scatter_dimensi...  94.8 us
    reduce_scatter x1, waiting for transfers between devices, on_device(): lax.psum_scatter(branch.astype(jnp.bfloat16), 'tp', scatter_dimension=1,...  94.3 us
    all_gather x1, waiting for transfers between devices, on_device(): lax.all_gather(normed_two, 'tp', axis=1, tiled=True)  93.3 us
    all_gather x1, waiting for transfers between devices, on_device(): lax.all_gather(d_resid.astype(jnp.bfloat16), 'tp', axis=1, tiled=True)  92.5 us
    dot_general x160, matrix products, block_causal(): jnp.einsum('thd,shd->hts', query_decayed, key_decayed, precision=MIXER_PR...  86.7 us
  transfers between devices with their start and end apart: 21, of which 18 were waited for; matrix products, arithmetic and copies ran while one was open for 7% of the time, Pallas kernels for 0%

commit v1 on v0

v1 whole, which is shorter than its diff:
```python
import functools

import jax
import jax.numpy as jnp
from jax import lax
from jax.experimental import pallas as pl
from jax.experimental.pallas import tpu as pltpu
from jax.sharding import Mesh, PartitionSpec as P

DK = 128
DV = 256
RANK = 16
PIECE = 256
CHUNK = 128
EPSILON = 1e-06
GATE_NORM = 16.0
F32 = jnp.float32
BF16 = jnp.bfloat16
VMEM_LIMIT = 60 * 1024 * 1024


def nn(left, right):
    return lax.dot_general(left, right, (((1,), (0,)), ((), ())), preferred_element_type=F32)


def nt(left, right):
    return lax.dot_general(left, right, (((1,), (1,)), ((), ())), preferred_element_type=F32)


def tn(left, right):
    return lax.dot_general(left, right, (((0,), (0,)), ((), ())), preferred_element_type=F32)


def iota2(axis):
    return lax.broadcasted_iota(jnp.int32, (CHUNK, CHUNK), axis)


def split_dot(matrix, values, terms):
    total = None
    for _ in range(terms):
        part = values.astype(BF16)
        values = values - part.astype(F32)
        product = nn(matrix, part)
        total = product if total is None else total + product
    return total


def state_rows(state, log_decay):
    high = log_decay.astype(BF16).astype(F32)
    rows = lax.broadcasted_iota(jnp.int32, (16, DK), 0)
    extra = jnp.where(rows == 0, high, jnp.where(rows == 1, log_decay - high, 0.0))
    return jnp.concatenate([state, extra], axis=0).astype(BF16)


def states_kernel(chunks, qkv_ref, gate_ref, sums_ref, local_ref, future_ref, end_ref):
    lower = (iota2(0) >= iota2(1)).astype(BF16)
    state = jnp.zeros((DV, DK), F32)
    total = jnp.zeros((1, DK), F32)
    for j in range(chunks):
        rows = pl.ds(j * CHUNK, CHUNK)
        gate_in = gate_ref[rows, :]
        gate_log = (jnp.minimum(gate_in, 0.0) - jnp.log1p(jnp.exp(-jnp.abs(gate_in)))) * (
            1.0 / GATE_NORM
        )
        sums = split_dot(lower, gate_log, 3)
        sums_ref[rows, :] = sums
        last = sums[CHUNK - 1 : CHUNK, :]
        key_rows = qkv_ref[rows, DK : 2 * DK].astype(F32)
        value_rows = qkv_ref[rows, 2 * DK :]
        local_ref[0, j] = state
        both = jnp.concatenate(
            [(key_rows * jnp.exp(last - sums)).astype(BF16), (key_rows * jnp.exp(sums)).astype(BF16)],
            axis=1,
        )
        update = tn(value_rows, both)
        state = state * jnp.exp(last) + update[:, :DK]
        total = total + last
        future_ref[0, j] = update[:, DK:].astype(BF16)
    end_ref[0] = state_rows(state, total)


def scores_of(queries, key_rows, sums, pic):
    middle = sums[CHUNK // 2 - 1 : CHUNK // 2, :]
    grow = jnp.exp(sums - middle)
    shrink = jnp.exp(middle - sums)
    q1 = (queries * grow).astype(BF16)
    k1 = (key_rows * shrink).astype(BF16)
    q2 = (queries * shrink).astype(BF16)
    k2 = (key_rows * grow).astype(BF16)
    row, col = iota2(0), iota2(1)
    diagonal = jnp.sum(queries * key_rows, axis=1, keepdims=True)
    above = jnp.logical_and(row < col, pic > 0)
    scores = jnp.where(
        row > col,
        nt(q1, k1),
        jnp.where(row == col, diagonal, jnp.where(above, nt(q2, k2), 0.0)),
    )
    return scores, q1, k1, q2, k2, grow, shrink, above


def mix_kernel(
    chunks,
    flags_ref,
    qkv_ref,
    sums_ref,
    local_ref,
    incoming_ref,
    future_ref,
    later_ref,
    outgate_ref,
    gain_ref,
    mixed_ref,
    gated_ref,
):
    incoming = incoming_ref[0].astype(F32)
    before = jnp.zeros((1, DK), F32)
    gain = gain_ref[...]
    for j in range(chunks):
        rows = pl.ds(j * CHUNK, CHUNK)
        sums = sums_ref[rows, :]
        last = sums[CHUNK - 1 : CHUNK, :]
        queries = qkv_ref[rows, :DK].astype(F32) * DK**-0.5
        key_rows = qkv_ref[rows, DK : 2 * DK].astype(F32)
        value_rows = qkv_ref[rows, 2 * DK :]
        scores = scores_of(queries, key_rows, sums, flags_ref[0, j])[0]
        state = (local_ref[0, j] + incoming * jnp.exp(before)).astype(BF16)
        later = later_ref[0] if j == chunks - 1 else future_ref[0, j + 1]
        cross = flags_ref[1, j].astype(F32)
        factors = jnp.concatenate(
            [
                (queries * jnp.exp(sums)).astype(BF16),
                (queries * (jnp.exp(last - sums) * cross)).astype(BF16),
            ],
            axis=1,
        )
        mixed = nn(scores.astype(BF16), value_rows) + nt(
            factors, jnp.concatenate([state, later], axis=1)
        )
        before = before + last
        mixed_ref[rows, :] = mixed
        scale = lax.rsqrt(jnp.mean(mixed * mixed, axis=1, keepdims=True) + EPSILON)
        gate = outgate_ref[rows, :]
        gated_ref[rows, :] = (mixed * scale * gain * gate * jax.nn.sigmoid(gate)).astype(BF16)


def gate_back_kernel(
    chunks,
    flags_ref,
    d_gated_ref,
    outgate_ref,
    mixed_ref,
    gain_ref,
    qkv_ref,
    sums_ref,
    d_outgate_ref,
    d_mixed_ref,
    gain_grad_ref,
    local_ref,
    end_ref,
    earlier_ref,
):
    gain = gain_ref[...]
    state = jnp.zeros((DV, DK), F32)
    total = jnp.zeros((1, DK), F32)
    gain_grad = jnp.zeros((1, DV), F32)
    for j in reversed(range(chunks)):
        rows = pl.ds(j * CHUNK, CHUNK)
        d_gated = d_gated_ref[rows, :]
        gate = outgate_ref[rows, :]
        mixed = mixed_ref[rows, :]
        sigma = jax.nn.sigmoid(gate)
        scale = lax.rsqrt(jnp.mean(mixed * mixed, axis=1, keepdims=True) + EPSILON)
        unit = mixed * scale
        d_grouped = d_gated * gate * sigma
        slope = sigma * (1.0 + gate * (1.0 - sigma))
        d_outgate_ref[rows, :] = (d_gated * unit * gain * slope).astype(BF16)
        gain_grad = gain_grad + jnp.sum(d_grouped * unit, axis=0, keepdims=True)
        weighted = gain * d_grouped
        d_mixed = scale * (weighted - unit * jnp.mean(weighted * unit, axis=1, keepdims=True))
        d_low = d_mixed.astype(BF16)
        d_mixed_ref[rows, :] = d_low
        sums = sums_ref[rows, :]
        last = sums[CHUNK - 1 : CHUNK, :]
        queries = qkv_ref[rows, :DK].astype(F32) * DK**-0.5
        local_ref[0, j] = state
        update = tn(d_low, (queries * jnp.exp(sums)).astype(BF16))
        if j == chunks - 1:
            cross = flags_ref[1, j].astype(F32)
            earlier_ref[0] = tn(
                d_low, (queries * (jnp.exp(last - sums) * cross)).astype(BF16)
            ).astype(BF16)
        state = state * jnp.exp(last) + update
        total = total + last
    gain_grad_ref[0] = gain_grad
    end_ref[0] = state_rows(state, total)


def mix_back_kernel(
    chunks,
    flags_ref,
    d_mixed_ref,
    qkv_ref,
    sums_ref,
    local_ref,
    incoming_ref,
    future_ref,
    later_ref,
    back_local_ref,
    back_incoming_ref,
    earlier_ref,
    gate_ref,
    d_qkv_ref,
    d_gate_ref,
):
    incoming = incoming_ref[0].astype(F32)
    back_incoming = back_incoming_ref[0].astype(F32)
    lasts = [sums_ref[pl.ds(j * CHUNK + CHUNK - 1, 1), :] for j in range(chunks)]
    row, col = iota2(0), iota2(1)
    upper = (row <= col).astype(BF16)
    before = jnp.zeros((1, DK), F32)
    d_future = earlier_ref[0]
    for j in range(chunks):
        rows = pl.ds(j * CHUNK, CHUNK)
        sums = sums_ref[rows, :]
        last = lasts[j]
        after = jnp.zeros((1, DK), F32)
        for l in range(j + 1, chunks):
            after = after + lasts[l]
        queries = qkv_ref[rows, :DK].astype(F32) * DK**-0.5
        key_rows = qkv_ref[rows, DK : 2 * DK].astype(F32)
        value_rows = qkv_ref[rows, 2 * DK :]
        d_mixed = d_mixed_ref[rows, :]
        scores, q1, k1, q2, k2, grow, shrink, above = scores_of(
            queries, key_rows, sums, flags_ref[0, j]
        )
        state = local_ref[0, j] + incoming * jnp.exp(before)
        back_state = back_local_ref[0, j] + back_incoming * jnp.exp(after)
        later = later_ref[0] if j == chunks - 1 else future_ref[0, j + 1]
        cross = flags_ref[1, j].astype(F32)
        from_start = jnp.exp(sums)
        to_end = jnp.exp(last - sums)
        to_later = to_end * cross
        d_scores = nt(d_mixed, value_rows)
        on_diagonal = jnp.sum(jnp.where(row == col, d_scores, 0.0), axis=1, keepdims=True)
        below = jnp.where(row > col, d_scores, 0.0).astype(BF16)
        ahead = jnp.where(above, d_scores, 0.0).astype(BF16)
        dq_causal = grow * nn(below, k1)
        dk_causal = shrink * tn(below, q1)
        dq_ahead = shrink * nn(ahead, k2)
        dk_ahead = grow * tn(ahead, q2)
        d_factors = nn(d_mixed, jnp.concatenate([state.astype(BF16), later], axis=1))
        dq_causal = dq_causal + from_start * d_factors[:, :DK]
        dq_later = to_later * d_factors[:, DK:]
        back_pair = jnp.concatenate([back_state.astype(BF16), d_future], axis=1)
        d_factors = nn(value_rows, back_pair)
        dk_state = to_end * d_factors[:, :DK]
        dk_earlier = from_start * d_factors[:, DK:]
        key_factors = jnp.concatenate(
            [(key_rows * to_end).astype(BF16), (key_rows * from_start).astype(BF16)], axis=1
        )
        d_values = tn(scores.astype(BF16), d_mixed) + nt(key_factors, back_pair)
        d_future = tn(d_mixed, (queries * to_later).astype(BF16)).astype(BF16)
        d_sums = queries * (dq_causal - dq_ahead - dq_later) + key_rows * (
            dk_ahead + dk_earlier - dk_causal - dk_state
        )
        d_last = (
            jnp.sum(key_rows * dk_state + queries * dq_later, axis=0, keepdims=True)
            + jnp.sum(state * back_state, axis=0, keepdims=True) * jnp.exp(last)
        )
        d_log = split_dot(upper, d_sums, 2) + d_last
        gate_in = gate_ref[rows, :]
        d_gate_ref[rows, :] = (d_log * jax.nn.sigmoid(-gate_in) * (1.0 / GATE_NORM)).astype(BF16)
        d_qkv_ref[rows, :DK] = (
            (dq_causal + dq_ahead + dq_later + on_diagonal * key_rows) * DK**-0.5
        ).astype(BF16)
        d_qkv_ref[rows, DK : 2 * DK] = (
            dk_causal + dk_ahead + dk_state + dk_earlier + on_diagonal * queries
        ).astype(BF16)
        d_qkv_ref[rows, 2 * DK :] = d_values.astype(BF16)
        before = before + last


def rows_block(length, width):
    return pl.BlockSpec((length, width), lambda h: (0, h))


def lead_block(*inner):
    return pl.BlockSpec((1, *inner), lambda h: (h,) + (0,) * len(inner))


def whole_block(*dims):
    return pl.BlockSpec(dims, lambda h: (0,) * len(dims))


def smem():
    return pl.BlockSpec(memory_space=pltpu.SMEM)


def params():
    return pltpu.CompilerParams(vmem_limit_bytes=VMEM_LIMIT)


def shaped(shape, kind):
    return jax.ShapeDtypeStruct(shape, kind)


def chunk_states(qkv, gate_in, heads):
    length = qkv.shape[0]
    chunks = length // CHUNK
    width = 2 * DK + DV
    return pl.pallas_call(
        functools.partial(states_kernel, chunks),
        grid=(heads,),
        in_specs=[rows_block(length, width), rows_block(length, DK)],
        out_specs=[
            rows_block(length, DK),
            lead_block(chunks, DV, DK),
            lead_block(chunks, DV, DK),
            lead_block(DV + 16, DK),
        ],
        out_shape=[
            shaped((length, heads * DK), F32),
            shaped((heads, chunks, DV, DK), F32),
            shaped((heads, chunks, DV, DK), BF16),
            shaped((heads, DV + 16, DK), BF16),
        ],
        compiler_params=params(),
        name="chunk_states",
    )(qkv, gate_in)


def mix(flags, qkv, sums, local, incoming, future, later, outgate, gain):
    length = qkv.shape[0]
    heads, chunks = local.shape[:2]
    width = 2 * DK + DV
    return pl.pallas_call(
        functools.partial(mix_kernel, chunks),
        grid=(heads,),
        in_specs=[
            smem(),
            rows_block(length, width),
            rows_block(length, DK),
            lead_block(chunks, DV, DK),
            lead_block(DV, DK),
            lead_block(chunks, DV, DK),
            lead_block(DV, DK),
            rows_block(length, DV),
            whole_block(1, DV),
        ],
        out_specs=[rows_block(length, DV), rows_block(length, DV)],
        out_shape=[shaped((length, heads * DV), F32), shaped((length, heads * DV), BF16)],
        compiler_params=params(),
        name="mix",
    )(flags, qkv, sums, local, incoming, future, later, outgate, gain)


def gate_back(flags, d_gated, outgate, mixed, gain, qkv, sums, heads):
    length = qkv.shape[0]
    chunks = length // CHUNK
    width = 2 * DK + DV
    return pl.pallas_call(
        functools.partial(gate_back_kernel, chunks),
        grid=(heads,),
        in_specs=[
            smem(),
            rows_block(length, DV),
            rows_block(length, DV),
            rows_block(length, DV),
            whole_block(1, DV),
            rows_block(length, width),
            rows_block(length, DK),
        ],
        out_specs=[
            rows_block(length, DV),
            rows_block(length, DV),
            lead_block(1, DV),
            lead_block(chunks, DV, DK),
            lead_block(DV + 16, DK),
            lead_block(DV, DK),
        ],
        out_shape=[
            shaped((length, heads * DV), BF16),
            shaped((length, heads * DV), BF16),
            shaped((heads, 1, DV), F32),
            shaped((heads, chunks, DV, DK), F32),
            shaped((heads, DV + 16, DK), BF16),
            shaped((heads, DV, DK), BF16),
        ],
        compiler_params=params(),
        name="gate_back",
    )(flags, d_gated, outgate, mixed, gain, qkv, sums)


def mix_back(
    flags, d_mixed, qkv, sums, local, incoming, future, later, back_local, back_incoming, earlier, gate_in
):
    length = qkv.shape[0]
    heads, chunks = local.shape[:2]
    width = 2 * DK + DV
    return pl.pallas_call(
        functools.partial(mix_back_kernel, chunks),
        grid=(heads,),
        in_specs=[
            smem(),
            rows_block(length, DV),
            rows_block(length, width),
            rows_block(length, DK),
            lead_block(chunks, DV, DK),
            lead_block(DV, DK),
            lead_block(chunks, DV, DK),
            lead_block(DV, DK),
            lead_block(chunks, DV, DK),
            lead_block(DV, DK),
            lead_block(DV, DK),
            rows_block(length, DK),
        ],
        out_specs=[rows_block(length, width), rows_block(length, DK)],
        out_shape=[shaped((length, heads * width), BF16), shaped((length, heads * DK), BF16)],
        compiler_params=params(),
        name="mix_back",
    )(
        flags, d_mixed, qkv, sums, local, incoming, future, later, back_local, back_incoming, earlier, gate_in
    )


def chain_kernel(count, backwards, place_ref, *refs):
    parts, other_ref, total_ref = refs[:count], refs[count], refs[count + 1]
    outs, scratch, result = refs[count + 2 : 2 * count + 2], refs[-2], refs[-1]
    place, joined = place_ref[0], place_ref[1]
    for k in range(count):
        scratch[lax.rem(place + k, count)] = parts[k][...].astype(F32)
    state = jnp.where(joined > 0, other_ref[:DV, :].astype(F32), 0.0)
    for z in reversed(range(count)) if backwards else range(count):
        result[z] = state.astype(BF16)
        log_decay = scratch[z, DV : DV + 1, :] + scratch[z, DV + 1 : DV + 2, :]
        state = state * jnp.exp(log_decay) + scratch[z, :DV, :]
    total_ref[...] = state.astype(BF16)
    for k in range(count):
        outs[k][...] = result[lax.rem(place + k, count)]


def chain(parts, other, place, joined, backwards):
    count = len(parts)
    return pl.pallas_call(
        functools.partial(chain_kernel, count, backwards),
        in_specs=[smem()] + [pl.BlockSpec(memory_space=pltpu.VMEM)] * (count + 1),
        out_specs=[pl.BlockSpec(memory_space=pltpu.VMEM)] * (count + 1),
        out_shape=[shaped((DV, DK), BF16)] * (count + 1),
        scratch_shapes=[
            pltpu.VMEM((count, DV + 16, DK), F32),
            pltpu.VMEM((count, DV, DK), BF16),
        ],
        compiler_params=params(),
        name="chain",
    )(jnp.stack([place, joined]).astype(jnp.int32), *parts, other)


def shifted(array, axis, by):
    size = lax.axis_size(axis)
    return lax.ppermute(array, axis, [(i, (i + by) % size) for i in range(size)])


def swapped(array, axis):
    return lax.ppermute(array, axis, [(0, 1), (1, 0)])


def exchange_states(ends, backwards):
    count = lax.axis_size("tp")
    place = lax.axis_index("tp")
    side = lax.axis_index("ctx")
    parts = [ends[0]] + [shifted(ends[k], "tp", -k) for k in range(1, count)]
    zero = jnp.zeros((DV, DK), BF16)
    total = chain(parts, zero, place, jnp.zeros_like(place), backwards)[0]
    other = swapped(total, "ctx")
    joined = (side == 0) if backwards else (side == 1)
    outs = chain(parts, other, place, joined.astype(place.dtype), backwards)[1:]
    return jnp.stack([outs[0]] + [shifted(outs[k], "tp", k) for k in range(1, count)])


def neighbour_future(first, odd_to_even):
    size = lax.axis_size("tp")
    if odd_to_even:
        moved = lax.ppermute(first, "tp", [(i + 1, i) for i in range(0, size - 1, 2)])
        return jnp.concatenate([moved[1:], moved[:1]], axis=0)
    moved = lax.ppermute(first, "tp", [(i, i + 1) for i in range(0, size - 1, 2)])
    return jnp.concatenate([moved[-1:], moved[:-1]], axis=0)


def split_axes():
    return all(lax.axis_size(axis) == 2 for axis in ("dpo", "core", "ctx"))


def column_order(back):
    if not split_axes():
        return None
    y, core, x = (lax.axis_index(axis) for axis in ("dpo", "core", "ctx"))
    order = []
    for j in range(8):
        high, middle, last = j >> 2, (j >> 1) & 1, j & 1
        if back:
            order.append(((core ^ middle) * 2 + (y ^ high)) * 2 + (x ^ last))
        else:
            order.append(((y ^ middle) * 2 + (core ^ high)) * 2 + (x ^ last))
    return order


def reorder(array, axis, back=False):
    order = column_order(back)
    if order is None:
        return array
    size = array.shape[axis] // len(order)
    return jnp.concatenate(
        [lax.dynamic_slice_in_dim(array, block * size, size, axis) for block in order], axis=axis
    )


def weight_axes(first):
    return ("ctx", "dpo") if first == "ctx" else ("dpo", "ctx")


def gather_weights(shards, first):
    count = lax.axis_size("tp")
    if not split_axes():
        place = lax.axis_index("tp")
        out = []
        for shard in shards:
            wide = lax.all_gather(shard, ("dpo", "core", "ctx"), axis=1, tiled=True)
            every = lax.all_gather(wide, "tp")
            every = jnp.take(every, lax.rem(place - jnp.arange(count) + count, count), axis=0)
            out.append(every.reshape(-1, every.shape[-1]))
        return jnp.concatenate(out, axis=0)
    one, two = weight_axes(first)
    shard = jnp.concatenate(shards, axis=0)
    slots = [shard] + [shifted(shard, "tp", k) for k in range(1, count)]
    rows, at = [], 0
    for part in shards:
        rows += [slot[at : at + part.shape[0]] for slot in slots]
        at += part.shape[0]
    pieces = {(0, 0): jnp.concatenate(rows, axis=0)}
    pieces[1, 0] = swapped(pieces[0, 0], one)
    pieces[0, 1] = swapped(pieces[0, 0], two)
    pieces[1, 1] = swapped(pieces[1, 0], two)
    own = [pieces[(y, x) if one == "dpo" else (x, y)] for y in (0, 1) for x in (0, 1)]
    return jnp.concatenate(own + [swapped(piece, "core") for piece in own], axis=1)


def scatter_grads(left, right, sizes, first):
    count = lax.axis_size("tp")
    if not split_axes():
        place = lax.axis_index("tp")
        whole = tn(left, right)
        out, at = [], 0
        for size in sizes:
            part = whole[at : at + count * size].reshape(count, size, -1)
            part = jnp.take(part, lax.rem(place - jnp.arange(count) + count, count), axis=0)
            part = lax.psum_scatter(part, "tp", scatter_dimension=0, tiled=True)[0]
            out.append(lax.psum_scatter(part, ("dpo", "core", "ctx"), scatter_dimension=1, tiled=True))
            at += count * size
        return out
    half = right.shape[1] // 2
    quarter = half // 4
    far = swapped(tn(left, right[:, half:]).astype(BF16), "core")
    near = tn(left, right[:, :half]) + far.astype(F32)
    blocks = {(i >> 1, i & 1): near[:, i * quarter : (i + 1) * quarter] for i in range(4)}
    if first == "ctx":
        blocks = {(x, y): block for (y, x), block in blocks.items()}
    one, two = weight_axes(first)
    sent = jnp.concatenate([blocks[1, 0], blocks[1, 1]], axis=1).astype(BF16)
    kept = jnp.concatenate([blocks[0, 0], blocks[0, 1]], axis=1).astype(BF16)
    sums = kept.astype(F32) + swapped(sent, one).astype(F32)
    sent, kept = sums[:, quarter:].astype(BF16), sums[:, :quarter].astype(BF16)
    sums = (kept.astype(F32) + swapped(sent, two).astype(F32)).astype(BF16)
    slots, at = [[] for _ in range(count)], 0
    for size in sizes:
        for k in range(count):
            slots[k].append(sums[at + k * size : at + (k + 1) * size])
        at += count * size
    slots = [jnp.concatenate(slot, axis=0) if len(slot) > 1 else slot[0] for slot in slots]
    total = slots[0].astype(F32)
    for k in range(1, count):
        total = total + shifted(slots[k], "tp", -k).astype(F32)
    out, at = [], 0
    for size in sizes:
        out.append(total[at : at + size])
        at += size
    return out


def sum_everywhere(values):
    if not split_axes() or lax.axis_size("tp") != 4:
        return lax.psum(values, ("dpo", "core", "ctx", "tp"))
    for axis in ("core", "ctx", "dpo"):
        values = values + swapped(values, axis)
    for pairs in ([(0, 1), (1, 0), (2, 3), (3, 2)], [(0, 2), (2, 0), (1, 3), (3, 1)]):
        values = values + lax.ppermute(values, "tp", pairs)
    return values


def rms_scale(values):
    return lax.rsqrt(jnp.mean(values * values, axis=-1, keepdims=True) + EPSILON)


def norm_back(upstream, values, scale, gain):
    weighted = upstream * gain
    return scale * weighted - values * scale**3 * jnp.mean(
        weighted * values, axis=-1, keepdims=True
    )


def on_device(
    hidden_in,
    cotangent,
    pic_starts,
    norm_mixer,
    w_query,
    w_key,
    w_value,
    w_outgate,
    w_rank_in,
    w_rank_out,
    gate_bias,
    group_gain,
    w_output,
    norm_ffn,
    w_gate,
    w_up,
    w_down,
):
    seq_count, length, model_width = hidden_in.shape
    assert seq_count == 1
    heads = lax.axis_size("tp")
    place = lax.axis_index("tp")
    chunks = length // CHUNK
    units = w_down.shape[0]
    half = units // 2

    cut = lambda array, index: array[index * half : (index + 1) * half]
    w_gate_t, w_up_t = w_gate.T, w_up.T
    w_in = jnp.concatenate([w_query.T, w_key.T, w_value.T], axis=0)
    w_in_all = gather_weights([w_in], "dpo")
    w_side_all = gather_weights([w_outgate.T, w_output], "ctx")
    w_og_all, w_out_all = w_side_all[: heads * DV], w_side_all[heads * DV :]
    ffn_all = [
        gather_weights([cut(w_gate_t, s), cut(w_up_t, s), cut(w_down, s)], ("dpo", "ctx")[s])
        for s in range(2)
    ]
    wide = heads * half

    head_order = lax.rem(place - jnp.arange(heads) + heads, heads)
    rank_out = jnp.take(w_rank_out.reshape(RANK, heads, DK), head_order, axis=1).reshape(
        RANK, heads * DK
    )
    bias = jnp.take(gate_bias.reshape(heads, DK), head_order, axis=0).reshape(heads * DK)
    rank_in = reorder(w_rank_in, 0)
    gain_one = reorder(norm_mixer, 0).astype(F32)
    gain_two = reorder(norm_ffn, 0).astype(F32)

    inputs_low = reorder(hidden_in[0], 1)
    upstream = reorder(cotangent[0], 1)
    inputs = inputs_low.astype(F32)
    scale_one = rms_scale(inputs)
    normed = (inputs * scale_one * gain_one).astype(BF16)

    part = lax.axis_index("ctx") * heads + place
    starts = part * length + jnp.arange(chunks, dtype=jnp.int32) * CHUNK
    inside = (starts[:, None] >= pic_starts[0][None, :]) & (
        starts[:, None] < pic_starts[0][None, :] + PIECE
    )
    in_piece = jnp.any(inside, axis=1)
    first_half = (starts % PIECE) == 0
    flags = jnp.stack([in_piece, in_piece & first_half]).astype(jnp.int32)

    qkv = nt(normed, w_in_all).astype(BF16)
    rank_low = nn(normed, rank_in).astype(BF16)
    gate_in = nn(rank_low, rank_out) + bias.astype(F32)
    sums, local, future, ends = chunk_states(qkv, gate_in, heads)
    later = neighbour_future(future[:, 0], True)
    incoming = exchange_states(ends, False)
    outgate = nt(normed, w_og_all)
    gain_group = group_gain.astype(F32)[None, :]
    mixed, gated = mix(flags, qkv, sums, local, incoming, future, later, outgate, gain_group)
    resid = inputs + nn(gated, w_out_all)
    scale_two = rms_scale(resid)
    normed_two = (resid * scale_two * gain_two).astype(BF16)

    feed = jnp.zeros_like(resid)
    d_norm_two = jnp.zeros_like(resid)
    grads = []
    for s in range(2):
        weights = ffn_all[s]
        gate_w, up_w, down_w = weights[:wide], weights[wide : 2 * wide], weights[2 * wide :]
        gate_pre, up_pre = nt(normed_two, gate_w), nt(normed_two, up_w)
        sigma = jax.nn.sigmoid(gate_pre)
        silu = gate_pre * sigma
        activation = (silu * up_pre).astype(BF16)
        feed = feed + nn(activation, down_w)
        d_act = nt(upstream, down_w)
        d_gate = (d_act * up_pre * (sigma * (1.0 + gate_pre * (1.0 - sigma)))).astype(BF16)
        d_up = (d_act * silu).astype(BF16)
        d_norm_two = d_norm_two + nn(d_gate, gate_w) + nn(d_up, up_w)
        order = ("ctx", "dpo")[s]
        grad_down = scatter_grads(activation, upstream, [half], order)[0]
        grad_gate = scatter_grads(d_gate, normed_two, [half], order)[0]
        grad_up = scatter_grads(d_up, normed_two, [half], order)[0]
        grads.append((grad_gate, grad_up, grad_down))
    hidden_out = reorder((resid + feed).astype(BF16), 1, True)[None]
    grad_gate, grad_up, grad_down = (jnp.concatenate(pair, axis=0) for pair in zip(*grads))

    grad_ffn_term = jnp.sum(d_norm_two * resid * scale_two, axis=0)
    d_resid = upstream.astype(F32) + norm_back(d_norm_two, resid, scale_two, gain_two)
    d_branch = d_resid.astype(BF16)
    d_gated = nt(d_branch, w_out_all)
    d_outgate, d_mixed, gain_terms, back_local, back_ends, earlier = gate_back(
        flags, d_gated, outgate, mixed, gain_group, qkv, sums, heads
    )
    grad_group_term = jnp.sum(gain_terms, axis=(0, 1))
    earlier = neighbour_future(earlier, False)
    back_incoming = exchange_states(back_ends, True)
    grad_output = scatter_grads(gated, d_branch, [DV], "ctx")[0]
    grad_outgate = scatter_grads(d_outgate, normed, [DV], "dpo")[0]
    d_qkv, d_gate_in = mix_back(
        flags, d_mixed, qkv, sums, local, incoming, future, later, back_local, back_incoming, earlier, gate_in
    )
    grad_in_heads = scatter_grads(d_qkv, normed, [2 * DK + DV], "ctx")[0]
    grad_bias_here = jnp.sum(d_gate_in.astype(F32), axis=0)
    grad_rank_here = tn(rank_low, d_gate_in)
    d_rank_low = nt(d_gate_in, rank_out).astype(BF16)
    d_normed = nn(d_qkv, w_in_all) + nn(d_outgate, w_og_all) + nt(d_rank_low, rank_in)
    grad_rank_in_term = tn(normed, d_rank_low)
    grad_mixer_term = jnp.sum(d_normed * inputs * scale_one, axis=0)
    grad_in = reorder(d_resid + norm_back(d_normed, inputs, scale_one, gain_one), 1, True)[None]

    rank_out_here = jnp.take(grad_rank_here.reshape(RANK, heads, DK), head_order, axis=1)
    bias_here = jnp.take(grad_bias_here.reshape(heads, DK), head_order, axis=0)
    small = (
        reorder(grad_mixer_term, 0, True),
        reorder(grad_rank_in_term, 0, True),
        rank_out_here,
        bias_here,
        grad_group_term,
        reorder(grad_ffn_term, 0, True),
    )
    flat = sum_everywhere(jnp.concatenate([term.reshape(-1, DK) for term in small], axis=0))
    shared, at = [], 0
    for term in small:
        rows = term.size // DK
        shared.append(flat[at : at + rows])
        at += rows
    return (
        hidden_out,
        grad_in,
        shared[0].reshape(norm_mixer.shape),
        grad_in_heads[:DK].T,
        grad_in_heads[DK : 2 * DK].T,
        grad_in_heads[2 * DK :].T,
        grad_outgate.T,
        shared[1].reshape(w_rank_in.shape),
        shared[2].reshape(w_rank_out.shape),
        shared[3].reshape(gate_bias.shape),
        shared[4].reshape(group_gain.shape),
        grad_output,
        shared[5].reshape(norm_ffn.shape),
        grad_gate.T,
        grad_up.T,
        grad_down,
    )


def solution(mesh):
    sizes = dict(mesh.shape)
    cores = 2
    inner = Mesh(
        mesh.devices.reshape(sizes["dp"] // cores, cores, sizes["ctx"], sizes["tp"]),
        ("dpo", "core", "ctx", "tp"),
    )
    dp = ("dpo", "core")
    tokens = P(dp, ("ctx", "tp"), None)
    columns = P((*dp, "ctx"), "tp")
    rows = P("tp", (*dp, "ctx"))
    return jax.shard_map(
        on_device,
        mesh=inner,
        in_specs=(
            tokens,
            tokens,
            P(dp, None),
            P(),
            columns,
            columns,
            columns,
            columns,
            P(),
            P(),
            P(),
            P(),
            rows,
            P(),
            columns,
            columns,
            rows,
        ),
        out_specs=(
            tokens,
            tokens,
            P(),
            columns,
            columns,
            columns,
            columns,
            P(),
            P(),
            P(),
            P(),
            rows,
            P(),
            columns,
            columns,
            rows,
        ),
        check_vma=False,
    )
```

time: 2120 us -> 711 us (0.34); the launches traced: 2080 us -> 699 us
  waiting for transfers between devices: 924 us -> 211 us
  matrix products: 501 us -> 140 us
  local copies, waits for them, and re-layouts: 401 us -> 147 us
  blocking collectives: 150 us -> 0 us
  starting transfers between devices: 2.19 us -> 116 us
  Pallas kernels: 0 us -> 45.8 us
  other arithmetic: 81.2 us -> 37 us
    reduce_scatter x12 -> x0, waiting for transfers between devices: 598 us -> none  [the longest x1 94.8 us: on_device(): lax.psum_scatter(d_normed_two.astype(jnp.bfloat16), 'tp', scatter_dimensi...]
    dot_general x605 -> x42, matrix products: 501 us -> 140 us  [the longest x11 51.2 us: nt(): lax.dot_general(left, right, (((1,), (1,)), ((), ())), preferred_element_...]
    all_gather x7 -> x0, waiting for transfers between devices: 323 us -> none  [the longest x1 97.1 us: on_device(): lax.all_gather(cotangent, 'tp', axis=1, tiled=True)]
    ppermute x0 -> x115, waiting for transfers between devices: none -> 211 us  [the longest x60 156 us: swapped(): return lax.ppermute(array, axis, [(0, 1), (1, 0)])]
    dynamic_slice x208 -> x1, local copies, waits for them, and re-layouts: 146 us -> 0.68 us  [reorder(): lax.dynamic_slice_in_dim(array, block * size, size, axis)]
    squeeze x224 -> x3, local copies, waits for them, and re-layouts: 120 us -> 3.95 us  [the longest x2 2.28 us: exchange_states(): parts = [ends[0]] + [shifted(ends[k], 'tp', -k) for k in range(1, count)]]
    ppermute x0 -> x115, starting transfers between devices: none -> 116 us  [the longest x51 69.3 us: shifted(): lax.ppermute(array, axis, [(i, (i + by) % size) for i in range(size)])]
    all_gather x8 -> x0, blocking collectives: 105 us -> none  [the longest x1 19.5 us: on_device(): lax.all_gather(w_value, ('dp', 'ctx'), axis=0, tiled=True)]
  transfers between devices with their start and end apart: 21 -> 115, of which waited for: 18 -> 40; matrix products, arithmetic and copies ran while one was open for 7% -> 33% of each run, Pallas kernels for 0% -> 5%
where the time goes in v1:
time: 711 us; the launch traced here: 699 us
  waiting for transfers between devices  211 us (30%)
  local copies, waits for them, and re-layouts  147 us (21%)
  matrix products  140 us (20%)
  starting transfers between devices  116 us (16%)
  Pallas kernels  45.8 us (6%)
  other arithmetic  37 us (5%)
    ppermute x60, waiting for transfers between devices, swapped(): return lax.ppermute(array, axis, [(0, 1), (1, 0)])  156 us
    unnamed x361, local copies, waits for them, and re-layouts  109 us
    ppermute x51, starting transfers between devices, shifted(): lax.ppermute(array, axis, [(i, (i + by) % size) for i in range(size)])  69.3 us
    dot_general x11, matrix products, nt(): lax.dot_general(left, right, (((1,), (1,)), ((), ())), preferred_element_...  51.2 us
    ppermute x51, waiting for transfers between devices, shifted(): lax.ppermute(array, axis, [(i, (i + by) % size) for i in range(size)])  47.9 us
    dot_general x20, matrix products, tn(): lax.dot_general(left, right, (((0,), (0,)), ((), ())), preferred_element_...  47.1 us
    dot_general x11, matrix products, nn(): lax.dot_general(left, right, (((1,), (0,)), ((), ())), preferred_element_...  41.2 us
    ppermute x60, starting transfers between devices, swapped(): return lax.ppermute(array, axis, [(0, 1), (1, 0)])  39.1 us
  transfers between devices with their start and end apart: 115, of which 40 were waited for; matrix products, arithmetic and copies ran while one was open for 33% of the time, Pallas kernels for 5%

profile of v1, /device:TPU:12, one launch (start us, length us, event | category | flops | bytes accessed | tf_op | source)
XLA Modules:
  0.0 698.7 jit_solution(11077586124091528290)
XLA Ops:
  12.9 3.5 collective-permute-start.19
  74.5 4.9 collective-permute-done.20
  92.2 5.7 collective-permute-done.2
  104.9 3.6 collective-permute-done.38
  138.0 10.3 %collective-permute-done.23 = bf16[2048,128]{1,0:T(8,128)(2,1)S(1)} collective-permute-done((bf16[2048,128]{1,0:T(8,128)(2,1)S(1)}, bf16[2048,128]{1,0:T(8,128)(2,1)S(1)}, u32[]{:S(2)}, u32[]{:S(2)}) %collective-permute-start.23) | collective-permute-done | bytes 524320 | tf_op jit(solution)/shard_map/ppermute | solution.py:464
  154.8 18.9 %collective-permute-done.5 = bf16[2048,128]{0,1:T(8,128)(2,1)S(1)} collective-permute-done((bf16[2048,128]{0,1:T(8,128)(2,1)S(1)}, bf16[2048,128]{0,1:T(8,128)(2,1)S(1)}, u32[]{:S(2)}, u32[]{:S(2)}) %collective-permute-start.5) | collective-permute-done | bytes 524320 | tf_op jit(solution)/shard_map/ppermute | solution.py:464
  182.1 18.4 %collective-permute-done.41 = bf16[4224,128]{1,0:T(8,128)(2,1)S(1)} collective-permute-done((bf16[4224,128]{1,0:T(8,128)(2,1)}, bf16[4224,128]{1,0:T(8,128)(2,1)S(1)}, u32[]{:S(2)}, u32[]{:S(2)}) %collective-permute-start.41) | collective-permute-done | bytes 1081376 | tf_op jit(solution)/shard_map/ppermute | solution.py:464
  205.2 4.2 convolution_convert_fusion.qkv_ref
  209.4 6.6 chunk_states.1
  220.8 2.9 collective-permute-start.12
  231.3 3.1 collective-permute-done.13.refs_4_
  240.9 4.6 fusion.41.outgate_ref
  249.9 8.5 %mix.1 = (f32[640,1024]{1,0:T(8,128)}, bf16[640,1024]{1,0:T(8,128)(2,1)}) custom-call(s32[2,5]{1,0:T(2,128)} %add_convert_fusion.28.flags_ref, bf16[640,2048]{1,0:T(8,128)(2,1)} %convolution_convert_fusion.qkv_ref, f32[640,512]{1,0:T(8,128)} %get-tuple-element.40.sums_ref, f32[4,5,256,128]{3,2,1,0:T(8,128)} %get-tuple-element.41.local_ref, ...), custom_call_target="tpu_custom_call" | custom-call | tf_op jit(solution)/shard_map/mix/pallas_call | solution.py:336
  258.4 3.6 multiply_reduce_fusion.2
  262.3 9.8 %collective-permute-done.33 = bf16[4224,128]{1,0:T(8,128)(2,1)} collective-permute-done((bf16[4224,128]{1,0:T(8,128)(2,1)}, bf16[4224,128]{1,0:T(8,128)(2,1)}, u32[]{:S(2)}, u32[]{:S(2)}) %collective-permute-start.33) | collective-permute-done | bytes 1081376 | tf_op jit(solution)/shard_map/ppermute | solution.py:464
  280.4 17.2 %collective-permute-done.43 = bf16[4224,128]{1,0:T(8,128)(2,1)S(1)} collective-permute-done((bf16[4224,128]{1,0:T(8,128)(2,1)S(1)}, bf16[4224,128]{1,0:T(8,128)(2,1)S(1)}, u32[]{:S(2)}, u32[]{:S(2)}) %collective-permute-start.43) | collective-permute-done | bytes 1081376 | tf_op jit(solution)/shard_map/ppermute | solution.py:464
  307.4 6.1 fusion.29
  313.5 4.0 fusion.33
  318.7 5.9 fusion.17
  324.6 6.0 fusion.21
  330.6 6.3 multiply_convert_fusion.2
  339.4 4.0 fusion.27
  346.0 4.5 fusion.31
  350.6 6.8 multiply_convert_fusion
  364.8 3.4 multiply_reduce_fusion
  368.2 3.7 fusion.99
  374.0 3.1 fusion.35.d_gated_ref
  377.1 8.9 %gate_back.1 = (bf16[640,1024]{1,0:T(8,128)(2,1)}, bf16[640,1024]{1,0:T(8,128)(2,1)}, f32[4,1,256]{2,1,0:T(1,128)}, f32[4,5,256,128]{3,2,1,0:T(8,128)}, bf16[4,2...) custom-call(s32[2,5]{1,0:T(2,128)} %add_convert_fusion.28.flags_ref, f32[640,1024]{1,0:T(8,128)} %fusion.35.d_gated_ref, ...), custom_call_target="tpu_custom_call" | custom-call | tf_op jit(solution)/shard_map/gate_back/pallas_call | solution.py:361
  386.0 3.7 convolution_convert_fusion.9
  389.6 3.1 fusion.39
  392.8 4.1 fusion.13
  404.1 3.3 collective-permute-start.48
  408.9 4.1 add_convert_fusion.7
  414.2 3.3 collective-permute-done.50.refs_3_
  420.0 3.8 collective-permute-done.51.refs_4_
  437.8 14.6 %mix_back.1 = (bf16[640,2048]{1,0:T(8,128)(2,1)}, bf16[640,512]{1,0:T(8,128)(2,1)}) custom-call(s32[2,5]{1,0:T(2,128)} %add_convert_fusion.28.flags_ref, bf16[640,1024]{1,0:T(8,128)(2,1)} %get-tuple-element.51.d_mixed_ref, bf16[640,2048]{1,0:T(8,128)(2,1)} %convolution_convert_fusion.qkv_ref, f32[640,512]{1,0:T(8,128)} %get-tuple-element.40.sums_ref, ...), custom_call_target="tpu_custom_call" | custom-call | tf_op jit(solution)/shard_map/mix_back/pallas_call | solution.py:400
  454.0 2.9 fusion.118
  457.3 3.3 convolution_convert_fusion.7
  461.2 9.4 %fusion.10 = (f32[1024]{0:T(1024)S(1)}, f32[640]{0:T(1024)S(1)}, f32[640,1024]{1,0:T(8,128)}) fusion(bf16[640,1024]{1,0:T(8,128)(2,1)S(1)} %constant_dynamic-update-slice_fusion, f32[640]{0:T(1024)S(1)} %get-tuple-element.266, f32[1024]{0:T(1024)S(1)} %copy-done.57, f32[640,1024]{1,0:T(8,128)} %fusion.118, f32[640,1024]{1,0:T(8,128)} %fusion.39, ...), kind=kOutput, calls=%fused_computation.43 | convolution fusion | flops 2690251264 | bytes 16004096 | tf_op jit(solution)/shard_map/dot_general | solution.py:23
  473.6 3.2 fusion.7
  477.8 4.5 collective-permute-done.57
  482.9 4.2 collective-permute-done.58
  488.5 3.4 collective-permute-done.59
  494.7 3.0 collective-permute-done.60
  501.7 2.9 add_convert_fusion.9
  509.1 2.9 add_convert_fusion.2
  512.4 3.0 add_convert_fusion.4
  515.9 2.8 add_convert_fusion.1
  538.1 16.5 %collective-permute-done.75 = bf16[1024,128]{0,1:T(8,128)(2,1)S(1)} collective-permute-done((bf16[1024,128]{0,1:T(8,128)(2,1)S(1)}, bf16[1024,128]{0,1:T(8,128)(2,1)S(1)}, u32[]{:S(2)}, u32[]{:S(2)}) %collective-permute-start.75) | collective-permute-done | bytes 262176 | tf_op jit(solution)/shard_map/ppermute | solution.py:464
  558.1 2.8 collective-permute-start.78
  562.7 3.0 collective-permute-start.71
  575.5 12.2 %collective-permute-done.104 = bf16[1408,256]{0,1:T(8,128)(2,1)} collective-permute-done((bf16[1408,256]{0,1:T(8,128)(2,1)}, bf16[1408,256]{0,1:T(8,128)(2,1)}, u32[]{:S(2)}, u32[]{:S(2)}) %collective-permute-start.104) | collective-permute-done | bytes 720928 | tf_op jit(solution)/shard_map/ppermute | solution.py:464
  592.6 10.6 %collective-permute-done.92 = bf16[1408,256]{0,1:T(8,128)(2,1)} collective-permute-done((bf16[1408,256]{0,1:T(8,128)(2,1)}, bf16[1408,256]{0,1:T(8,128)(2,1)}, u32[]{:S(2)}, u32[]{:S(2)}) %collective-permute-start.92) | collective-permute-done | bytes 720928 | tf_op jit(solution)/shard_map/ppermute | solution.py:464
  606.1 12.5 %collective-permute-done.80 = bf16[1408,256]{0,1:T(8,128)(2,1)S(1)} collective-permute-done((bf16[1408,256]{0,1:T(8,128)(2,1)}, bf16[1408,256]{0,1:T(8,128)(2,1)S(1)}, u32[]{:S(2)}, u32[]{:S(2)}) %collective-permute-start.80) | collective-permute-done | bytes 720928 | tf_op jit(solution)/shard_map/ppermute | solution.py:464
  622.6 3.5 add_convert_fusion
  629.2 4.8 collective-permute-done.99
  637.4 4.4 collective-permute-done.87
  644.5 2.9 collective-permute-start.114
  647.5 3.8 collective-permute-done.112
  661.7 2.9 collective-permute-done.96
  664.7 4.1 collective-permute-start.83
  673.3 4.0 collective-permute-start.89
  682.5 4.8 collective-permute-done.63
  689.7 2.8 collective-permute-start.66
  (736 shorter events, 325.9 us)
Async XLA Ops:
  6.4 94.3 %collective-permute-start.28 = (bf16[1056,128]{1,0:T(8,128)(2,1)}, bf16[1056,128]{1,0:T(8,128)(2,1)S(1)}, u32[]{:S(2)}, u32[]{:S(2)}) collective-permute-start(bf16[1056,128]{1,0:T(8,128)(2,1)} %pad_maximum_fusion.8), channel_id=1, source_target_pairs={{0,1},{1,2},{2,3},{3,0},{4,5},{5,6},{6,7},{7,4},{8,9},{9,10},{10,1... | collective-permute-start | bytes 811016 | tf_op jit(solution)/shard_map/ppermute | solution.py:460
  8.0 93.6 %collective-permute-start.29 = (bf16[1056,128]{1,0:T(8,128)(2,1)}, bf16[1056,128]{1,0:T(8,128)(2,1)S(1)}, u32[]{:S(2)}, u32[]{:S(2)}) collective-permute-start(bf16[1056,128]{1,0:T(8,128)(2,1)} %pad_maximum_fusion.8), channel_id=1, source_target_pairs={{0,2},{1,3},{2,0},{3,1},{4,6},{5,7},{6,4},{7,5},{8,10},{9,11},{10,... | collective-permute-start | bytes 811016 | tf_op jit(solution)/shard_map/ppermute | solution.py:460
  9.3 94.5 %collective-permute-start.30 = (bf16[1056,128]{1,0:T(8,128)(2,1)}, bf16[1056,128]{1,0:T(8,128)(2,1)S(1)}, u32[]{:S(2)}, u32[]{:S(2)}) collective-permute-start(bf16[1056,128]{1,0:T(8,128)(2,1)} %pad_maximum_fusion.8), channel_id=1, source_target_pairs={{0,3},{1,0},{2,1},{3,2},{4,7},{5,4},{6,5},{7,6},{8,11},{9,8},{10,9... | collective-permute-start | bytes 811016 | tf_op jit(solution)/shard_map/ppermute | solution.py:460
  12.7 56.8 %collective-permute-start.18 = (bf16[512,128]{1,0:T(8,128)(2,1)}, bf16[512,128]{1,0:T(8,128)(2,1)}, u32[]{:S(2)}, u32[]{:S(2)}) collective-permute-start(bf16[512,128]{1,0:T(8,128)(2,1)} %pad_maximum_fusion.15), channel_id=1, source_target_pairs={{0,1},{1,2},{2,3},{3,0},{4,5},{5,6},{6,7},{7,4},{8,9},{9,10},{10,1... | collective-permute-start | bytes 393224 | tf_op jit(solution)/shard_map/ppermute | solution.py:460
  12.9 58.1 %collective-permute-start.19 = (bf16[512,128]{1,0:T(8,128)(2,1)}, bf16[512,128]{1,0:T(8,128)(2,1)}, u32[]{:S(2)}, u32[]{:S(2)}) collective-permute-start(bf16[512,128]{1,0:T(8,128)(2,1)} %pad_maximum_fusion.15), channel_id=1, source_target_pairs={{0,2},{1,3},{2,0},{3,1},{4,6},{5,7},{6,4},{7,5},{8,10},{9,11},{10,... | collective-permute-start | bytes 393224 | tf_op jit(solution)/shard_map/ppermute | solution.py:460
  71.1 17.7 %collective-permute-start = (bf16[512,128]{0,1:T(8,128)(2,1)}, bf16[512,128]{0,1:T(8,128)(2,1)S(1)}, u32[]{:S(2)}, u32[]{:S(2)}) collective-permute-start(bf16[512,128]{0,1:T(8,128)(2,1)} %pad_maximum_fusion.14), channel_id=1, source_target_pairs={{0,1},{1,2},{2,3},{3,0},{4,5},{5,6},{6,7},{7,4},{8,9},{9,10},{10,1... | collective-permute-start | bytes 393224 | tf_op jit(solution)/shard_map/ppermute | solution.py:460
  90.5 18.0 %collective-permute-start.38 = (bf16[1056,128]{1,0:T(8,128)(2,1)S(1)}, bf16[1056,128]{1,0:T(8,128)(2,1)S(1)}, u32[]{:S(2)}, u32[]{:S(2)}) collective-permute-start(bf16[1056,128]{1,0:T(8,128)(2,1)S(1)} %copy-done.38), channel_id=1, source_target_pairs={{0,1},{1,2},{2,3},{3,0},{4,5},{5,6},{6,7},{7,4},{8,9},{9,10},{10,1... | collective-permute-start | bytes 811016 | tf_op jit(solution)/shard_map/ppermute | solution.py:460
  97.9 13.5 %collective-permute-start.39 = (bf16[1056,128]{1,0:T(8,128)(2,1)S(1)}, bf16[1056,128]{1,0:T(8,128)(2,1)S(1)}, u32[]{:S(2)}, u32[]{:S(2)}) collective-permute-start(bf16[1056,128]{1,0:T(8,128)(2,1)S(1)} %copy-done.38), channel_id=1, source_target_pairs={{0,2},{1,3},{2,0},{3,1},{4,6},{5,7},{6,4},{7,5},{8,10},{9,11},{10,... | collective-permute-start | bytes 811016 | tf_op jit(solution)/shard_map/ppermute | solution.py:460
  100.8 13.0 %collective-permute-start.40 = (bf16[1056,128]{1,0:T(8,128)(2,1)S(1)}, bf16[1056,128]{1,0:T(8,128)(2,1)S(1)}, u32[]{:S(2)}, u32[]{:S(2)}) collective-permute-start(bf16[1056,128]{1,0:T(8,128)(2,1)S(1)} %copy-done.38), channel_id=1, source_target_pairs={{0,3},{1,0},{2,1},{3,2},{4,7},{5,4},{6,5},{7,6},{8,11},{9,8},{10,9... | collective-permute-start | bytes 811016 | tf_op jit(solution)/shard_map/ppermute | solution.py:460
  101.6 31.4 %collective-permute-start.21 = (bf16[2048,128]{1,0:T(8,128)(2,1)}, bf16[2048,128]{1,0:T(8,128)(2,1)S(1)}, u32[]{:S(2)}, u32[]{:S(2)}) collective-permute-start(bf16[2048,128]{1,0:T(8,128)(2,1)} %get-tuple-element.243), channel_id=1, source_target_pairs={{0,4},{4,0},{1,5},{5,1},{2,6},{6,2},{3,7},{7,3},{8,12},{12,8},{9,1... | collective-permute-start | bytes 1572872 | tf_op jit(solution)/shard_map/ppermute | solution.py:464
  103.7 30.2 %collective-permute-start.22 = (bf16[2048,128]{1,0:T(8,128)(2,1)}, bf16[2048,128]{1,0:T(8,128)(2,1)S(1)}, u32[]{:S(2)}, u32[]{:S(2)}) collective-permute-start(bf16[2048,128]{1,0:T(8,128)(2,1)} %get-tuple-element.243), channel_id=1, source_target_pairs={{0,16},{16,0},{1,17},{17,1},{2,18},{18,2},{3,19},{19,3},{4,20},{20... | collective-permute-start | bytes 1572872 | tf_op jit(solution)/shard_map/ppermute | solution.py:464
  108.5 40.7 %collective-permute-start.24 = (bf16[2048,128]{1,0:T(8,128)(2,1)S(1)}, bf16[2048,128]{1,0:T(8,128)(2,1)S(1)}, u32[]{:S(2)}, u32[]{:S(2)}) collective-permute-start(bf16[2048,128]{1,0:T(8,128)(2,1)S(1)} %copy-done.61), channel_id=1, source_target_pairs={{0,8},{8,0},{1,9},{9,1},{2,10},{10,2},{3,11},{11,3},{4,12},{12,4},... | collective-permute-start | bytes 1572872 | tf_op jit(solution)/shard_map/ppermute | solution.py:464
  111.4 24.9 %collective-permute-start.3 = (bf16[2048,128]{0,1:T(8,128)(2,1)S(1)}, bf16[2048,128]{0,1:T(8,128)(2,1)S(1)}, u32[]{:S(2)}, u32[]{:S(2)}) collective-permute-start(bf16[2048,128]{0,1:T(8,128)(2,1)S(1)} %get-tuple-element.249), channel_id=1, source_target_pairs={{0,4},{4,0},{1,5},{5,1},{2,6},{6,2},{3,7},{7,3},{8,12},{12,8},{9,1... | collective-permute-start | bytes 1572872 | tf_op jit(solution)/shard_map/ppermute | solution.py:464
  113.8 24.1 %collective-permute-start.4 = (bf16[2048,128]{0,1:T(8,128)(2,1)S(1)}, bf16[2048,128]{0,1:T(8,128)(2,1)S(1)}, u32[]{:S(2)}, u32[]{:S(2)}) collective-permute-start(bf16[2048,128]{0,1:T(8,128)(2,1)S(1)} %get-tuple-element.249), channel_id=1, source_target_pairs={{0,16},{16,0},{1,17},{17,1},{2,18},{18,2},{3,19},{19,3},{4,20},{20... | collective-permute-start | bytes 1572872 | tf_op jit(solution)/shard_map/ppermute | solution.py:464
  133.0 40.8 %collective-permute-start.6 = (bf16[2048,128]{0,1:T(8,128)(2,1)S(1)}, bf16[2048,128]{0,1:T(8,128)(2,1)S(1)}, u32[]{:S(2)}, u32[]{:S(2)}) collective-permute-start(bf16[2048,128]{0,1:T(8,128)(2,1)S(1)} %get-tuple-element.249), channel_id=1, source_target_pairs={{0,8},{8,0},{1,9},{9,1},{2,10},{10,2},{3,11},{11,3},{4,12},{12,4},... | collective-permute-start | bytes 1572872 | tf_op jit(solution)/shard_map/ppermute | solution.py:464
  133.9 14.3 %collective-permute-start.23 = (bf16[2048,128]{1,0:T(8,128)(2,1)S(1)}, bf16[2048,128]{1,0:T(8,128)(2,1)S(1)}, u32[]{:S(2)}, u32[]{:S(2)}) collective-permute-start(bf16[2048,128]{1,0:T(8,128)(2,1)S(1)} %collective-permute-done.21), channel_id=1, source_target_pairs={{0,16},{16,0},{1,17},{17,1},{2,18},{18,2},{3,19},{19,3},{4,20},{20... | collective-permute-start | bytes 1572872 | tf_op jit(solution)/shard_map/ppermute | solution.py:464
  136.3 40.3 %collective-permute-start.31 = (bf16[4224,128]{1,0:T(8,128)(2,1)}, bf16[4224,128]{1,0:T(8,128)(2,1)}, u32[]{:S(2)}, u32[]{:S(2)}) collective-permute-start(bf16[4224,128]{1,0:T(8,128)(2,1)} %get-tuple-element.205), channel_id=1, source_target_pairs={{0,4},{4,0},{1,5},{5,1},{2,6},{6,2},{3,7},{7,3},{8,12},{12,8},{9,1... | collective-permute-start | bytes 3244040 | tf_op jit(solution)/shard_map/ppermute | solution.py:464
  137.9 13.7 %collective-permute-start.25 = (bf16[2048,128]{1,0:T(8,128)(2,1)S(1)}, bf16[2048,128]{1,0:T(8,128)(2,1)S(1)}, u32[]{:S(2)}, u32[]{:S(2)}) collective-permute-start(bf16[2048,128]{1,0:T(8,128)(2,1)S(1)} %collective-permute-done.21), channel_id=1, source_target_pairs={{0,8},{8,0},{1,9},{9,1},{2,10},{10,2},{3,11},{11,3},{4,12},{12,4},... | collective-permute-start | bytes 1572872 | tf_op jit(solution)/shard_map/ppermute | solution.py:464
  149.2 24.6 %collective-permute-start.5 = (bf16[2048,128]{0,1:T(8,128)(2,1)S(1)}, bf16[2048,128]{0,1:T(8,128)(2,1)S(1)}, u32[]{:S(2)}, u32[]{:S(2)}) collective-permute-start(bf16[2048,128]{0,1:T(8,128)(2,1)S(1)} %collective-permute-done.4), channel_id=1, source_target_pairs={{0,4},{4,0},{1,5},{5,1},{2,6},{6,2},{3,7},{7,3},{8,12},{12,8},{9,1... | collective-permute-start | bytes 1572872 | tf_op jit(solution)/shard_map/ppermute | solution.py:464
  151.5 27.7 %collective-permute-start.32 = (bf16[4224,128]{1,0:T(8,128)(2,1)}, bf16[4224,128]{1,0:T(8,128)(2,1)}, u32[]{:S(2)}, u32[]{:S(2)}) collective-permute-start(bf16[4224,128]{1,0:T(8,128)(2,1)} %get-tuple-element.205), channel_id=1, source_target_pairs={{0,16},{16,0},{1,17},{17,1},{2,18},{18,2},{3,19},{19,3},{4,20},{20... | collective-permute-start | bytes 3244040 | tf_op jit(solution)/shard_map/ppermute | solution.py:464
  153.9 20.5 %collective-permute-start.7 = (bf16[2048,128]{0,1:T(8,128)(2,1)S(1)}, bf16[2048,128]{0,1:T(8,128)(2,1)S(1)}, u32[]{:S(2)}, u32[]{:S(2)}) collective-permute-start(bf16[2048,128]{0,1:T(8,128)(2,1)S(1)} %collective-permute-done.3), channel_id=1, source_target_pairs={{0,8},{8,0},{1,9},{9,1},{2,10},{10,2},{3,11},{11,3},{4,12},{12,4},... | collective-permute-start | bytes 1572872 | tf_op jit(solution)/shard_map/ppermute | solution.py:464
  173.8 101.2 %collective-permute-start.34 = (bf16[4224,128]{1,0:T(8,128)(2,1)}, bf16[4224,128]{1,0:T(8,128)(2,1)}, u32[]{:S(2)}, u32[]{:S(2)}) collective-permute-start(bf16[4224,128]{1,0:T(8,128)(2,1)} %get-tuple-element.205), channel_id=1, source_target_pairs={{0,8},{8,0},{1,9},{9,1},{2,10},{10,2},{3,11},{11,3},{4,12},{12,4},... | collective-permute-start | bytes 3244040 | tf_op jit(solution)/shard_map/ppermute | solution.py:464
  174.4 26.1 %collective-permute-start.41 = (bf16[4224,128]{1,0:T(8,128)(2,1)}, bf16[4224,128]{1,0:T(8,128)(2,1)S(1)}, u32[]{:S(2)}, u32[]{:S(2)}) collective-permute-start(bf16[4224,128]{1,0:T(8,128)(2,1)} %get-tuple-element.211), channel_id=1, source_target_pairs={{0,4},{4,0},{1,5},{5,1},{2,6},{6,2},{3,7},{7,3},{8,12},{12,8},{9,1... | collective-permute-start | bytes 3244040 | tf_op jit(solution)/shard_map/ppermute | solution.py:464
  176.0 25.8 %collective-permute-start.42 = (bf16[4224,128]{1,0:T(8,128)(2,1)}, bf16[4224,128]{1,0:T(8,128)(2,1)S(1)}, u32[]{:S(2)}, u32[]{:S(2)}) collective-permute-start(bf16[4224,128]{1,0:T(8,128)(2,1)} %get-tuple-element.211), channel_id=1, source_target_pairs={{0,16},{16,0},{1,17},{17,1},{2,18},{18,2},{3,19},{19,3},{4,20},{20... | collective-permute-start | bytes 3244040 | tf_op jit(solution)/shard_map/ppermute | solution.py:464
  176.7 53.8 %collective-permute-start.27 = (bf16[2048,128]{1,0:T(8,128)(2,1)S(1)}, bf16[2048,128]{1,0:T(8,128)(2,1)S(1)}, u32[]{:S(2)}, u32[]{:S(2)}) collective-permute-start(bf16[2048,128]{1,0:T(8,128)(2,1)S(1)} %collective-permute-done.23), channel_id=1, source_target_pairs={{0,8},{8,0},{1,9},{9,1},{2,10},{10,2},{3,11},{11,3},{4,12},{12,4},... | collective-permute-start | bytes 1572872 | tf_op jit(solution)/shard_map/ppermute | solution.py:464
  179.2 23.8 %collective-permute-start.9 = (bf16[2048,128]{0,1:T(8,128)(2,1)S(1)}, bf16[2048,128]{0,1:T(8,128)(2,1)S(1)}, u32[]{:S(2)}, u32[]{:S(2)}) collective-permute-start(bf16[2048,128]{0,1:T(8,128)(2,1)S(1)} %collective-permute-done.5), channel_id=1, source_target_pairs={{0,8},{8,0},{1,9},{9,1},{2,10},{10,2},{3,11},{11,3},{4,12},{12,4},... | collective-permute-start | bytes 1572872 | tf_op jit(solution)/shard_map/ppermute | solution.py:464
  225.4 21.7 %collective-permute-start.17 = (bf16[4,256,128]{2,1,0:T(8,128)(2,1)}, bf16[4,256,128]{2,1,0:T(8,128)(2,1)}, u32[]{:S(2)}, u32[]{:S(2)}) collective-permute-start(bf16[4,256,128]{2,1,0:T(8,128)(2,1)} %slice_bitcast_fusion), channel_id=1, source_target_pairs={{1,0},{3,2},{5,4},{7,6},{9,8},{11,10},{13,12},{15,14},{17,16},{19,... | collective-permute-start | bytes 786440 | tf_op jit(solution)/shard_map/ppermute | solution.py:483
  245.5 56.1 %collective-permute-start.44 = (bf16[4224,128]{1,0:T(8,128)(2,1)}, bf16[4224,128]{1,0:T(8,128)(2,1)}, u32[]{:S(2)}, u32[]{:S(2)}) collective-permute-start(bf16[4224,128]{1,0:T(8,128)(2,1)} %get-tuple-element.211), channel_id=1, source_target_pairs={{0,8},{8,0},{1,9},{9,1},{2,10},{10,2},{3,11},{11,3},{4,12},{12,4},... | collective-permute-start | bytes 3244040 | tf_op jit(solution)/shard_map/ppermute | solution.py:464
  245.5 26.6 %collective-permute-start.33 = (bf16[4224,128]{1,0:T(8,128)(2,1)}, bf16[4224,128]{1,0:T(8,128)(2,1)}, u32[]{:S(2)}, u32[]{:S(2)}) collective-permute-start(bf16[4224,128]{1,0:T(8,128)(2,1)} %collective-permute-done.32), channel_id=1, source_target_pairs={{0,4},{4,0},{1,5},{5,1},{2,6},{6,2},{3,7},{7,3},{8,12},{12,8},{9,1... | collective-permute-start | bytes 3244040 | tf_op jit(solution)/shard_map/ppermute | solution.py:464
  246.2 31.3 %collective-permute-start.35 = (bf16[4224,128]{1,0:T(8,128)(2,1)}, bf16[4224,128]{1,0:T(8,128)(2,1)}, u32[]{:S(2)}, u32[]{:S(2)}) collective-permute-start(bf16[4224,128]{1,0:T(8,128)(2,1)} %collective-permute-done.31), channel_id=1, source_target_pairs={{0,8},{8,0},{1,9},{9,1},{2,10},{10,2},{3,11},{11,3},{4,12},{12,4},... | collective-permute-start | bytes 3244040 | tf_op jit(solution)/shard_map/ppermute | solution.py:464
  247.1 51.7 %collective-permute-start.36 = (bf16[4224,128]{1,0:T(8,128)(2,1)}, bf16[4224,128]{1,0:T(8,128)(2,1)}, u32[]{:S(2)}, u32[]{:S(2)}) collective-permute-start(bf16[4224,128]{1,0:T(8,128)(2,1)} %collective-permute-done.32), channel_id=1, source_target_pairs={{0,8},{8,0},{1,9},{9,1},{2,10},{10,2},{3,11},{11,3},{4,12},{12,4},... | collective-permute-start | bytes 3244040 | tf_op jit(solution)/shard_map/ppermute | solution.py:464
  272.1 25.4 %collective-permute-start.43 = (bf16[4224,128]{1,0:T(8,128)(2,1)S(1)}, bf16[4224,128]{1,0:T(8,128)(2,1)S(1)}, u32[]{:S(2)}, u32[]{:S(2)}) collective-permute-start(bf16[4224,128]{1,0:T(8,128)(2,1)S(1)} %copy-done.24), channel_id=1, source_target_pairs={{0,16},{16,0},{1,17},{17,1},{2,18},{18,2},{3,19},{19,3},{4,20},{20... | collective-permute-start | bytes 3244040 | tf_op jit(solution)/shard_map/ppermute | solution.py:464
  275.1 28.9 %collective-permute-start.45 = (bf16[4224,128]{1,0:T(8,128)(2,1)S(1)}, bf16[4224,128]{1,0:T(8,128)(2,1)S(1)}, u32[]{:S(2)}, u32[]{:S(2)}) collective-permute-start(bf16[4224,128]{1,0:T(8,128)(2,1)S(1)} %copy-done.24), channel_id=1, source_target_pairs={{0,8},{8,0},{1,9},{9,1},{2,10},{10,2},{3,11},{11,3},{4,12},{12,4},... | collective-permute-start | bytes 3244040 | tf_op jit(solution)/shard_map/ppermute | solution.py:464
  277.5 27.7 %collective-permute-start.46 = (bf16[4224,128]{1,0:T(8,128)(2,1)S(1)}, bf16[4224,128]{1,0:T(8,128)(2,1)S(1)}, u32[]{:S(2)}, u32[]{:S(2)}) collective-permute-start(bf16[4224,128]{1,0:T(8,128)(2,1)S(1)} %copy-done.26), channel_id=1, source_target_pairs={{0,8},{8,0},{1,9},{9,1},{2,10},{10,2},{3,11},{11,3},{4,12},{12,4},... | collective-permute-start | bytes 3244040 | tf_op jit(solution)/shard_map/ppermute | solution.py:464
  298.7 18.8 %collective-permute-start.47 = (bf16[4224,128]{1,0:T(8,128)(2,1)S(1)}, bf16[4224,128]{1,0:T(8,128)(2,1)S(1)}, u32[]{:S(2)}, u32[]{:S(2)}) collective-permute-start(bf16[4224,128]{1,0:T(8,128)(2,1)S(1)} %collective-permute-done.43), channel_id=1, source_target_pairs={{0,8},{8,0},{1,9},{9,1},{2,10},{10,2},{3,11},{11,3},{4,12},{12,4},... | collective-permute-start | bytes 3244040 | tf_op jit(solution)/shard_map/ppermute | solution.py:464
  402.1 105.3 %collective-permute-start.103 = (bf16[1408,512]{0,1:T(8,128)(2,1)}, bf16[1408,512]{0,1:T(8,128)(2,1)}, u32[]{:S(2)}, u32[]{:S(2)}) collective-permute-start(bf16[1408,512]{0,1:T(8,128)(2,1)} %convolution_convert_fusion.2), channel_id=1, source_target_pairs={{0,8},{8,0},{1,9},{9,1},{2,10},{10,2},{3,11},{11,3},{4,12},{12,4},... | collective-permute-start | bytes 4325384 | tf_op jit(solution)/shard_map/ppermute | solution.py:464
  402.1 33.1 %collective-permute-start.55 = (bf16[4,256,128]{2,1,0:T(8,128)(2,1)}, bf16[4,256,128]{2,1,0:T(8,128)(2,1)}, u32[]{:S(2)}, u32[]{:S(2)}) collective-permute-start(bf16[4,256,128]{2,1,0:T(8,128)(2,1)} %get-tuple-element.59), channel_id=1, source_target_pairs={{0,1},{2,3},{4,5},{6,7},{8,9},{10,11},{12,13},{14,15},{16,17},{18,... | collective-permute-start | bytes 786440 | tf_op jit(solution)/shard_map/ppermute | solution.py:485
  431.3 84.0 %collective-permute-start.109 = (bf16[1408,512]{0,1:T(8,128)(2,1)}, bf16[1408,512]{0,1:T(8,128)(2,1)}, u32[]{:S(2)}, u32[]{:S(2)}) collective-permute-start(bf16[1408,512]{0,1:T(8,128)(2,1)} %convolution_convert_fusion.1), channel_id=1, source_target_pairs={{0,8},{8,0},{1,9},{9,1},{2,10},{10,2},{3,11},{11,3},{4,12},{12,4},... | collective-permute-start | bytes 4325384 | tf_op jit(solution)/shard_map/ppermute | solution.py:464
  432.6 72.1 %collective-permute-start.73 = (bf16[1024,512]{0,1:T(8,128)(2,1)}, bf16[1024,512]{0,1:T(8,128)(2,1)}, u32[]{:S(2)}, u32[]{:S(2)}) collective-permute-start(bf16[1024,512]{0,1:T(8,128)(2,1)} %convolution_convert_fusion.8), channel_id=1, source_target_pairs={{0,8},{8,0},{1,9},{9,1},{2,10},{10,2},{3,11},{11,3},{4,12},{12,4},... | collective-permute-start | bytes 3145736 | tf_op jit(solution)/shard_map/ppermute | solution.py:464
  433.7 67.5 %collective-permute-start.67 = (bf16[1024,512]{1,0:T(8,128)(2,1)}, bf16[1024,512]{1,0:T(8,128)(2,1)}, u32[]{:S(2)}, u32[]{:S(2)}) collective-permute-start(bf16[1024,512]{1,0:T(8,128)(2,1)} %convolution_convert_fusion.9), channel_id=1, source_target_pairs={{0,8},{8,0},{1,9},{9,1},{2,10},{10,2},{3,11},{11,3},{4,12},{12,4},... | collective-permute-start | bytes 3145736 | tf_op jit(solution)/shard_map/ppermute | solution.py:464
  497.7 14.3 %collective-permute-start.91 = (bf16[1408,512]{0,1:T(8,128)(2,1)}, bf16[1408,512]{0,1:T(8,128)(2,1)}, u32[]{:S(2)}, u32[]{:S(2)}) collective-permute-start(bf16[1408,512]{0,1:T(8,128)(2,1)} %convolution_convert_fusion.4), channel_id=1, source_target_pairs={{0,8},{8,0},{1,9},{9,1},{2,10},{10,2},{3,11},{11,3},{4,12},{12,4},... | collective-permute-start | bytes 4325384 | tf_op jit(solution)/shard_map/ppermute | solution.py:464
  501.1 18.6 %collective-permute-start.97 = (bf16[1408,512]{0,1:T(8,128)(2,1)}, bf16[1408,512]{0,1:T(8,128)(2,1)S(1)}, u32[]{:S(2)}, u32[]{:S(2)}) collective-permute-start(bf16[1408,512]{0,1:T(8,128)(2,1)} %convolution_convert_fusion.3), channel_id=1, source_target_pairs={{0,8},{8,0},{1,9},{9,1},{2,10},{10,2},{3,11},{11,3},{4,12},{12,4},... | collective-permute-start | bytes 4325384 | tf_op jit(solution)/shard_map/ppermute | solution.py:464
  504.7 18.8 %collective-permute-start.79 = (bf16[1408,512]{0,1:T(8,128)(2,1)S(1)}, bf16[1408,512]{0,1:T(8,128)(2,1)S(1)}, u32[]{:S(2)}, u32[]{:S(2)}) collective-permute-start(bf16[1408,512]{0,1:T(8,128)(2,1)S(1)} %copy-done.86), channel_id=1, source_target_pairs={{0,8},{8,0},{1,9},{9,1},{2,10},{10,2},{3,11},{11,3},{4,12},{12,4},... | collective-permute-start | bytes 4325384 | tf_op jit(solution)/shard_map/ppermute | solution.py:464
  508.6 18.3 %collective-permute-start.85 = (bf16[1408,512]{0,1:T(8,128)(2,1)S(1)}, bf16[1408,512]{0,1:T(8,128)(2,1)S(1)}, u32[]{:S(2)}, u32[]{:S(2)}) collective-permute-start(bf16[1408,512]{0,1:T(8,128)(2,1)S(1)} %copy-done.85), channel_id=1, source_target_pairs={{0,8},{8,0},{1,9},{9,1},{2,10},{10,2},{3,11},{11,3},{4,12},{12,4},... | collective-permute-start | bytes 4325384 | tf_op jit(solution)/shard_map/ppermute | solution.py:464
  512.0 109.0 %collective-permute-start.61 = (bf16[2048,512]{0,1:T(8,128)(2,1)}, bf16[2048,512]{0,1:T(8,128)(2,1)}, u32[]{:S(2)}, u32[]{:S(2)}) collective-permute-start(bf16[2048,512]{0,1:T(8,128)(2,1)} %convolution_convert_fusion.7), channel_id=1, source_target_pairs={{0,8},{8,0},{1,9},{9,1},{2,10},{10,2},{3,11},{11,3},{4,12},{12,4},... | collective-permute-start | bytes 6291464 | tf_op jit(solution)/shard_map/ppermute | solution.py:464
  515.4 19.3 %collective-permute-start.74 = (bf16[1024,256]{0,1:T(8,128)(2,1)S(1)}, bf16[1024,256]{0,1:T(8,128)(2,1)S(1)}, u32[]{:S(2)}, u32[]{:S(2)}) collective-permute-start(bf16[1024,256]{0,1:T(8,128)(2,1)S(1)} %pad_maximum_fusion.6), channel_id=1, source_target_pairs={{0,4},{4,0},{1,5},{5,1},{2,6},{6,2},{3,7},{7,3},{8,12},{12,8},{9,1... | collective-permute-start | bytes 1572872 | tf_op jit(solution)/shard_map/ppermute | solution.py:464
  519.7 16.6 %collective-permute-start.68 = (bf16[1024,256]{1,0:T(8,128)(2,1)S(1)}, bf16[1024,256]{1,0:T(8,128)(2,1)S(1)}, u32[]{:S(2)}, u32[]{:S(2)}) collective-permute-start(bf16[1024,256]{1,0:T(8,128)(2,1)S(1)} %concatenate.212), channel_id=1, source_target_pairs={{0,16},{16,0},{1,17},{17,1},{2,18},{18,2},{3,19},{19,3},{4,20},{20... | collective-permute-start | bytes 1572872 | tf_op jit(solution)/shard_map/ppermute | solution.py:464
  523.5 49.1 %collective-permute-start.110 = (bf16[1408,256]{0,1:T(8,128)(2,1)}, bf16[1408,256]{0,1:T(8,128)(2,1)}, u32[]{:S(2)}, u32[]{:S(2)}) collective-permute-start(bf16[1408,256]{0,1:T(8,128)(2,1)} %concatenate.218), channel_id=1, source_target_pairs={{0,16},{16,0},{1,17},{17,1},{2,18},{18,2},{3,19},{19,3},{4,20},{20... | collective-permute-start | bytes 2162696 | tf_op jit(solution)/shard_map/ppermute | solution.py:464
  534.9 19.6 %collective-permute-start.75 = (bf16[1024,128]{0,1:T(8,128)(2,1)S(1)}, bf16[1024,128]{0,1:T(8,128)(2,1)S(1)}, u32[]{:S(2)}, u32[]{:S(2)}) collective-permute-start(bf16[1024,128]{0,1:T(8,128)(2,1)S(1)} %slice.726), channel_id=1, source_target_pairs={{0,16},{16,0},{1,17},{17,1},{2,18},{18,2},{3,19},{19,3},{4,20},{20... | collective-permute-start | bytes 786440 | tf_op jit(solution)/shard_map/ppermute | solution.py:464
  536.5 21.6 %collective-permute-start.69 = (bf16[1024,128]{1,0:T(8,128)(2,1)S(1)}, bf16[1024,128]{1,0:T(8,128)(2,1)S(1)}, u32[]{:S(2)}, u32[]{:S(2)}) collective-permute-start(bf16[1024,128]{1,0:T(8,128)(2,1)S(1)} %slice.710), channel_id=1, source_target_pairs={{0,4},{4,0},{1,5},{5,1},{2,6},{6,2},{3,7},{7,3},{8,12},{12,8},{9,1... | collective-permute-start | bytes 786440 | tf_op jit(solution)/shard_map/ppermute | solution.py:464
  568.4 19.4 %collective-permute-start.104 = (bf16[1408,256]{0,1:T(8,128)(2,1)}, bf16[1408,256]{0,1:T(8,128)(2,1)}, u32[]{:S(2)}, u32[]{:S(2)}) collective-permute-start(bf16[1408,256]{0,1:T(8,128)(2,1)} %pad_maximum_fusion.3), channel_id=1, source_target_pairs={{0,4},{4,0},{1,5},{5,1},{2,6},{6,2},{3,7},{7,3},{8,12},{12,8},{9,1... | collective-permute-start | bytes 2162696 | tf_op jit(solution)/shard_map/ppermute | solution.py:464
  569.8 33.4 %collective-permute-start.92 = (bf16[1408,256]{0,1:T(8,128)(2,1)}, bf16[1408,256]{0,1:T(8,128)(2,1)}, u32[]{:S(2)}, u32[]{:S(2)}) collective-permute-start(bf16[1408,256]{0,1:T(8,128)(2,1)} %pad_maximum_fusion.2), channel_id=1, source_target_pairs={{0,4},{4,0},{1,5},{5,1},{2,6},{6,2},{3,7},{7,3},{8,12},{12,8},{9,1... | collective-permute-start | bytes 2162696 | tf_op jit(solution)/shard_map/ppermute | solution.py:464
  570.4 19.3 %collective-permute-start.98 = (bf16[1408,256]{0,1:T(8,128)(2,1)}, bf16[1408,256]{0,1:T(8,128)(2,1)}, u32[]{:S(2)}, u32[]{:S(2)}) collective-permute-start(bf16[1408,256]{0,1:T(8,128)(2,1)} %concatenate.216), channel_id=1, source_target_pairs={{0,16},{16,0},{1,17},{17,1},{2,18},{18,2},{3,19},{19,3},{4,20},{20... | collective-permute-start | bytes 2162696 | tf_op jit(solution)/shard_map/ppermute | solution.py:464
  572.7 45.9 %collective-permute-start.80 = (bf16[1408,256]{0,1:T(8,128)(2,1)}, bf16[1408,256]{0,1:T(8,128)(2,1)S(1)}, u32[]{:S(2)}, u32[]{:S(2)}) collective-permute-start(bf16[1408,256]{0,1:T(8,128)(2,1)} %pad_maximum_fusion.1), channel_id=1, source_target_pairs={{0,4},{4,0},{1,5},{5,1},{2,6},{6,2},{3,7},{7,3},{8,12},{12,8},{9,1... | collective-permute-start | bytes 2162696 | tf_op jit(solution)/shard_map/ppermute | solution.py:464
  587.8 31.6 %collective-permute-start.86 = (bf16[1408,256]{0,1:T(8,128)(2,1)S(1)}, bf16[1408,256]{0,1:T(8,128)(2,1)S(1)}, u32[]{:S(2)}, u32[]{:S(2)}) collective-permute-start(bf16[1408,256]{0,1:T(8,128)(2,1)S(1)} %copy-done.27), channel_id=1, source_target_pairs={{0,16},{16,0},{1,17},{17,1},{2,18},{18,2},{3,19},{19,3},{4,20},{20... | collective-permute-start | bytes 2162696 | tf_op jit(solution)/shard_map/ppermute | solution.py:464
  589.7 36.7 %collective-permute-start.105 = (bf16[1408,128]{0,1:T(8,128)(2,1)S(1)}, bf16[1408,128]{0,1:T(8,128)(2,1)S(1)}, u32[]{:S(2)}, u32[]{:S(2)}) collective-permute-start(bf16[1408,128]{0,1:T(8,128)(2,1)S(1)} %slice.771), channel_id=1, source_target_pairs={{0,16},{16,0},{1,17},{17,1},{2,18},{18,2},{3,19},{19,3},{4,20},{20... | collective-permute-start | bytes 1081352 | tf_op jit(solution)/shard_map/ppermute | solution.py:464
  603.2 23.9 %collective-permute-start.111 = (bf16[1408,128]{0,1:T(8,128)(2,1)S(1)}, bf16[1408,128]{0,1:T(8,128)(2,1)S(1)}, u32[]{:S(2)}, u32[]{:S(2)}) collective-permute-start(bf16[1408,128]{0,1:T(8,128)(2,1)S(1)} %slice.777), channel_id=1, source_target_pairs={{0,4},{4,0},{1,5},{5,1},{2,6},{6,2},{3,7},{7,3},{8,12},{12,8},{9,1... | collective-permute-start | bytes 1081352 | tf_op jit(solution)/shard_map/ppermute | solution.py:464
  619.4 14.6 %collective-permute-start.99 = (bf16[1408,128]{0,1:T(8,128)(2,1)S(1)}, bf16[1408,128]{0,1:T(8,128)(2,1)S(1)}, u32[]{:S(2)}, u32[]{:S(2)}) collective-permute-start(bf16[1408,128]{0,1:T(8,128)(2,1)S(1)} %slice.761), channel_id=1, source_target_pairs={{0,4},{4,0},{1,5},{5,1},{2,6},{6,2},{3,7},{7,3},{8,12},{12,8},{9,1... | collective-permute-start | bytes 1081352 | tf_op jit(solution)/shard_map/ppermute | solution.py:464
  621.1 15.8 %collective-permute-start.81 = (bf16[1408,128]{0,1:T(8,128)(2,1)S(1)}, bf16[1408,128]{0,1:T(8,128)(2,1)S(1)}, u32[]{:S(2)}, u32[]{:S(2)}) collective-permute-start(bf16[1408,128]{0,1:T(8,128)(2,1)S(1)} %slice.739), channel_id=1, source_target_pairs={{0,16},{16,0},{1,17},{17,1},{2,18},{18,2},{3,19},{19,3},{4,20},{20... | collective-permute-start | bytes 1081352 | tf_op jit(solution)/shard_map/ppermute | solution.py:464
  626.4 15.3 %collective-permute-start.87 = (bf16[1408,128]{0,1:T(8,128)(2,1)S(1)}, bf16[1408,128]{0,1:T(8,128)(2,1)S(1)}, u32[]{:S(2)}, u32[]{:S(2)}) collective-permute-start(bf16[1408,128]{0,1:T(8,128)(2,1)S(1)} %slice.745), channel_id=1, source_target_pairs={{0,4},{4,0},{1,5},{5,1},{2,6},{6,2},{3,7},{7,3},{8,12},{12,8},{9,1... | collective-permute-start | bytes 1081352 | tf_op jit(solution)/shard_map/ppermute | solution.py:464
  627.1 46.1 %collective-permute-start.62 = (bf16[2048,256]{0,1:T(8,128)(2,1)S(1)}, bf16[2048,256]{0,1:T(8,128)(2,1)S(1)}, u32[]{:S(2)}, u32[]{:S(2)}) collective-permute-start(bf16[2048,256]{0,1:T(8,128)(2,1)S(1)} %pad_maximum_fusion), channel_id=1, source_target_pairs={{0,4},{4,0},{1,5},{5,1},{2,6},{6,2},{3,7},{7,3},{8,12},{12,8},{9,1... | collective-permute-start | bytes 3145736 | tf_op jit(solution)/shard_map/ppermute | solution.py:464
  628.9 13.2 %collective-permute-start.106 = (bf16[352,128]{0,1:T(8,128)(2,1)S(1)}, bf16[352,128]{0,1:T(8,128)(2,1)S(1)}, u32[]{:S(2)}, u32[]{:S(2)}) collective-permute-start(bf16[352,128]{0,1:T(8,128)(2,1)S(1)} %get-tuple-element.179), channel_id=1, source_target_pairs={{0,3},{1,0},{2,1},{3,2},{4,7},{5,4},{6,5},{7,6},{8,11},{9,8},{10,9... | collective-permute-start | bytes 270344 | tf_op jit(solution)/shard_map/ppermute | solution.py:460
  664.6 13.1 %collective-permute-start.82 = (bf16[352,128]{0,1:T(8,128)(2,1)S(1)}, bf16[352,128]{0,1:T(8,128)(2,1)S(1)}, u32[]{:S(2)}, u32[]{:S(2)}) collective-permute-start(bf16[352,128]{0,1:T(8,128)(2,1)S(1)} %get-tuple-element.191), channel_id=1, source_target_pairs={{0,3},{1,0},{2,1},{3,2},{4,7},{5,4},{6,5},{7,6},{8,11},{9,8},{10,9... | collective-permute-start | bytes 270344 | tf_op jit(solution)/shard_map/ppermute | solution.py:460
  664.7 13.4 %collective-permute-start.83 = (bf16[352,128]{0,1:T(8,128)(2,1)S(1)}, bf16[352,128]{0,1:T(8,128)(2,1)S(1)}, u32[]{:S(2)}, u32[]{:S(2)}) collective-permute-start(bf16[352,128]{0,1:T(8,128)(2,1)S(1)} %get-tuple-element.193), channel_id=1, source_target_pairs={{0,2},{1,3},{2,0},{3,1},{4,6},{5,7},{6,4},{7,5},{8,10},{9,11},{10,... | collective-permute-start | bytes 270344 | tf_op jit(solution)/shard_map/ppermute | solution.py:460
  (157 other events, 1551.7 us)

commit v2 on v1

--- a/solution.py
+++ b/solution.py
@@ -52,7 +52,7 @@
     return jnp.concatenate([state, extra], axis=0).astype(BF16)
 
 
-def states_kernel(chunks, qkv_ref, gate_ref, sums_ref, local_ref, future_ref, end_ref):
+def states_kernel(chunks, qk_ref, value_ref, gate_ref, sums_ref, local_ref, future_ref, end_ref):
     lower = (iota2(0) >= iota2(1)).astype(BF16)
     state = jnp.zeros((DV, DK), F32)
     total = jnp.zeros((1, DK), F32)
@@ -65,8 +65,8 @@
         sums = split_dot(lower, gate_log, 3)
         sums_ref[rows, :] = sums
         last = sums[CHUNK - 1 : CHUNK, :]
-        key_rows = qkv_ref[rows, DK : 2 * DK].astype(F32)
-        value_rows = qkv_ref[rows, 2 * DK :]
+        key_rows = qk_ref[rows, DK:].astype(F32)
+        value_rows = value_ref[rows, :]
         local_ref[0, j] = state
         both = jnp.concatenate(
             [(key_rows * jnp.exp(last - sums)).astype(BF16), (key_rows * jnp.exp(sums)).astype(BF16)],
@@ -101,7 +101,8 @@
 def mix_kernel(
     chunks,
     flags_ref,
-    qkv_ref,
+    qk_ref,
+    value_ref,
     sums_ref,
     local_ref,
     incoming_ref,
@@ -119,9 +120,9 @@
         rows = pl.ds(j * CHUNK, CHUNK)
         sums = sums_ref[rows, :]
         last = sums[CHUNK - 1 : CHUNK, :]
-        queries = qkv_ref[rows, :DK].astype(F32) * DK**-0.5
-        key_rows = qkv_ref[rows, DK : 2 * DK].astype(F32)
-        value_rows = qkv_ref[rows, 2 * DK :]
+        queries = qk_ref[rows, :DK].astype(F32) * DK**-0.5
+        key_rows = qk_ref[rows, DK:].astype(F32)
+        value_rows = value_ref[rows, :]
         scores = scores_of(queries, key_rows, sums, flags_ref[0, j])[0]
         state = (local_ref[0, j] + incoming * jnp.exp(before)).astype(BF16)
         later = later_ref[0] if j == chunks - 1 else future_ref[0, j + 1]
@@ -150,7 +151,7 @@
     outgate_ref,
     mixed_ref,
     gain_ref,
-    qkv_ref,
+    qk_ref,
     sums_ref,
     d_outgate_ref,
     d_mixed_ref,
@@ -181,7 +182,7 @@
         d_mixed_ref[rows, :] = d_low
         sums = sums_ref[rows, :]
         last = sums[CHUNK - 1 : CHUNK, :]
-        queries = qkv_ref[rows, :DK].astype(F32) * DK**-0.5
+        queries = qk_ref[rows, :DK].astype(F32) * DK**-0.5
         local_ref[0, j] = state
         update = tn(d_low, (queries * jnp.exp(sums)).astype(BF16))
         if j == chunks - 1:
@@ -199,7 +200,8 @@
     chunks,
     flags_ref,
     d_mixed_ref,
-    qkv_ref,
+    qk_ref,
+    value_ref,
     sums_ref,
     local_ref,
     incoming_ref,
@@ -209,7 +211,8 @@
     back_incoming_ref,
     earlier_ref,
     gate_ref,
-    d_qkv_ref,
+    d_qk_ref,
+    d_value_ref,
     d_gate_ref,
 ):
     incoming = incoming_ref[0].astype(F32)
@@ -226,9 +229,9 @@
         after = jnp.zeros((1, DK), F32)
         for l in range(j + 1, chunks):
             after = after + lasts[l]
-        queries = qkv_ref[rows, :DK].astype(F32) * DK**-0.5
-        key_rows = qkv_ref[rows, DK : 2 * DK].astype(F32)
-        value_rows = qkv_ref[rows, 2 * DK :]
+        queries = qk_ref[rows, :DK].astype(F32) * DK**-0.5
+        key_rows = qk_ref[rows, DK:].astype(F32)
+        value_rows = value_ref[rows, :]
         d_mixed = d_mixed_ref[rows, :]
         scores, q1, k1, q2, k2, grow, shrink, above = scores_of(
             queries, key_rows, sums, flags_ref[0, j]
@@ -270,13 +273,13 @@
         d_log = split_dot(upper, d_sums, 2) + d_last
         gate_in = gate_ref[rows, :]
         d_gate_ref[rows, :] = (d_log * jax.nn.sigmoid(-gate_in) * (1.0 / GATE_NORM)).astype(BF16)
-        d_qkv_ref[rows, :DK] = (
+        d_qk_ref[rows, :DK] = (
             (dq_causal + dq_ahead + dq_later + on_diagonal * key_rows) * DK**-0.5
         ).astype(BF16)
-        d_qkv_ref[rows, DK : 2 * DK] = (
+        d_qk_ref[rows, DK:] = (
             dk_causal + dk_ahead + dk_state + dk_earlier + on_diagonal * queries
         ).astype(BF16)
-        d_qkv_ref[rows, 2 * DK :] = d_values.astype(BF16)
+        d_value_ref[rows, :] = d_values.astype(BF16)
         before = before + last
 
 
@@ -304,14 +307,13 @@
     return jax.ShapeDtypeStruct(shape, kind)
 
 
-def chunk_states(qkv, gate_in, heads):
-    length = qkv.shape[0]
+def chunk_states(qk, values, gate_in, heads):
+    length = qk.shape[0]
     chunks = length // CHUNK
-    width = 2 * DK + DV
     return pl.pallas_call(
         functools.partial(states_kernel, chunks),
         grid=(heads,),
-        in_specs=[rows_block(length, width), rows_block(length, DK)],
+        in_specs=[rows_block(length, 2 * DK), rows_block(length, DV), rows_block(length, DK)],
         out_specs=[
             rows_block(length, DK),
             lead_block(chunks, DV, DK),
@@ -326,19 +328,19 @@
         ],
         compiler_params=params(),
         name="chunk_states",
-    )(qkv, gate_in)
-
-
-def mix(flags, qkv, sums, local, incoming, future, later, outgate, gain):
-    length = qkv.shape[0]
+    )(qk, values, gate_in)
+
+
+def mix(flags, qk, values, sums, local, incoming, future, later, outgate, gain):
+    length = qk.shape[0]
     heads, chunks = local.shape[:2]
-    width = 2 * DK + DV
     return pl.pallas_call(
         functools.partial(mix_kernel, chunks),
         grid=(heads,),
         in_specs=[
             smem(),
-            rows_block(length, width),
+            rows_block(length, 2 * DK),
+            rows_block(length, DV),
             rows_block(length, DK),
             lead_block(chunks, DV, DK),
             lead_block(DV, DK),
@@ -351,13 +353,12 @@
         out_shape=[shaped((length, heads * DV), F32), shaped((length, heads * DV), BF16)],
         compiler_params=params(),
         name="mix",
-    )(flags, qkv, sums, local, incoming, future, later, outgate, gain)
-
-
-def gate_back(flags, d_gated, outgate, mixed, gain, qkv, sums, heads):
-    length = qkv.shape[0]
+    )(flags, qk, values, sums, local, incoming, future, later, outgate, gain)
+
+
+def gate_back(flags, d_gated, outgate, mixed, gain, qk, sums, heads):
+    length = qk.shape[0]
     chunks = length // CHUNK
-    width = 2 * DK + DV
     return pl.pallas_call(
         functools.partial(gate_back_kernel, chunks),
         grid=(heads,),
@@ -367,7 +368,7 @@
             rows_block(length, DV),
             rows_block(length, DV),
             whole_block(1, DV),
-            rows_block(length, width),
+            rows_block(length, 2 * DK),
             rows_block(length, DK),
         ],
         out_specs=[
@@ -388,22 +389,22 @@
         ],
         compiler_params=params(),
         name="gate_back",
-    )(flags, d_gated, outgate, mixed, gain, qkv, sums)
+    )(flags, d_gated, outgate, mixed, gain, qk, sums)
 
 
 def mix_back(
-    flags, d_mixed, qkv, sums, local, incoming, future, later, back_local, back_incoming, earlier, gate_in
+    flags, d_mixed, qk, values, sums, local, incoming, future, later, back_local, back_incoming, earlier, gate_in
 ):
-    length = qkv.shape[0]
+    length = qk.shape[0]
     heads, chunks = local.shape[:2]
-    width = 2 * DK + DV
     return pl.pallas_call(
         functools.partial(mix_back_kernel, chunks),
         grid=(heads,),
         in_specs=[
             smem(),
             rows_block(length, DV),
-            rows_block(length, width),
+            rows_block(length, 2 * DK),
+            rows_block(length, DV),
             rows_block(length, DK),
             lead_block(chunks, DV, DK),
             lead_block(DV, DK),
@@ -414,12 +415,16 @@
             lead_block(DV, DK),
             rows_block(length, DK),
         ],
-        out_specs=[rows_block(length, width), rows_block(length, DK)],
-        out_shape=[shaped((length, heads * width), BF16), shaped((length, heads * DK), BF16)],
+        out_specs=[rows_block(length, 2 * DK), rows_block(length, DV), rows_block(length, DK)],
+        out_shape=[
+            shaped((length, heads * 2 * DK), BF16),
+            shaped((length, heads * DV), BF16),
+            shaped((length, heads * DK), BF16),
+        ],
         compiler_params=params(),
         name="mix_back",
     )(
-        flags, d_mixed, qkv, sums, local, incoming, future, later, back_local, back_incoming, earlier, gate_in
+        flags, d_mixed, qk, values, sums, local, incoming, future, later, back_local, back_incoming, earlier, gate_in
     )
 
 
@@ -486,114 +491,434 @@
     return jnp.concatenate([moved[-1:], moved[:-1]], axis=0)
 
 
+def take_columns(ref, order_ref, out_ref):
+    for j in range(8):
+        out_ref[:, j * 128 : (j + 1) * 128] = ref[:, pl.ds(pl.multiple_of(order_ref[j] * 128, 128), 128)]
+
+
+def begin_kernel(
+    heads,
+    order_ref,
+    hidden_ref,
+    cot_ref,
+    gain_one_ref,
+    gain_two_ref,
+    rank_in_ref,
+    rank_out_ref,
+    bias_ref,
+    inputs_ref,
+    upstream_ref,
+    normed_ref,
+    new_one_ref,
+    new_two_ref,
+    new_rank_in_ref,
+    new_rank_out_ref,
+    new_bias_ref,
+):
+    take_columns(gain_one_ref, order_ref, new_one_ref)
+    take_columns(gain_two_ref, order_ref, new_two_ref)
+    for j in range(8):
+        new_rank_in_ref[j * 128 : (j + 1) * 128, :] = rank_in_ref[
+            pl.ds(pl.multiple_of(order_ref[j] * 128, 128), 128), :
+        ]
+    for k in range(heads):
+        lanes = pl.ds(pl.multiple_of(order_ref[16 + k] * DK, DK), DK)
+        new_rank_out_ref[:, k * DK : (k + 1) * DK] = rank_out_ref[:, lanes]
+        new_bias_ref[:, k * DK : (k + 1) * DK] = bias_ref[:, lanes]
+    take_columns(cot_ref, order_ref, upstream_ref)
+    take_columns(hidden_ref, order_ref, inputs_ref)
+    for i in range(hidden_ref.shape[0] // CHUNK):
+        rows = pl.ds(i * CHUNK, CHUNK)
+        values = inputs_ref[rows, :].astype(F32)
+        scale = lax.rsqrt(jnp.mean(values * values, axis=1, keepdims=True) + EPSILON)
+        normed_ref[rows, :] = (values * scale * new_one_ref[...]).astype(BF16)
+
+
+def call_whole(kernel, smem_args, args, outs, name):
+    vmem = pl.BlockSpec(memory_space=pltpu.VMEM)
+    return pl.pallas_call(
+        kernel,
+        in_specs=[smem()] * len(smem_args) + [vmem] * len(args),
+        out_specs=[vmem] * len(outs),
+        out_shape=outs,
+        compiler_params=params(),
+        name=name,
+    )(*smem_args, *args)
+
+
+def output_kernel(back_ref, resid_ref, feed_ref, out_ref):
+    for j in range(8):
+        lanes = pl.ds(pl.multiple_of(back_ref[8 + j] * 128, 128), 128)
+        out_ref[:, j * 128 : (j + 1) * 128] = (resid_ref[:, lanes] + feed_ref[:, lanes]).astype(BF16)
+
+
+def finish_kernel(heads, back_ref, d_resid_ref, d_normed_ref, inputs_ref, gain_ref, rank_in_ref, rank_out_ref,
+                  bias_ref, group_ref, ffn_ref, grad_ref, small_ref, scratch):
+    gain = gain_ref[...]
+    total = jnp.zeros((1, gain.shape[1]), F32)
+    for i in range(inputs_ref.shape[0] // CHUNK):
+        rows = pl.ds(i * CHUNK, CHUNK)
+        values = inputs_ref[rows, :].astype(F32)
+        scale = lax.rsqrt(jnp.mean(values * values, axis=1, keepdims=True) + EPSILON)
+        unit = values * scale
+        upstream = d_normed_ref[rows, :]
+        total = total + jnp.sum(upstream * unit, axis=0, keepdims=True)
+        weighted = upstream * gain
+        scratch[0:CHUNK, :] = d_resid_ref[rows, :] + scale * (
+            weighted - unit * jnp.mean(weighted * unit, axis=1, keepdims=True)
+        )
+        for j in range(8):
+            lanes = pl.ds(pl.multiple_of(back_ref[8 + j] * 128, 128), 128)
+            grad_ref[rows, j * 128 : (j + 1) * 128] = scratch[0:CHUNK, lanes]
+    small_ref[...] = jnp.zeros_like(small_ref)
+    scratch[0:16, :] = rank_in_ref[...]
+    scratch[24:25, :] = total
+    scratch[25:26, :] = ffn_ref[...]
+    for j in range(8):
+        lanes = pl.ds(pl.multiple_of(back_ref[8 + j] * 128, 128), 128)
+        small_ref[0:16, j * 128 : (j + 1) * 128] = scratch[0:16, lanes]
+        small_ref[24:26, j * 128 : (j + 1) * 128] = scratch[24:26, lanes]
+    width = heads * DK
+    for k in range(heads):
+        lanes = pl.ds(pl.multiple_of(back_ref[16 + k] * DK, DK), DK)
+        small_ref[16:24, k * DK : (k + 1) * DK] = rank_out_ref[0:8, lanes]
+        small_ref[16:24, width + k * DK : width + (k + 1) * DK] = rank_out_ref[8:16, lanes]
+        small_ref[26:27, k * DK : (k + 1) * DK] = bias_ref[:, lanes]
+    small_ref[26:27, width : width + DV] = group_ref[...]
+
+
 def split_axes():
     return all(lax.axis_size(axis) == 2 for axis in ("dpo", "core", "ctx"))
 
 
-def column_order(back):
+def column_order():
+    heads = lax.axis_size("tp")
+    place = lax.axis_index("tp")
+    order, back = list(range(8)), list(range(8))
+    if split_axes():
+        y, core, x = (lax.axis_index(axis) for axis in ("dpo", "core", "ctx"))
+        for j in range(8):
+            high, middle, last = j >> 2, (j >> 1) & 1, j & 1
+            order[j] = ((y ^ middle) * 2 + (core ^ high)) * 2 + (x ^ last)
+            back[j] = ((core ^ middle) * 2 + (y ^ high)) * 2 + (x ^ last)
+    slots = [lax.rem(place - k + heads, heads) for k in range(heads)]
+    return jnp.stack([jnp.asarray(v, jnp.int32) for v in order + back + slots])
+
+
+def tie(array, *others):
+    others = [other for other in others if other is not None]
+    return lax.optimization_barrier((array, *others))[0] if others else array
+
+
+def weight_axes(first):
+    return ("ctx", "dpo") if first == "ctx" else ("dpo", "ctx")
+
+
+def join_kernel(swap, *refs):
+    out = refs[-1]
+    for i in range(4):
+        for half in range(2):
+            block = 4 * (i // 2) + (2 * half + i % 2 if swap else 2 * (i % 2) + half)
+            out[:, block * 128 : (block + 1) * 128] = refs[2 * i + half][...]
+
+
+def join_columns(pieces, swap):
+    rows = pieces[0].shape[0] // 2
+    tile = 512
+    specs, args = [], []
+    for piece in pieces:
+        for half in range(2):
+            specs.append(pl.BlockSpec((tile, 128), functools.partial(lambda at, i: (at + i, 0), half * (rows // tile))))
+            args.append(piece)
+    return pl.pallas_call(
+        functools.partial(join_kernel, swap),
+        grid=(rows // tile,),
+        in_specs=specs,
+        out_specs=pl.BlockSpec((tile, 1024), lambda i: (i, 0)),
+        out_shape=shaped((rows, 1024), pieces[0].dtype),
+        compiler_params=params(),
+        name="join",
+    )(*args)
+
+
+def ffn_kernel(
+    units,
+    order_ref,
+    every_ref,
+    rows_ref,
+    upstream_ref,
+    feed_ref,
+    d_rows_ref,
+    grads_ref,
+    near_ref,
+    far_ref,
+    weights,
+    lefts,
+):
+    rows, upstream = rows_ref[...], upstream_ref[...]
+    for j in range(8):
+        weights[:, j * 128 : (j + 1) * 128] = every_ref[order_ref[j], 0]
+    both, down = weights[: 2 * units, :], weights[2 * units :, :]
+    gate_pre = nt(weights[:units, :], rows)
+    sigma = jax.nn.sigmoid(gate_pre)
+    silu = gate_pre * sigma
+    slope = sigma * (1.0 + gate_pre * (1.0 - sigma))
+    up_pre = nt(weights[units : 2 * units, :], rows)
+    d_act = nt(down, upstream)
+    lefts[2 * units :, :] = (silu * up_pre).astype(BF16)
+    lefts[:units, :] = (d_act * up_pre * slope).astype(BF16)
+    lefts[units : 2 * units, :] = (d_act * silu).astype(BF16)
+    d_rows = tn(lefts[: 2 * units, :], both)
+    feed = tn(lefts[2 * units :, :], down)
+
+    @pl.when(pl.program_id(0) == 0)
+    def _():
+        d_rows_ref[...] = d_rows
+        feed_ref[...] = feed
+
+    @pl.when(pl.program_id(0) > 0)
+    def _():
+        d_rows_ref[...] += d_rows
+        feed_ref[...] += feed
+
+    for pair in range(4):
+        lanes = slice(pair * 256, (pair + 1) * 256)
+        grads_in = nn(lefts[: 2 * units, :], rows[:, lanes]).astype(BF16)
+        grads_down = nn(lefts[2 * units :, :], upstream[:, lanes]).astype(BF16)
+        down_ref = near_ref if pair < 2 else far_ref
+        for j in range(2):
+            block = order_ref[2 * pair + j]
+            grads_ref[block, 0, : 2 * units, :] = grads_in[:, j * 128 : (j + 1) * 128]
+            down_ref[2 * (pair % 2) + j, 0] = grads_down[:, j * 128 : (j + 1) * 128]
+    padding = grads_ref.shape[2] - 2 * units
+    if padding:
+        grads_ref[:, 0, 2 * units :, :] = jnp.zeros((8, padding, 128), BF16)
+
+
+def feed_forward(order, every, rows, upstream):
+    length, width = rows.shape
+    blocks, slots, total, _ = every.shape
+    units = total // 3
+    padded = -(-2 * units // 48) * 48
+    whole = pl.BlockSpec((length, width), lambda t, order: (0, 0))
+    half = pl.BlockSpec((4, 1, units, 128), lambda t, order: (0, t, 0, 0))
+    return pl.pallas_call(
+        functools.partial(ffn_kernel, units),
+        grid_spec=pltpu.PrefetchScalarGridSpec(
+            num_scalar_prefetch=1,
+            grid=(slots,),
+            in_specs=[
+                pl.BlockSpec((blocks, 1, total, 128), lambda t, order: (0, t, 0, 0)),
+                whole,
+                whole,
+            ],
+            out_specs=[
+                whole,
+                whole,
+                pl.BlockSpec((blocks, 1, padded, 128), lambda t, order: (0, t, 0, 0)),
+                half,
+                half,
+            ],
+            scratch_shapes=[pltpu.VMEM((total, width), BF16), pltpu.VMEM((total, length), BF16)],
+        ),
+        out_shape=[
+            shaped((length, width), F32),
+            shaped((length, width), F32),
+            shaped((blocks, slots, padded, 128), BF16),
+            shaped((4, slots, units, 128), BF16),
+            shaped((4, slots, units, 128), BF16),
+        ],
+        compiler_params=params(),
+        name="feed_forward",
+    )(order, every, rows, upstream)
+
+
+def gather_units(parts):
+    count = lax.axis_size("tp")
+    shard = jnp.concatenate(parts, axis=0)
+    rows = shard.shape[0]
+    if not split_axes():
+        wide = lax.all_gather(shard, ("dpo", "core", "ctx"), axis=1, tiled=True)
+        every = lax.all_gather(wide, "tp").reshape(count, rows, 8, 128)
+        return jnp.transpose(every, (2, 0, 1, 3))
+    every = lax.all_gather(shard, ("dpo", "core", "ctx", "tp"))
+    return every.reshape(8, count, rows, 128)
+
+
+def scatter_units(grads):
+    blocks, count, rows, lanes = grads.shape
+    if not split_axes():
+        whole = jnp.transpose(grads, (1, 2, 0, 3)).reshape(count, rows, blocks * lanes)
+        whole = lax.psum_scatter(whole, "tp", scatter_dimension=0, tiled=True)[0]
+        return lax.psum_scatter(whole, ("dpo", "core", "ctx"), scatter_dimension=1, tiled=True)
+    return lax.psum_scatter(
+        grads.reshape(blocks * count, rows, lanes), ("dpo", "core", "ctx", "tp"), scatter_dimension=0
+    )
+
+
+def gather_slots(shards):
+    count = lax.axis_size("tp")
+    shard = jnp.concatenate(shards, axis=0)
+    slots = [shard] + [shifted(shard, "tp", k) for k in range(1, count)]
+    stacks, at = [], 0
+    for part in shards:
+        stacks.append([slot[at : at + part.shape[0]] for slot in slots])
+        at += part.shape[0]
+    return stacks
+
+
+class Gather:
+    def __init__(self, stacks, first):
+        self.first = weight_axes(first)
+        self.stack = jnp.concatenate(sum(stacks, []), axis=0)
+
+    def hop_one(self, *hold):
+        own = tie(self.stack, *hold)
+        if not split_axes():
+            self.whole = lax.all_gather(own, ("dpo", "core", "ctx"), axis=1, tiled=True)
+            return None
+        self.own = own
+        self.near = swapped(own, self.first[0])
+        return self.near
+
+    def hop_two(self, *hold):
+        if not split_axes():
+            return None
+        self.pair = tie(jnp.concatenate([self.own, self.near], axis=0), *hold)
+        self.far = swapped(self.pair, self.first[1])
+        return self.far
+
+    def hop_core(self, *hold):
+        if not split_axes():
+            return self.whole
+        far = tie(self.far, *hold)
+        pieces = [self.pair, far, swapped(self.pair, "core"), swapped(far, "core")]
+        return join_columns(pieces, self.first[0] == "dpo")
+
+
+class Scatter:
+    def __init__(self, first):
+        self.first = weight_axes(first)
+
+    def core(self, far):
+        self.sent = far
+        if split_axes():
+            self.received = swapped(far, "core")
+        return far
+
+    def one(self, near):
+        if not split_axes():
+            self.kept = jnp.concatenate([near, self.sent.astype(F32)], axis=-1)
+            return None
+        near = near + self.received.astype(F32)
+        quarter = near.shape[-1] // 4
+        blocks = [near[..., i * quarter : (i + 1) * quarter] for i in range(4)]
+        if self.first[0] == "ctx":
+            kept, sent = (blocks[0], blocks[2]), (blocks[1], blocks[3])
+        else:
+            kept, sent = (blocks[0], blocks[1]), (blocks[2], blocks[3])
+        self.kept = jnp.concatenate(kept, axis=-1).astype(BF16)
+        self.sent = jnp.concatenate(sent, axis=-1).astype(BF16)
+        self.received = swapped(self.sent, self.first[0])
+        return self.sent
+
+    def two(self, *hold):
+        if not split_axes():
+            return None
+        kept = tie(self.kept, *hold)
+        quarter = kept.shape[-1] // 2
+        sums = kept.astype(F32) + self.received.astype(F32)
+        self.kept, self.sent = sums[..., :quarter].astype(BF16), sums[..., quarter:].astype(BF16)
+        self.received = swapped(self.sent, self.first[1])
+        return self.sent
+
+    def sums(self, *hold):
+        kept = tie(self.kept, *hold)
+        if not split_axes():
+            return kept
+        return (kept.astype(F32) + self.received.astype(F32)).astype(BF16)
+
+
+class BlockScatter(Scatter):
+    def one(self, near, received):
+        total = near.astype(F32) + received.astype(F32)
+        one, two = ((0, 2), (1, 3)) if self.first[0] == "ctx" else ((0, 1), (2, 3))
+        self.kept = jnp.stack([total[i] for i in one]).astype(BF16)
+        self.sent = jnp.stack([total[i] for i in two]).astype(BF16)
+        self.received = swapped(self.sent, self.first[0])
+        return self.sent
+
+    def two(self, *hold):
+        kept = tie(self.kept, *hold)
+        self.kept, self.sent = (
+            (kept[i].astype(F32) + self.received[i].astype(F32)).astype(BF16) for i in range(2)
+        )
+        self.received = swapped(self.sent, self.first[1])
+        return self.sent
+
+
+def hop_two_together(ones, *hold):
     if not split_axes():
         return None
-    y, core, x = (lax.axis_index(axis) for axis in ("dpo", "core", "ctx"))
-    order = []
-    for j in range(8):
-        high, middle, last = j >> 2, (j >> 1) & 1, j & 1
-        if back:
-            order.append(((core ^ middle) * 2 + (y ^ high)) * 2 + (x ^ last))
-        else:
-            order.append(((y ^ middle) * 2 + (core ^ high)) * 2 + (x ^ last))
-    return order
-
-
-def reorder(array, axis, back=False):
-    order = column_order(back)
-    if order is None:
-        return array
-    size = array.shape[axis] // len(order)
-    return jnp.concatenate(
-        [lax.dynamic_slice_in_dim(array, block * size, size, axis) for block in order], axis=axis
-    )
-
-
-def weight_axes(first):
-    return ("ctx", "dpo") if first == "ctx" else ("dpo", "ctx")
-
-
-def gather_weights(shards, first):
+    kept, sent = [], []
+    for one in ones:
+        quarter = one.kept.shape[-1] // 2
+        sums = tie(one.kept, *hold).astype(F32) + one.received.astype(F32)
+        kept.append(sums[..., :quarter].astype(BF16))
+        sent.append(sums[..., quarter:].astype(BF16))
+    received = swapped(jnp.concatenate(sent, axis=0), ones[0].first[1])
+    at = 0
+    for i, one in enumerate(ones):
+        rows = kept[i].shape[0]
+        one.kept, one.received = kept[i], received[at : at + rows]
+        at += rows
+    return received
+
+
+def send_slots(slots):
     count = lax.axis_size("tp")
+    return [slots[0]] + [shifted(slots[k], "tp", -k) for k in range(1, count)]
+
+
+def add_slots(parts):
+    total = parts[0].astype(F32)
+    for part in parts[1:]:
+        total = total + part.astype(F32)
     if not split_axes():
-        place = lax.axis_index("tp")
-        out = []
-        for shard in shards:
-            wide = lax.all_gather(shard, ("dpo", "core", "ctx"), axis=1, tiled=True)
-            every = lax.all_gather(wide, "tp")
-            every = jnp.take(every, lax.rem(place - jnp.arange(count) + count, count), axis=0)
-            out.append(every.reshape(-1, every.shape[-1]))
-        return jnp.concatenate(out, axis=0)
-    one, two = weight_axes(first)
-    shard = jnp.concatenate(shards, axis=0)
-    slots = [shard] + [shifted(shard, "tp", k) for k in range(1, count)]
-    rows, at = [], 0
-    for part in shards:
-        rows += [slot[at : at + part.shape[0]] for slot in slots]
-        at += part.shape[0]
-    pieces = {(0, 0): jnp.concatenate(rows, axis=0)}
-    pieces[1, 0] = swapped(pieces[0, 0], one)
-    pieces[0, 1] = swapped(pieces[0, 0], two)
-    pieces[1, 1] = swapped(pieces[1, 0], two)
-    own = [pieces[(y, x) if one == "dpo" else (x, y)] for y in (0, 1) for x in (0, 1)]
-    return jnp.concatenate(own + [swapped(piece, "core") for piece in own], axis=1)
-
-
-def scatter_grads(left, right, sizes, first):
-    count = lax.axis_size("tp")
-    if not split_axes():
-        place = lax.axis_index("tp")
-        whole = tn(left, right)
-        out, at = [], 0
-        for size in sizes:
-            part = whole[at : at + count * size].reshape(count, size, -1)
-            part = jnp.take(part, lax.rem(place - jnp.arange(count) + count, count), axis=0)
-            part = lax.psum_scatter(part, "tp", scatter_dimension=0, tiled=True)[0]
-            out.append(lax.psum_scatter(part, ("dpo", "core", "ctx"), scatter_dimension=1, tiled=True))
-            at += count * size
-        return out
-    half = right.shape[1] // 2
-    quarter = half // 4
-    far = swapped(tn(left, right[:, half:]).astype(BF16), "core")
-    near = tn(left, right[:, :half]) + far.astype(F32)
-    blocks = {(i >> 1, i & 1): near[:, i * quarter : (i + 1) * quarter] for i in range(4)}
-    if first == "ctx":
-        blocks = {(x, y): block for (y, x), block in blocks.items()}
-    one, two = weight_axes(first)
-    sent = jnp.concatenate([blocks[1, 0], blocks[1, 1]], axis=1).astype(BF16)
-    kept = jnp.concatenate([blocks[0, 0], blocks[0, 1]], axis=1).astype(BF16)
-    sums = kept.astype(F32) + swapped(sent, one).astype(F32)
-    sent, kept = sums[:, quarter:].astype(BF16), sums[:, :quarter].astype(BF16)
-    sums = (kept.astype(F32) + swapped(sent, two).astype(F32)).astype(BF16)
-    slots, at = [[] for _ in range(count)], 0
-    for size in sizes:
-        for k in range(count):
-            slots[k].append(sums[at + k * size : at + (k + 1) * size])
-        at += count * size
-    slots = [jnp.concatenate(slot, axis=0) if len(slot) > 1 else slot[0] for slot in slots]
-    total = slots[0].astype(F32)
-    for k in range(1, count):
-        total = total + shifted(slots[k], "tp", -k).astype(F32)
-    out, at = [], 0
-    for size in sizes:
-        out.append(total[at : at + size])
-        at += size
-    return out
-
-
-def sum_everywhere(values):
-    if not split_axes() or lax.axis_size("tp") != 4:
-        return lax.psum(values, ("dpo", "core", "ctx", "tp"))
+        total = lax.psum_scatter(
+            total, ("dpo", "core", "ctx"), scatter_dimension=total.ndim - 1, tiled=True
+        )
+    return total
+
+
+def ordered_sum_kernel(count, order_ref, *refs):
+    scratch, out_ref = refs[-1], refs[-2]
+    for k in range(count):
+        scratch[k] = refs[k][...].astype(F32)
+    total = scratch[order_ref[16]]
+    for z in range(1, count):
+        total = total + scratch[order_ref[16 + z]]
+    out_ref[...] = total
+
+
+def sum_here(values):
     for axis in ("core", "ctx", "dpo"):
         values = values + swapped(values, axis)
-    for pairs in ([(0, 1), (1, 0), (2, 3), (3, 2)], [(0, 2), (2, 0), (1, 3), (3, 1)]):
-        values = values + lax.ppermute(values, "tp", pairs)
     return values
+
+
+def sum_slots(parts, order):
+    vmem = pl.BlockSpec(memory_space=pltpu.VMEM)
+    shape = parts[0].shape
+    return pl.pallas_call(
+        functools.partial(ordered_sum_kernel, len(parts)),
+        in_specs=[smem()] + [vmem] * len(parts),
+        out_specs=vmem,
+        out_shape=shaped(shape, F32),
+        scratch_shapes=[pltpu.VMEM((len(parts), *shape), F32)],
+        compiler_params=params(),
+        name="ordered_sum",
+    )(order, *parts)
 
 
 def rms_scale(values):
@@ -626,40 +951,52 @@
     w_up,
     w_down,
 ):
-    seq_count, length, model_width = hidden_in.shape
-    assert seq_count == 1
+    seq_count, length, width = hidden_in.shape
+    assert seq_count == 1 and width == 1024 and length % CHUNK == 0
     heads = lax.axis_size("tp")
     place = lax.axis_index("tp")
     chunks = length // CHUNK
     units = w_down.shape[0]
-    half = units // 2
-
-    cut = lambda array, index: array[index * half : (index + 1) * half]
-    w_gate_t, w_up_t = w_gate.T, w_up.T
-    w_in = jnp.concatenate([w_query.T, w_key.T, w_value.T], axis=0)
-    w_in_all = gather_weights([w_in], "dpo")
-    w_side_all = gather_weights([w_outgate.T, w_output], "ctx")
-    w_og_all, w_out_all = w_side_all[: heads * DV], w_side_all[heads * DV :]
-    ffn_all = [
-        gather_weights([cut(w_gate_t, s), cut(w_up_t, s), cut(w_down, s)], ("dpo", "ctx")[s])
-        for s in range(2)
+
+    stacks = gather_slots(
+        [jnp.concatenate([w_query.T, w_key.T], axis=0), w_outgate.T, w_value.T, w_output]
+    )
+    takes = [Gather(stacks[:2], "dpo"), Gather(stacks[2:], "ctx")]
+    order = column_order()
+    ffn_all = gather_units([w_gate.T, w_up.T, w_down])
+    first_hops = [take.hop_one() for take in takes]
+    for take in takes:
+        take.hop_two(*first_hops)
+    w_one, w_two = (take.hop_core() for take in takes)
+    w_qk, w_og_all = w_one[: heads * 2 * DK], w_one[heads * 2 * DK :]
+    w_val, w_out_all = w_two[: heads * DV], w_two[heads * DV :]
+
+    kinds = [
+        shaped((length, width), BF16),
+        shaped((length, width), BF16),
+        shaped((length, width), BF16),
+        shaped((1, width), F32),
+        shaped((1, width), F32),
+        shaped((width, RANK), BF16),
+        shaped((RANK, heads * DK), BF16),
+        shaped((1, heads * DK), F32),
     ]
-    wide = heads * half
-
-    head_order = lax.rem(place - jnp.arange(heads) + heads, heads)
-    rank_out = jnp.take(w_rank_out.reshape(RANK, heads, DK), head_order, axis=1).reshape(
-        RANK, heads * DK
-    )
-    bias = jnp.take(gate_bias.reshape(heads, DK), head_order, axis=0).reshape(heads * DK)
-    rank_in = reorder(w_rank_in, 0)
-    gain_one = reorder(norm_mixer, 0).astype(F32)
-    gain_two = reorder(norm_ffn, 0).astype(F32)
-
-    inputs_low = reorder(hidden_in[0], 1)
-    upstream = reorder(cotangent[0], 1)
+    inputs_low, upstream, normed, gain_one, gain_two, rank_in, rank_out, bias = call_whole(
+        functools.partial(begin_kernel, heads),
+        [order],
+        [
+            hidden_in[0],
+            cotangent[0],
+            norm_mixer.astype(F32)[None],
+            norm_ffn.astype(F32)[None],
+            w_rank_in,
+            w_rank_out,
+            gate_bias.astype(F32)[None],
+        ],
+        kinds,
+        "begin",
+    )
     inputs = inputs_low.astype(F32)
-    scale_one = rms_scale(inputs)
-    normed = (inputs * scale_one * gain_one).astype(BF16)
 
     part = lax.axis_index("ctx") * heads + place
     starts = part * length + jnp.arange(chunks, dtype=jnp.int32) * CHUNK
@@ -670,96 +1007,142 @@
     first_half = (starts % PIECE) == 0
     flags = jnp.stack([in_piece, in_piece & first_half]).astype(jnp.int32)
 
-    qkv = nt(normed, w_in_all).astype(BF16)
     rank_low = nn(normed, rank_in).astype(BF16)
-    gate_in = nn(rank_low, rank_out) + bias.astype(F32)
-    sums, local, future, ends = chunk_states(qkv, gate_in, heads)
+    gate_in = nn(rank_low, rank_out) + bias
+    qk = nt(normed, w_qk).astype(BF16)
+    values = nt(normed, w_val).astype(BF16)
+    sums, local, future, ends = chunk_states(qk, values, gate_in, heads)
     later = neighbour_future(future[:, 0], True)
     incoming = exchange_states(ends, False)
     outgate = nt(normed, w_og_all)
     gain_group = group_gain.astype(F32)[None, :]
-    mixed, gated = mix(flags, qkv, sums, local, incoming, future, later, outgate, gain_group)
+    mixed, gated = mix(flags, qk, values, sums, local, incoming, future, later, outgate, gain_group)
     resid = inputs + nn(gated, w_out_all)
     scale_two = rms_scale(resid)
     normed_two = (resid * scale_two * gain_two).astype(BF16)
 
-    feed = jnp.zeros_like(resid)
-    d_norm_two = jnp.zeros_like(resid)
-    grads = []
-    for s in range(2):
-        weights = ffn_all[s]
-        gate_w, up_w, down_w = weights[:wide], weights[wide : 2 * wide], weights[2 * wide :]
-        gate_pre, up_pre = nt(normed_two, gate_w), nt(normed_two, up_w)
-        sigma = jax.nn.sigmoid(gate_pre)
-        silu = gate_pre * sigma
-        activation = (silu * up_pre).astype(BF16)
-        feed = feed + nn(activation, down_w)
-        d_act = nt(upstream, down_w)
-        d_gate = (d_act * up_pre * (sigma * (1.0 + gate_pre * (1.0 - sigma)))).astype(BF16)
-        d_up = (d_act * silu).astype(BF16)
-        d_norm_two = d_norm_two + nn(d_gate, gate_w) + nn(d_up, up_w)
-        order = ("ctx", "dpo")[s]
-        grad_down = scatter_grads(activation, upstream, [half], order)[0]
-        grad_gate = scatter_grads(d_gate, normed_two, [half], order)[0]
-        grad_up = scatter_grads(d_up, normed_two, [half], order)[0]
-        grads.append((grad_gate, grad_up, grad_down))
-    hidden_out = reorder((resid + feed).astype(BF16), 1, True)[None]
-    grad_gate, grad_up, grad_down = (jnp.concatenate(pair, axis=0) for pair in zip(*grads))
-
-    grad_ffn_term = jnp.sum(d_norm_two * resid * scale_two, axis=0)
+    side = width // 2
+    feed, d_norm_two, grads_ffn, near_down, far_down = feed_forward(
+        order, ffn_all, normed_two, upstream
+    )
+    grads_ffn = scatter_units(grads_ffn)
+    fast = split_axes()
+    pairs = heads // 2
+    give_down = [BlockScatter("ctx"), BlockScatter("dpo")]
+    received_down = swapped(far_down, "core") if fast else None
+
+    def step_down(step, *args):
+        return [getattr(one, step)(*args) for one in give_down] if fast else []
+
+    grad_ffn_term = jnp.sum(d_norm_two * resid * scale_two, axis=0, keepdims=True)
     d_resid = upstream.astype(F32) + norm_back(d_norm_two, resid, scale_two, gain_two)
     d_branch = d_resid.astype(BF16)
+    give_out, give_gate = Scatter("ctx"), Scatter("dpo")
     d_gated = nt(d_branch, w_out_all)
+    if fast:
+        sent_down = [
+            give_down[i].one(
+                near_down[:, i * pairs : (i + 1) * pairs], received_down[:, i * pairs : (i + 1) * pairs]
+            )
+            for i in range(2)
+        ]
+        d_gated = tie(d_gated, *sent_down)
     d_outgate, d_mixed, gain_terms, back_local, back_ends, earlier = gate_back(
-        flags, d_gated, outgate, mixed, gain_group, qkv, sums, heads
-    )
-    grad_group_term = jnp.sum(gain_terms, axis=(0, 1))
+        flags, d_gated, outgate, mixed, gain_group, qk, sums, heads
+    )
+    grad_group_term = jnp.sum(gain_terms, axis=0)
     earlier = neighbour_future(earlier, False)
     back_incoming = exchange_states(back_ends, True)
-    grad_output = scatter_grads(gated, d_branch, [DV], "ctx")[0]
-    grad_outgate = scatter_grads(d_outgate, normed, [DV], "dpo")[0]
-    d_qkv, d_gate_in = mix_back(
-        flags, d_mixed, qkv, sums, local, incoming, future, later, back_local, back_incoming, earlier, gate_in
-    )
-    grad_in_heads = scatter_grads(d_qkv, normed, [2 * DK + DV], "ctx")[0]
-    grad_bias_here = jnp.sum(d_gate_in.astype(F32), axis=0)
+    give_out.core(tn(gated, d_branch[:, side:]).astype(BF16))
+    give_gate.core(tn(d_outgate, normed[:, side:]).astype(BF16))
+    near_out = give_out.one(tn(gated, d_branch[:, :side]))
+    near_gate = give_gate.one(tn(d_outgate, normed[:, :side]))
+    d_mixed = tie(d_mixed, near_out, near_gate)
+    d_qk, d_val, d_gate_in = mix_back(
+        flags, d_mixed, qk, values, sums, local, incoming, future, later, back_local, back_incoming, earlier, gate_in
+    )
+    give_qk, give_val = Scatter("dpo"), Scatter("ctx")
+    far_in = [
+        give_qk.core(tn(d_qk, normed[:, side:]).astype(BF16)),
+        give_val.core(tn(d_val, normed[:, side:]).astype(BF16)),
+    ]
+    second_down = step_down("two", *far_in)
+    grad_bias_here = jnp.sum(d_gate_in.astype(F32), axis=0, keepdims=True)
     grad_rank_here = tn(rank_low, d_gate_in)
     d_rank_low = nt(d_gate_in, rank_out).astype(BF16)
-    d_normed = nn(d_qkv, w_in_all) + nn(d_outgate, w_og_all) + nt(d_rank_low, rank_in)
-    grad_rank_in_term = tn(normed, d_rank_low)
-    grad_mixer_term = jnp.sum(d_normed * inputs * scale_one, axis=0)
-    grad_in = reorder(d_resid + norm_back(d_normed, inputs, scale_one, gain_one), 1, True)[None]
-
-    rank_out_here = jnp.take(grad_rank_here.reshape(RANK, heads, DK), head_order, axis=1)
-    bias_here = jnp.take(grad_bias_here.reshape(heads, DK), head_order, axis=0)
-    small = (
-        reorder(grad_mixer_term, 0, True),
-        reorder(grad_rank_in_term, 0, True),
-        rank_out_here,
-        bias_here,
+    d_low = tie(d_qk, *far_in, *second_down)
+    d_normed = nn(d_low, w_qk) + nn(d_val, w_val) + nn(d_outgate, w_og_all) + nt(d_rank_low, rank_in)
+    d_tied = tie((d_qk, d_val), d_normed)
+    near_in = [give_qk.one(tn(d_tied[0], normed[:, :side])), give_val.one(tn(d_tied[1], normed[:, :side]))]
+    d_normed = tie(d_normed, *near_in)
+    grad_rank_in_term = tn(d_rank_low, normed)
+    grad_in, small = pl.pallas_call(
+        functools.partial(finish_kernel, heads),
+        in_specs=[smem()] + [pl.BlockSpec(memory_space=pltpu.VMEM)] * 9,
+        out_specs=[pl.BlockSpec(memory_space=pltpu.VMEM)] * 2,
+        out_shape=[shaped((length, width), F32), shaped((32, width), F32)],
+        scratch_shapes=[pltpu.VMEM((CHUNK, width), F32)],
+        compiler_params=params(),
+        name="finish",
+    )(
+        order,
+        d_resid,
+        d_normed,
+        inputs_low,
+        gain_one,
+        grad_rank_in_term,
+        grad_rank_here,
+        grad_bias_here,
         grad_group_term,
-        reorder(grad_ffn_term, 0, True),
-    )
-    flat = sum_everywhere(jnp.concatenate([term.reshape(-1, DK) for term in small], axis=0))
-    shared, at = [], 0
-    for term in small:
-        rows = term.size // DK
-        shared.append(flat[at : at + rows])
-        at += rows
+        grad_ffn_term,
+    )
+    sums_down = step_down("sums", *near_in)
+    if fast:
+        slots_down = jnp.concatenate(sums_down, axis=0)
+        parts_down = lax.all_to_all(slots_down, "tp", 0, 0, tiled=True)
+        grad_down = add_slots([parts_down[k] for k in range(heads)])
+    else:
+        slots_down = jnp.concatenate([near_down, far_down], axis=0)
+        slots_down = jnp.transpose(slots_down, (1, 2, 0, 3)).reshape(heads, units, width)
+        grad_down = lax.psum_scatter(slots_down.astype(F32), "tp", scatter_dimension=0, tiled=True)
+        grad_down = add_slots([grad_down[0]])
+    hop_two_together([give_out, give_val])
+    hop_two_together([give_gate, give_qk])
+    slots_in = [
+        one.sums().reshape(heads, DV, -1) for one in (give_out, give_gate, give_qk, give_val)
+    ]
+    slots_in = [[part[k] for part in slots_in] for k in range(heads)]
+    if fast:
+        small = sum_here(small).astype(BF16)
+        parts_in = send_slots(
+            [jnp.concatenate(slot + [small.reshape(-1, DK)], axis=0) for slot in slots_in]
+        )
+        rows = parts_in[0].shape[0] - small.size // DK
+        small = sum_slots([part[rows:].reshape(small.shape) for part in parts_in], order)
+        mixer_grads = add_slots([part[:rows] for part in parts_in])
+    else:
+        small = lax.psum(small, ("dpo", "core", "ctx", "tp"))
+        mixer_grads = add_slots(send_slots([jnp.concatenate(slot, axis=0) for slot in slots_in]))
+    hidden_out = call_whole(
+        output_kernel, [order], [resid, feed], [shaped((length, width), BF16)], "output"
+    )[0][None]
+    grad_output, grad_outgate, grad_heads = mixer_grads[:DV], mixer_grads[DV : 2 * DV], mixer_grads[2 * DV :]
+    grads_ffn = grads_ffn.astype(F32)
+    grad_gate, grad_up = grads_ffn[:units], grads_ffn[units : 2 * units]
     return (
         hidden_out,
-        grad_in,
-        shared[0].reshape(norm_mixer.shape),
-        grad_in_heads[:DK].T,
-        grad_in_heads[DK : 2 * DK].T,
-        grad_in_heads[2 * DK :].T,
+        grad_in[None],
+        small[24],
+        grad_heads[:DK].T,
+        grad_heads[DK : 2 * DK].T,
+        grad_heads[2 * DK :].T,
         grad_outgate.T,
-        shared[1].reshape(w_rank_in.shape),
-        shared[2].reshape(w_rank_out.shape),
-        shared[3].reshape(gate_bias.shape),
-        shared[4].reshape(group_gain.shape),
+        small[:RANK].T,
+        jnp.concatenate([small[16:24, : heads * DK], small[16:24, heads * DK :]], axis=0),
+        small[26, : heads * DK],
+        small[26, heads * DK : heads * DK + DV],
         grad_output,
-        shared[5].reshape(norm_ffn.shape),
+        small[25],
         grad_gate.T,
         grad_up.T,
         grad_down,

time: 711 us -> 477 us (0.67)
  the two profiles are of different devices: /device:TPU:12 before, /device:TPU:24 now
where the time goes in v2:
time: 477 us; the launch traced here: 468 us
  waiting for transfers between devices  140 us (29%)
  Pallas kernels  136 us (29%)
  starting transfers between devices  56.9 us (12%)
  matrix products  44.8 us (9%)
  other arithmetic  43.4 us (9%)
  local copies, waits for them, and re-layouts  31.7 us (7%)
  between operations  15.5 us (3%)
    ppermute x18, waiting for transfers between devices, shifted(): lax.ppermute(array, axis, [(i, (i + by) % size) for i in range(size)])  80.4 us
    pallas_call x1, Pallas kernels, feed_forward(): pl.pallas_call(functools.partial(ffn_kernel, units), grid_spec=pltpu.Pref...  62.6 us
    ppermute x28, waiting for transfers between devices, swapped(): return lax.ppermute(array, axis, [(0, 1), (1, 0)])  50.4 us
    ppermute x18, starting transfers between devices, shifted(): lax.ppermute(array, axis, [(i, (i + by) % size) for i in range(size)])  25.8 us
    ppermute x28, starting transfers between devices, swapped(): return lax.ppermute(array, axis, [(0, 1), (1, 0)])  22.8 us
    dot_general x6, matrix products, nt(): lax.dot_general(left, right, (((1,), (1,)), ((), ())), preferred_element_...  15.6 us
    dot_general x10, matrix products, tn(): lax.dot_general(left, right, (((0,), (0,)), ((), ())), preferred_element_...  15.2 us
    pallas_call x1, Pallas kernels, mix_back(): pl.pallas_call(functools.partial(mix_back_kernel, chunks), grid=(heads,),...  14.4 us
  transfers between devices with their start and end apart: 51, of which 17 were waited for; matrix products, arithmetic and copies ran while one was open for 24% of the time, Pallas kernels for 16%

profile of v2, /device:TPU:24, one launch (start us, length us, event | category | flops | bytes accessed | tf_op | source)
XLA Modules:
  0.0 468.1 jit_solution(17544473651774593641)
XLA Ops:
  7.2 1.9 pad_maximum_fusion.3
  13.1 1.9 collective-permute-start.1
  15.5 6.1 %collective-permute-done = bf16[1024,128]{1,0:T(8,128)(2,1)S(1)} collective-permute-done((bf16[1024,128]{1,0:T(8,128)(2,1)S(1)}, bf16[1024,128]{1,0:T(8,128)(2,1)S(1)}, u32[]{:S(2)}, u32[]{:S(2)}) %collective-permute-start) | collective-permute-done | bytes 262176 | tf_op jit(solution)/shard_map/ppermute | solution.py:465
  21.6 27.9 %collective-permute-done.1 = bf16[1024,128]{1,0:T(8,128)(2,1)S(1)} collective-permute-done((bf16[1024,128]{1,0:T(8,128)(2,1)S(1)}, bf16[1024,128]{1,0:T(8,128)(2,1)S(1)}, u32[]{:S(2)}, u32[]{:S(2)}) %collective-permute-start.1) | collective-permute-done | bytes 262176 | tf_op jit(solution)/shard_map/ppermute | solution.py:465
  49.8 1.6 collective-permute-start.4
  51.4 1.5 collective-permute-start.3
  53.0 17.4 %collective-permute-done.4 = bf16[2048,128]{1,0:T(8,128)(2,1)S(1)} collective-permute-done((bf16[2048,128]{1,0:T(8,128)(2,1)S(1)}, bf16[2048,128]{1,0:T(8,128)(2,1)S(1)}, u32[]{:S(2)}, u32[]{:S(2)}) %collective-permute-start.4) | collective-permute-done | bytes 524320 | tf_op jit(solution)/shard_map/ppermute | solution.py:469
  70.4 2.3 collective-permute-done.3
  73.1 1.6 collective-permute-start.8
  78.6 4.8 %begin.1 = (bf16[640,1024]{1,0:T(8,128)(2,1)}, bf16[640,1024]{1,0:T(8,128)(2,1)}, bf16[640,1024]{1,0:T(8,128)(2,1)}, f32[1,1024]{1,0:T(1,128)}, f32[1,1024]{1,0:...) custom-call(s32[20]{0:T(128)} %stack.162.order_ref.back_ref, ...), custom_call_target="tpu_custom_call" | custom-call | tf_op jit(solution)/shard_map/begin/pallas_call | solution.py:539
  84.0 15.3 %collective-permute-done.5.refs_2_.refs_3_ = bf16[4096,128]{1,0:T(8,128)(2,1)} collective-permute-done((bf16[4096,128]{1,0:T(8,128)(2,1)S(1)}, bf16[4096,128]{1,0:T(8,128)(2,1)}, u32[]{:S(2)}, u32[]{:S(2)}) %collective-permute-start.5) | collective-permute-done | bytes 1048608 | tf_op jit(solution)/shard_map/ppermute | solution.py:469
  101.2 1.8 convolution_convert_fusion.4
  103.0 2.2 convolution_add_fusion.gate_ref
  106.2 5.3 %join.2 = bf16[2048,1024]{1,0:T(8,128)(2,1)} custom-call(bf16[4096,128]{1,0:T(8,128)(2,1)} %copy-done.8, bf16[4096,128]{1,0:T(8,128)(2,1)} %copy-done.8, bf16[4096,128]{1,0:T(8,128)(2,1)} %collective-permute-done.5.refs_2_.refs_3_, bf16[4096,128]{1,0:T(8,128)(2,1)} %collective-permute-done.5.refs_2_.refs_3_, bf16[4096,128]{1,0:T(8,128)(2,1)} %copy-done.13, ...), custom_call_target="tpu_custom_call" | custom-call | tf_op jit(solution)/shard_map/join/pallas_call | solution.py:633
  111.5 5.4 %join.3 = bf16[2048,1024]{1,0:T(8,128)(2,1)} custom-call(bf16[4096,128]{1,0:T(8,128)(2,1)} %copy-done.7, bf16[4096,128]{1,0:T(8,128)(2,1)} %copy-done.7, bf16[4096,128]{1,0:T(8,128)(2,1)} %copy-done.12, bf16[4096,128]{1,0:T(8,128)(2,1)} %copy-done.12, bf16[4096,128]{1,0:T(8,128)(2,1)} %collective-permute-done.9.refs_4_.refs_5_, ...), custom_call_target="tpu_custom_call" | custom-call | tf_op jit(solution)/shard_map/join/pallas_call | solution.py:633
  116.9 4.4 fusion.18.qk_ref
  121.4 2.6 fusion.21.value_ref
  124.0 6.6 %chunk_states.1 = (f32[640,512]{1,0:T(8,128)}, f32[4,5,256,128]{3,2,1,0:T(8,128)}, bf16[4,5,256,128]{3,2,1,0:T(8,128)(2,1)}, bf16[4,272,128]{2,1,0:T(8,128)(2,1)}) custom-call(bf16[640,1024]{1,0:T(8,128)(2,1)} %fusion.18.qk_ref, bf16[640,1024]{1,0:T(8,128)(2,1)} %fusion.21.value_ref, f32[640,512]{1,0:T(8,128)} %convolution_add_fusion.gate_ref), custom_call_target="tpu_custom_call" | custom-call | tf_op jit(solution)/shard_map/chunk_states/pallas_call | solution.py:313
  130.6 1.6 slice_bitcast_fusion.9
  132.2 3.8 collective-permute-start.12
  136.0 2.0 collective-permute-start.11
  138.6 12.9 %collective-permute-done.12.refs_2_ = bf16[272,128]{1,0:T(8,128)(2,1)S(1)} collective-permute-done((bf16[272,128]{1,0:T(8,128)(2,1)S(1)}, bf16[272,128]{1,0:T(8,128)(2,1)S(1)}, u32[]{:S(2)}, u32[]{:S(2)}) %collective-permute-start.12) | collective-permute-done | bytes 69664 | tf_op jit(solution)/shard_map/ppermute | solution.py:465
  152.2 1.8 chain.4
  154.0 1.4 collective-permute-start.14
  159.1 1.8 chain.5
  161.7 2.2 collective-permute-start.17
  163.9 4.6 fusion.6.outgate_ref
  170.5 8.1 %mix.1 = (f32[640,1024]{1,0:T(8,128)}, bf16[640,1024]{1,0:T(8,128)(2,1)}) custom-call(s32[2,5]{1,0:T(2,128)} %add_convert_fusion.21.flags_ref, bf16[640,1024]{1,0:T(8,128)(2,1)} %fusion.18.qk_ref, bf16[640,1024]{1,0:T(8,128)(2,1)} %fusion.21.value_ref, f32[640,512]{1,0:T(8,128)} %get-tuple-element.75.sums_ref, ...), custom_call_target="tpu_custom_call" | custom-call | tf_op jit(solution)/shard_map/mix/pallas_call | solution.py:337
  178.6 4.0 multiply_reduce_fusion.2
  182.7 1.6 multiply_convert_fusion.rows_ref
  184.2 62.6 %feed_forward.1 = (f32[640,1024]{1,0:T(8,128)}, f32[640,1024]{1,0:T(8,128)}, bf16[8,4,1440,128]{3,2,1,0:T(8,128)(2,1)}, bf16[4,4,704,128]{3,2,1,0:T(8,128)(2,1)}, bf16[4,4,704,128]{3,2,1,0:T(8,128)(2,1)}) custom-call(s32[20]{0:T(128)} %stack.162.order_ref.back_ref, bf16[8,4,2112,128]{3,2,1,0:T(8,128)(2,1)} %bitcast.147, ...), custom_call_target="tpu_custom_call" | custom-call | tf_op jit(solution)/shard_map/feed_forward/pallas_call | solution.py:705
  247.0 3.1 multiply_reduce_fusion
  250.1 2.2 fusion.51
  254.0 3.1 fusion.d_gated_ref
  259.1 1.4 collective-permute-start.37
  264.2 8.8 %gate_back.1 = (bf16[640,1024]{1,0:T(8,128)(2,1)}, bf16[640,1024]{1,0:T(8,128)(2,1)}, f32[4,1,256]{2,1,0:T(1,128)}, f32[4,5,256,128]{3,2,1,0:T(8,128)}, bf16[4,2...) custom-call(s32[2,5]{1,0:T(2,128)} %add_convert_fusion.21.flags_ref, f32[640,1024]{1,0:T(8,128)} %fusion.d_gated_ref, ...), custom_call_target="tpu_custom_call" | custom-call | tf_op jit(solution)/shard_map/gate_back/pallas_call | solution.py:362
  273.0 3.4 convolution_convert_fusion.2
  277.1 2.2 collective-permute-start.24
  280.1 1.4 collective-permute-start.22
  283.3 3.8 collective-permute-done.23.refs_2_
  287.7 1.8 chain.6
  294.7 1.8 chain.7
  296.5 1.5 collective-permute-start.26
  298.5 2.0 collective-permute-start.28
  302.9 6.2 %collective-permute-done.27 = bf16[256,128]{1,0:T(8,128)(2,1)S(1)} collective-permute-done((bf16[256,128]{1,0:T(8,128)(2,1)}, bf16[256,128]{1,0:T(8,128)(2,1)S(1)}, u32[]{:S(2)}, u32[]{:S(2)}) %collective-permute-start.27) | collective-permute-done | bytes 65568 | tf_op jit(solution)/shard_map/ppermute | solution.py:465
  310.0 1.6 pad_maximum_fusion.10.back_incoming_ref
  314.1 2.3 add_convert_fusion.4
  318.7 14.4 %mix_back.1 = (bf16[640,1024]{1,0:T(8,128)(2,1)}, bf16[640,1024]{1,0:T(8,128)(2,1)}, bf16[640,512]{1,0:T(8,128)(2,1)}) custom-call(s32[2,5]{1,0:T(2,128)} %add_convert_fusion.21.flags_ref, bf16[640,1024]{1,0:T(8,128)(2,1)} %get-tuple-element.95.d_mixed_ref, bf16[640,1024]{1,0:T(8,128)(2,1)} %fusion.18.qk_ref, bf16[640,1024]{1,0:T(8,128)(2,1)} %fusion.21.value_ref, ...), custom_call_target="tpu_custom_call" | custom-call | tf_op jit(solution)/shard_map/mix_back/pallas_call | solution.py:400
  333.1 2.5 convolution_convert_fusion.1
  336.8 2.1 fusion.48
  339.7 2.0 fusion.49
  345.5 1.5 fusion.8
  348.1 1.5 fusion.12
  349.7 3.1 add_add_fusion.d_normed_ref
  362.5 6.2 %finish.1 = (f32[640,1024]{1,0:T(8,128)}, f32[32,1024]{1,0:T(8,128)}) custom-call(s32[20]{0:T(128)} %stack.162.order_ref.back_ref, f32[640,1024]{1,0:T(8,128)} %get-tuple-element.155.d_resid_ref, f32[640,1024]{1,0:T(8,128)} %add_add_fusion.d_normed_ref, bf16[640,1024]{1,0:T(8,128)(2,1)} %get-tuple-element.68.inputs_ref, ...), custom_call_target="tpu_custom_call" | custom-call | tf_op jit(solution)/shard_map/finish/pallas_call | solution.py:1079
  373.2 10.0 %collective-permute-done.35 = f32[32,1024]{1,0:T(8,128)S(1)} collective-permute-done((f32[32,1024]{1,0:T(8,128)S(1)}, f32[32,1024]{1,0:T(8,128)S(1)}, u32[]{:S(2)}, u32[]{:S(2)}) %collective-permute-start.35) | collective-permute-done | bytes 131104 | tf_op jit(solution)/shard_map/ppermute | solution.py:469
  391.9 5.6 %all-to-all-start = ((bf16[4,704,128]{2,1,0:T(8,128)(2,1)}), bf16[4,704,128]{2,1,0:T(8,128)(2,1)S(1)}, u32[]{:S(2)}, u32[]{:S(2)}) async-start(bf16[4,704,128]{2,1,0:T(8,128)(2,1)} %pad_maximum_fusion.2), calls=%async_computation.1 | async-start | bytes 1441792 | tf_op jit(solution)/shard_map/all_to_all | solution.py:1102
  400.0 3.7 collective-permute-done.39
  404.1 4.3 collective-permute-start.44
  408.4 1.9 collective-permute-start.43
  410.3 4.4 output.1
  414.7 9.4 %all-to-all-done = bf16[4,704,128]{2,1,0:T(8,128)(2,1)S(1)} async-done(((bf16[4,704,128]{2,1,0:T(8,128)(2,1)}), bf16[4,704,128]{2,1,0:T(8,128)(2,1)S(1)}, u32[]{:S(2)}, u32[]{:S(2)}) %all-to-all-start) | async-done | bytes 720928 | tf_op jit(solution)/shard_map/all_to_all | solution.py:1102
  426.2 22.6 %collective-permute-done.44 = bf16[1280,128]{0,1:T(8,128)(2,1)S(1)} collective-permute-done((bf16[1280,128]{0,1:T(8,128)(2,1)S(1)}, bf16[1280,128]{0,1:T(8,128)(2,1)S(1)}, u32[]{:S(2)}, u32[]{:S(2)}) %collective-permute-start.44) | collective-permute-done | bytes 327712 | tf_op jit(solution)/shard_map/ppermute | solution.py:465
  450.4 1.7 ordered_sum.1
  (305 shorter events, 90.0 us)
Async XLA Ops:
  7.2 177.1 %all-gather.3.cloned.1.call-start = ((), (), s32[]{:S(2)}) async-start(), calls=%async_computation.3 | async-start | bytes 17842176 | tf_op jit(solution)/shard_map/all_gather | solution.py:744
  9.2 449.6 %reduce-scatter.2.cloned.1.call-start = ((), (), s32[]{:S(2)}) async-start(), calls=%async_computation.2 | async-start | bytes 12165120 | tf_op jit(solution)/shard_map/reduce_scatter | solution.py:754
  13.0 8.5 %collective-permute-start = (bf16[1024,128]{1,0:T(8,128)(2,1)S(1)}, bf16[1024,128]{1,0:T(8,128)(2,1)S(1)}, u32[]{:S(2)}, u32[]{:S(2)}) collective-permute-start(bf16[1024,128]{1,0:T(8,128)(2,1)S(1)} %constant_dynamic-update-slice_fusion), channel_id=1, source_target_pairs={{0,1},{1,2},{2,3},{3,0},{4,5},{5,6},{6,7},{7,4},{8,9},{9,10},{10,1... | collective-permute-start | bytes 786440 | tf_op jit(solution)/shard_map/ppermute | solution.py:465
  13.1 36.4 %collective-permute-start.1 = (bf16[1024,128]{1,0:T(8,128)(2,1)S(1)}, bf16[1024,128]{1,0:T(8,128)(2,1)S(1)}, u32[]{:S(2)}, u32[]{:S(2)}) collective-permute-start(bf16[1024,128]{1,0:T(8,128)(2,1)S(1)} %constant_dynamic-update-slice_fusion), channel_id=1, source_target_pairs={{0,2},{1,3},{2,0},{3,1},{4,6},{5,7},{6,4},{7,5},{8,10},{9,11},{10,... | collective-permute-start | bytes 786440 | tf_op jit(solution)/shard_map/ppermute | solution.py:465
  15.0 34.5 %collective-permute-start.2 = (bf16[1024,128]{1,0:T(8,128)(2,1)S(1)}, bf16[1024,128]{1,0:T(8,128)(2,1)S(1)}, u32[]{:S(2)}, u32[]{:S(2)}) collective-permute-start(bf16[1024,128]{1,0:T(8,128)(2,1)S(1)} %constant_dynamic-update-slice_fusion), channel_id=1, source_target_pairs={{0,3},{1,0},{2,1},{3,2},{4,7},{5,4},{6,5},{7,6},{8,11},{9,8},{10,9... | collective-permute-start | bytes 786440 | tf_op jit(solution)/shard_map/ppermute | solution.py:465
  49.6 25.1 %copy-start.54 = (bf16[256]{0:T(256)(128)(2,1)S(1)}, bf16[256]{0:T(256)(128)(2,1)}, u32[]{:S(2)}) copy-start(bf16[256]{0:T(256)(128)(2,1)} %param.28) | copy-start | bytes 1540
  49.6 25.7 %copy-start.49 = (bf16[512]{0:T(512)(128)(2,1)S(1)}, bf16[512]{0:T(512)(128)(2,1)}, u32[]{:S(2)}) copy-start(bf16[512]{0:T(512)(128)(2,1)} %param.27) | copy-start | bytes 3076
  49.6 26.3 %copy-start.47 = (bf16[1024]{0:T(1024)(128)(2,1)S(1)}, bf16[1024]{0:T(1024)(128)(2,1)}, u32[]{:S(2)}) copy-start(bf16[1024]{0:T(1024)(128)(2,1)} %param.20) | copy-start | bytes 6148
  49.6 26.9 %copy-start.48 = (bf16[1024]{0:T(1024)(128)(2,1)S(1)}, bf16[1024]{0:T(1024)(128)(2,1)}, u32[]{:S(2)}) copy-start(bf16[1024]{0:T(1024)(128)(2,1)} %param.30) | copy-start | bytes 6148
  49.7 27.4 %copy-start.45 = (bf16[1024,16]{0,1:T(8,128)(2,1)S(1)}, bf16[1024,16]{0,1:T(8,128)(2,1)}, u32[]{:S(2)}) copy-start(bf16[1024,16]{0,1:T(8,128)(2,1)} %param.25) | copy-start | bytes 98308
  49.8 20.5 %collective-permute-start.4 = (bf16[2048,128]{1,0:T(8,128)(2,1)S(1)}, bf16[2048,128]{1,0:T(8,128)(2,1)S(1)}, u32[]{:S(2)}, u32[]{:S(2)}) collective-permute-start(bf16[2048,128]{1,0:T(8,128)(2,1)S(1)} %get-tuple-element.213), channel_id=1, source_target_pairs={{0,4},{4,0},{1,5},{5,1},{2,6},{6,2},{3,7},{7,3},{8,12},{12,8},{9,1... | collective-permute-start | bytes 1572872 | tf_op jit(solution)/shard_map/ppermute | solution.py:469
  51.4 21.3 %collective-permute-start.3 = (bf16[2048,128]{1,0:T(8,128)(2,1)S(1)}, bf16[2048,128]{1,0:T(8,128)(2,1)S(1)}, u32[]{:S(2)}, u32[]{:S(2)}) collective-permute-start(bf16[2048,128]{1,0:T(8,128)(2,1)S(1)} %get-tuple-element.214), channel_id=1, source_target_pairs={{0,16},{16,0},{1,17},{17,1},{2,18},{18,2},{3,19},{19,3},{4,20},{20... | collective-permute-start | bytes 1572872 | tf_op jit(solution)/shard_map/ppermute | solution.py:469
  72.8 30.2 %copy-start.8 = (bf16[4096,128]{1,0:T(8,128)(2,1)}, bf16[4096,128]{1,0:T(8,128)(2,1)S(1)}, u32[]{:S(2)}) copy-start(bf16[4096,128]{1,0:T(8,128)(2,1)S(1)} %constant_dynamic-update-slice_fusion.14.refs_0_.refs_1_) | copy-start | bytes 3145732
  72.8 26.6 %collective-permute-start.5 = (bf16[4096,128]{1,0:T(8,128)(2,1)S(1)}, bf16[4096,128]{1,0:T(8,128)(2,1)}, u32[]{:S(2)}, u32[]{:S(2)}) collective-permute-start(bf16[4096,128]{1,0:T(8,128)(2,1)S(1)} %constant_dynamic-update-slice_fusion.14.refs_0_.refs_1_), channel_id=1, source_target_pairs={{0,4},{4,0},{1,5},{5,1},{2,6},{6,2},{3,7},{7,3},{8,12},{12,8},{9,1... | collective-permute-start | bytes 3145736 | tf_op jit(solution)/shard_map/ppermute | solution.py:469
  73.1 26.3 %collective-permute-start.8 = (bf16[4096,128]{1,0:T(8,128)(2,1)S(1)}, bf16[4096,128]{1,0:T(8,128)(2,1)S(1)}, u32[]{:S(2)}, u32[]{:S(2)}) collective-permute-start(bf16[4096,128]{1,0:T(8,128)(2,1)S(1)} %constant_dynamic-update-slice_fusion.32.refs_0_.refs_1_), channel_id=1, source_target_pairs={{0,16},{16,0},{1,17},{17,1},{2,18},{18,2},{3,19},{19,3},{4,20},{20... | collective-permute-start | bytes 3145736 | tf_op jit(solution)/shard_map/ppermute | solution.py:469
  83.5 21.7 %collective-permute-start.6 = (bf16[4096,128]{1,0:T(8,128)(2,1)S(1)}, bf16[4096,128]{1,0:T(8,128)(2,1)S(1)}, u32[]{:S(2)}, u32[]{:S(2)}) collective-permute-start(bf16[4096,128]{1,0:T(8,128)(2,1)S(1)} %constant_dynamic-update-slice_fusion.14.refs_0_.refs_1_), channel_id=1, source_target_pairs={{0,8},{8,0},{1,9},{9,1},{2,10},{10,2},{3,11},{11,3},{4,12},{12,4},... | collective-permute-start | bytes 3145736 | tf_op jit(solution)/shard_map/ppermute | solution.py:469
  83.5 28.0 %collective-permute-start.9 = (bf16[4096,128]{1,0:T(8,128)(2,1)S(1)}, bf16[4096,128]{1,0:T(8,128)(2,1)}, u32[]{:S(2)}, u32[]{:S(2)}) collective-permute-start(bf16[4096,128]{1,0:T(8,128)(2,1)S(1)} %constant_dynamic-update-slice_fusion.32.refs_0_.refs_1_), channel_id=1, source_target_pairs={{0,8},{8,0},{1,9},{9,1},{2,10},{10,2},{3,11},{11,3},{4,12},{12,4},... | collective-permute-start | bytes 3145736 | tf_op jit(solution)/shard_map/ppermute | solution.py:469
  99.4 6.8 %collective-permute-start.7 = (bf16[4096,128]{1,0:T(8,128)(2,1)}, bf16[4096,128]{1,0:T(8,128)(2,1)}, u32[]{:S(2)}, u32[]{:S(2)}) collective-permute-start(bf16[4096,128]{1,0:T(8,128)(2,1)} %collective-permute-done.5.refs_2_.refs_3_), channel_id=1, source_target_pairs={{0,8},{8,0},{1,9},{9,1},{2,10},{10,2},{3,11},{11,3},{4,12},{12,4},... | collective-permute-start | bytes 3145736 | tf_op jit(solution)/shard_map/ppermute | solution.py:469
  99.4 12.1 %collective-permute-start.10 = (bf16[4096,128]{1,0:T(8,128)(2,1)S(1)}, bf16[4096,128]{1,0:T(8,128)(2,1)}, u32[]{:S(2)}, u32[]{:S(2)}) collective-permute-start(bf16[4096,128]{1,0:T(8,128)(2,1)S(1)} %collective-permute-done.8.refs_2_.refs_3_), channel_id=1, source_target_pairs={{0,8},{8,0},{1,9},{9,1},{2,10},{10,2},{3,11},{11,3},{4,12},{12,4},... | collective-permute-start | bytes 3145736 | tf_op jit(solution)/shard_map/ppermute | solution.py:469
  132.2 6.4 %collective-permute-start.13 = (bf16[272,128]{1,0:T(8,128)(2,1)S(1)}, bf16[272,128]{1,0:T(8,128)(2,1)S(1)}, u32[]{:S(2)}, u32[]{:S(2)}) collective-permute-start(bf16[272,128]{1,0:T(8,128)(2,1)S(1)} %get-tuple-element.191), channel_id=1, source_target_pairs={{0,1},{1,2},{2,3},{3,0},{4,5},{5,6},{6,7},{7,4},{8,9},{9,10},{10,1... | collective-permute-start | bytes 208904 | tf_op jit(solution)/shard_map/ppermute | solution.py:465
  132.2 19.3 %collective-permute-start.12 = (bf16[272,128]{1,0:T(8,128)(2,1)S(1)}, bf16[272,128]{1,0:T(8,128)(2,1)S(1)}, u32[]{:S(2)}, u32[]{:S(2)}) collective-permute-start(bf16[272,128]{1,0:T(8,128)(2,1)S(1)} %get-tuple-element.192), channel_id=1, source_target_pairs={{0,2},{1,3},{2,0},{3,1},{4,6},{5,7},{6,4},{7,5},{8,10},{9,11},{10,... | collective-permute-start | bytes 208904 | tf_op jit(solution)/shard_map/ppermute | solution.py:465
  136.0 15.5 %collective-permute-start.11 = (bf16[272,128]{1,0:T(8,128)(2,1)S(1)}, bf16[272,128]{1,0:T(8,128)(2,1)S(1)}, u32[]{:S(2)}, u32[]{:S(2)}) collective-permute-start(bf16[272,128]{1,0:T(8,128)(2,1)S(1)} %get-tuple-element.193), channel_id=1, source_target_pairs={{0,3},{1,0},{2,1},{3,2},{4,7},{5,4},{6,5},{7,6},{8,11},{9,8},{10,9... | collective-permute-start | bytes 208904 | tf_op jit(solution)/shard_map/ppermute | solution.py:465
  154.0 4.5 collective-permute-start.14
  156.4 13.3 %collective-permute-start.18 = (bf16[4,256,128]{2,1,0:T(8,128)(2,1)S(1)}, bf16[4,256,128]{2,1,0:T(8,128)(2,1)S(1)}, u32[]{:S(2)}, u32[]{:S(2)}) collective-permute-start(bf16[4,256,128]{2,1,0:T(8,128)(2,1)S(1)} %slice_bitcast_fusion.2), channel_id=1, source_target_pairs={{1,0},{3,2},{5,4},{7,6},{9,8},{11,10},{13,12},{15,14},{17,16},{19,... | collective-permute-start | bytes 786440 | tf_op jit(solution)/shard_map/ppermute | solution.py:488
  160.9 7.6 %collective-permute-start.15 = (bf16[256,128]{1,0:T(8,128)(2,1)}, bf16[256,128]{1,0:T(8,128)(2,1)S(1)}, u32[]{:S(2)}, u32[]{:S(2)}) collective-permute-start(bf16[256,128]{1,0:T(8,128)(2,1)} %get-tuple-element.80), channel_id=1, source_target_pairs={{0,1},{1,2},{2,3},{3,0},{4,5},{5,6},{6,7},{7,4},{8,9},{9,10},{10,1... | collective-permute-start | bytes 196616 | tf_op jit(solution)/shard_map/ppermute | solution.py:465
  160.9 8.0 %collective-permute-start.16 = (bf16[256,128]{1,0:T(8,128)(2,1)}, bf16[256,128]{1,0:T(8,128)(2,1)S(1)}, u32[]{:S(2)}, u32[]{:S(2)}) collective-permute-start(bf16[256,128]{1,0:T(8,128)(2,1)} %get-tuple-element.81), channel_id=1, source_target_pairs={{0,2},{1,3},{2,0},{3,1},{4,6},{5,7},{6,4},{7,5},{8,10},{9,11},{10,... | collective-permute-start | bytes 196616 | tf_op jit(solution)/shard_map/ppermute | solution.py:465
  161.7 7.2 %collective-permute-start.17 = (bf16[256,128]{1,0:T(8,128)(2,1)}, bf16[256,128]{1,0:T(8,128)(2,1)S(1)}, u32[]{:S(2)}, u32[]{:S(2)}) collective-permute-start(bf16[256,128]{1,0:T(8,128)(2,1)} %get-tuple-element.82), channel_id=1, source_target_pairs={{0,3},{1,0},{2,1},{3,2},{4,7},{5,4},{6,5},{7,6},{8,11},{9,8},{10,9... | collective-permute-start | bytes 196616 | tf_op jit(solution)/shard_map/ppermute | solution.py:465
  182.6 67.5 %copy-start = (f32[640,1024]{1,0:T(8,128)}, f32[640,1024]{1,0:T(8,128)S(1)}, u32[]{:S(2)}) copy-start(f32[640,1024]{1,0:T(8,128)S(1)} %get-tuple-element.253.resid_ref) | copy-start | bytes 7864324
  246.9 13.7 %collective-permute-start.19 = (bf16[4,4,704,128]{3,2,1,0:T(8,128)(2,1)}, bf16[4,4,704,128]{3,2,1,0:T(8,128)(2,1)S(1)}, u32[]{:S(2)}, u32[]{:S(2)}) collective-permute-start(bf16[4,4,704,128]{3,2,1,0:T(8,128)(2,1)} %get-tuple-element.90), channel_id=1, source_target_pairs={{0,8},{8,0},{1,9},{9,1},{2,10},{10,2},{3,11},{11,3},{4,12},{12,4},... | collective-permute-start | bytes 8650760 | tf_op jit(solution)/shard_map/ppermute | solution.py:469
  253.4 3.6 collective-permute-start.20
  259.1 31.7 %collective-permute-start.37 = (bf16[1024,256]{0,1:T(8,128)(2,1)}, bf16[1024,256]{0,1:T(8,128)(2,1)S(1)}, u32[]{:S(2)}, u32[]{:S(2)}) collective-permute-start(bf16[1024,256]{0,1:T(8,128)(2,1)} %pad_maximum_fusion.4), channel_id=1, source_target_pairs={{0,4},{4,0},{1,5},{5,1},{2,6},{6,2},{3,7},{7,3},{8,12},{12,8},{9,1... | collective-permute-start | bytes 1572872 | tf_op jit(solution)/shard_map/ppermute | solution.py:469
  276.5 16.3 %copy-start.46 = (f32[4,1,256]{2,1,0:T(1,128)S(1)}, f32[4,1,256]{2,1,0:T(1,128)}, u32[]{:S(2)}) copy-start(f32[4,1,256]{2,1,0:T(1,128)} %get-tuple-element.114) | copy-start | bytes 12292
  276.5 37.7 %collective-permute-start.21 = (bf16[1024,512]{0,1:T(8,128)(2,1)}, bf16[1024,512]{0,1:T(8,128)(2,1)}, u32[]{:S(2)}, u32[]{:S(2)}) collective-permute-start(bf16[1024,512]{0,1:T(8,128)(2,1)} %convolution_convert_fusion.2), channel_id=1, source_target_pairs={{0,8},{8,0},{1,9},{9,1},{2,10},{10,2},{3,11},{11,3},{4,12},{12,4},... | collective-permute-start | bytes 3145736 | tf_op jit(solution)/shard_map/ppermute | solution.py:469
  277.1 4.8 %collective-permute-start.24 = (bf16[272,128]{1,0:T(8,128)(2,1)S(1)}, bf16[272,128]{1,0:T(8,128)(2,1)S(1)}, u32[]{:S(2)}, u32[]{:S(2)}) collective-permute-start(bf16[272,128]{1,0:T(8,128)(2,1)S(1)} %get-tuple-element.187), channel_id=1, source_target_pairs={{0,1},{1,2},{2,3},{3,0},{4,5},{5,6},{6,7},{7,4},{8,9},{9,10},{10,1... | collective-permute-start | bytes 208904 | tf_op jit(solution)/shard_map/ppermute | solution.py:465
  279.3 7.8 %collective-permute-start.23 = (bf16[272,128]{1,0:T(8,128)(2,1)S(1)}, bf16[272,128]{1,0:T(8,128)(2,1)S(1)}, u32[]{:S(2)}, u32[]{:S(2)}) collective-permute-start(bf16[272,128]{1,0:T(8,128)(2,1)S(1)} %get-tuple-element.188), channel_id=1, source_target_pairs={{0,2},{1,3},{2,0},{3,1},{4,6},{5,7},{6,4},{7,5},{8,10},{9,11},{10,... | collective-permute-start | bytes 208904 | tf_op jit(solution)/shard_map/ppermute | solution.py:465
  280.1 7.0 %collective-permute-start.22 = (bf16[272,128]{1,0:T(8,128)(2,1)S(1)}, bf16[272,128]{1,0:T(8,128)(2,1)S(1)}, u32[]{:S(2)}, u32[]{:S(2)}) collective-permute-start(bf16[272,128]{1,0:T(8,128)(2,1)S(1)} %get-tuple-element.189), channel_id=1, source_target_pairs={{0,3},{1,0},{2,1},{3,2},{4,7},{5,4},{6,5},{7,6},{8,11},{9,8},{10,9... | collective-permute-start | bytes 208904 | tf_op jit(solution)/shard_map/ppermute | solution.py:465
  282.0 29.6 %collective-permute-start.29 = (bf16[4,256,128]{2,1,0:T(8,128)(2,1)}, bf16[4,256,128]{2,1,0:T(8,128)(2,1)}, u32[]{:S(2)}, u32[]{:S(2)}) collective-permute-start(bf16[4,256,128]{2,1,0:T(8,128)(2,1)} %get-tuple-element.103), channel_id=1, source_target_pairs={{0,1},{2,3},{4,5},{6,7},{8,9},{10,11},{12,13},{14,15},{16,17},{18,... | collective-permute-start | bytes 786440 | tf_op jit(solution)/shard_map/ppermute | solution.py:490
  289.6 4.5 collective-permute-start.25
  292.8 23.6 %copy-start.15 = (bf16[1024,256]{0,1:T(8,128)(2,1)}, bf16[1024,256]{0,1:T(8,128)(2,1)S(1)}, u32[]{:S(2)}) copy-start(bf16[1024,256]{0,1:T(8,128)(2,1)S(1)} %add_convert_fusion.9) | copy-start | bytes 1572868
  296.5 17.6 %copy-start.19 = (bf16[640,1024]{1,0:T(8,128)(2,1)S(1)}, bf16[640,1024]{1,0:T(8,128)(2,1)}, u32[]{:S(2)}) copy-start(bf16[640,1024]{1,0:T(8,128)(2,1)} %get-tuple-element.94) | copy-start | bytes 3932164
  296.5 5.2 %collective-permute-start.26 = (bf16[256,128]{1,0:T(8,128)(2,1)}, bf16[256,128]{1,0:T(8,128)(2,1)S(1)}, u32[]{:S(2)}, u32[]{:S(2)}) collective-permute-start(bf16[256,128]{1,0:T(8,128)(2,1)} %get-tuple-element.100), channel_id=1, source_target_pairs={{0,1},{1,2},{2,3},{3,0},{4,5},{5,6},{6,7},{7,4},{8,9},{9,10},{10,1... | collective-permute-start | bytes 196616 | tf_op jit(solution)/shard_map/ppermute | solution.py:465
  298.0 11.1 %collective-permute-start.27 = (bf16[256,128]{1,0:T(8,128)(2,1)}, bf16[256,128]{1,0:T(8,128)(2,1)S(1)}, u32[]{:S(2)}, u32[]{:S(2)}) collective-permute-start(bf16[256,128]{1,0:T(8,128)(2,1)} %get-tuple-element.101), channel_id=1, source_target_pairs={{0,2},{1,3},{2,0},{3,1},{4,6},{5,7},{6,4},{7,5},{8,10},{9,11},{10,... | collective-permute-start | bytes 196616 | tf_op jit(solution)/shard_map/ppermute | solution.py:465
  298.5 11.5 %collective-permute-start.28 = (bf16[256,128]{1,0:T(8,128)(2,1)}, bf16[256,128]{1,0:T(8,128)(2,1)S(1)}, u32[]{:S(2)}, u32[]{:S(2)}) collective-permute-start(bf16[256,128]{1,0:T(8,128)(2,1)} %get-tuple-element.102), channel_id=1, source_target_pairs={{0,3},{1,0},{2,1},{3,2},{4,7},{5,4},{6,5},{7,6},{8,11},{9,8},{10,9... | collective-permute-start | bytes 196616 | tf_op jit(solution)/shard_map/ppermute | solution.py:465
  301.7 38.0 %collective-permute-start.31 = (bf16[2,2,704,128]{3,2,1,0:T(8,128)(2,1)}, bf16[2,2,704,128]{3,2,1,0:T(8,128)(2,1)}, u32[]{:S(2)}, u32[]{:S(2)}) collective-permute-start(bf16[2,2,704,128]{3,2,1,0:T(8,128)(2,1)} %get-tuple-element.163), channel_id=1, source_target_pairs={{0,16},{16,0},{1,17},{17,1},{2,18},{18,2},{3,19},{19,3},{4,20},{20... | collective-permute-start | bytes 2162696 | tf_op jit(solution)/shard_map/ppermute | solution.py:469
  309.1 27.7 %collective-permute-start.30 = (bf16[2,2,704,128]{3,2,1,0:T(8,128)(2,1)}, bf16[2,2,704,128]{3,2,1,0:T(8,128)(2,1)}, u32[]{:S(2)}, u32[]{:S(2)}) collective-permute-start(bf16[2,2,704,128]{3,2,1,0:T(8,128)(2,1)} %pad_maximum_fusion), channel_id=1, source_target_pairs={{0,4},{4,0},{1,5},{5,1},{2,6},{6,2},{3,7},{7,3},{8,12},{12,8},{9,1... | collective-permute-start | bytes 2162696 | tf_op jit(solution)/shard_map/ppermute | solution.py:469
  317.6 36.9 %collective-permute-start.40 = (bf16[1024,256]{0,1:T(8,128)(2,1)}, bf16[1024,256]{0,1:T(8,128)(2,1)}, u32[]{:S(2)}, u32[]{:S(2)}) collective-permute-start(bf16[1024,256]{0,1:T(8,128)(2,1)} %concatenate.105), channel_id=1, source_target_pairs={{0,16},{16,0},{1,17},{17,1},{2,18},{18,2},{3,19},{19,3},{4,20},{20... | collective-permute-start | bytes 1572872 | tf_op jit(solution)/shard_map/ppermute | solution.py:469
  338.8 33.3 %collective-permute-start.46 = (bf16[2,704,128]{2,1,0:T(8,128)(2,1)}, bf16[2,704,128]{2,1,0:T(8,128)(2,1)}, u32[]{:S(2)}, u32[]{:S(2)}) collective-permute-start(bf16[2,704,128]{2,1,0:T(8,128)(2,1)} %get-tuple-element.159), channel_id=1, source_target_pairs={{0,16},{16,0},{1,17},{17,1},{2,18},{18,2},{3,19},{19,3},{4,20},{20... | collective-permute-start | bytes 1081352 | tf_op jit(solution)/shard_map/ppermute | solution.py:469
  341.7 26.9 %collective-permute-start.47 = (bf16[2,704,128]{2,1,0:T(8,128)(2,1)}, bf16[2,704,128]{2,1,0:T(8,128)(2,1)}, u32[]{:S(2)}, u32[]{:S(2)}) collective-permute-start(bf16[2,704,128]{2,1,0:T(8,128)(2,1)} %get-tuple-element.161), channel_id=1, source_target_pairs={{0,4},{4,0},{1,5},{5,1},{2,6},{6,2},{3,7},{7,3},{8,12},{12,8},{9,1... | collective-permute-start | bytes 1081352 | tf_op jit(solution)/shard_map/ppermute | solution.py:469
  342.8 15.8 %collective-permute-start.33 = (bf16[1024,512]{0,1:T(8,128)(2,1)S(1)}, bf16[1024,512]{0,1:T(8,128)(2,1)S(1)}, u32[]{:S(2)}, u32[]{:S(2)}) collective-permute-start(bf16[1024,512]{0,1:T(8,128)(2,1)S(1)} %convolution_convert_fusion), channel_id=1, source_target_pairs={{0,8},{8,0},{1,9},{9,1},{2,10},{10,2},{3,11},{11,3},{4,12},{12,4},... | collective-permute-start | bytes 3145736 | tf_op jit(solution)/shard_map/ppermute | solution.py:469
  342.8 12.9 %collective-permute-start.32 = (bf16[1024,512]{0,1:T(8,128)(2,1)S(1)}, bf16[1024,512]{0,1:T(8,128)(2,1)S(1)}, u32[]{:S(2)}, u32[]{:S(2)}) collective-permute-start(bf16[1024,512]{0,1:T(8,128)(2,1)S(1)} %convolution_convert_fusion.1), channel_id=1, source_target_pairs={{0,8},{8,0},{1,9},{9,1},{2,10},{10,2},{3,11},{11,3},{4,12},{12,4},... | collective-permute-start | bytes 3145736 | tf_op jit(solution)/shard_map/ppermute | solution.py:469
  357.7 26.7 %collective-permute-start.41 = (bf16[1024,256]{0,1:T(8,128)(2,1)}, bf16[1024,256]{0,1:T(8,128)(2,1)}, u32[]{:S(2)}, u32[]{:S(2)}) collective-permute-start(bf16[1024,256]{0,1:T(8,128)(2,1)} %concatenate.106), channel_id=1, source_target_pairs={{0,16},{16,0},{1,17},{17,1},{2,18},{18,2},{3,19},{19,3},{4,20},{20... | collective-permute-start | bytes 1572872 | tf_op jit(solution)/shard_map/ppermute | solution.py:469
  361.3 26.1 %collective-permute-start.38 = (bf16[1024,256]{0,1:T(8,128)(2,1)}, bf16[1024,256]{0,1:T(8,128)(2,1)}, u32[]{:S(2)}, u32[]{:S(2)}) collective-permute-start(bf16[1024,256]{0,1:T(8,128)(2,1)} %pad_maximum_fusion.5), channel_id=1, source_target_pairs={{0,4},{4,0},{1,5},{5,1},{2,6},{6,2},{3,7},{7,3},{8,12},{12,8},{9,1... | collective-permute-start | bytes 1572872 | tf_op jit(solution)/shard_map/ppermute | solution.py:469
  368.7 15.7 %copy-start.22 = (bf16[1024,512]{0,1:T(8,128)(2,1)S(1)}, bf16[1024,512]{0,1:T(8,128)(2,1)}, u32[]{:S(2)}) copy-start(bf16[1024,512]{0,1:T(8,128)(2,1)} %copy-done.21) | copy-start | bytes 3145732
  368.7 1.6 collective-permute-start.34
  369.8 15.8 %slice-start.1 = ((bf16[1024,256]{0,1:T(8,128)(2,1)}), bf16[1024,128]{0,1:T(8,128)(2,1)S(1)}, s32[]{:S(2)}) async-start(bf16[1024,256]{0,1:T(8,128)(2,1)} %copy-done.17), calls=%async_computation.5 | async-start | bytes 524288 | tf_op jit(solution)/shard_map/slice | solution.py:868
  371.2 16.3 %copy-start.26 = (bf16[1024,128]{0,1:T(8,128)(2,1)S(1)}, bf16[1024,128]{0,1:T(8,128)(2,1)}, u32[]{:S(2)}) copy-start(bf16[1024,128]{0,1:T(8,128)(2,1)} %get-tuple-element.173) | copy-start | bytes 786436
  371.2 12.0 %collective-permute-start.35 = (f32[32,1024]{1,0:T(8,128)S(1)}, f32[32,1024]{1,0:T(8,128)S(1)}, u32[]{:S(2)}, u32[]{:S(2)}) collective-permute-start(f32[32,1024]{1,0:T(8,128)S(1)} %add.331), channel_id=1, source_target_pairs={{0,4},{4,0},{1,5},{5,1},{2,6},{6,2},{3,7},{7,3},{8,12},{12,8},{9,1... | collective-permute-start | bytes 393224 | tf_op jit(solution)/shard_map/ppermute | solution.py:469
  383.2 14.3 %collective-permute-start.36 = (f32[32,1024]{1,0:T(8,128)S(1)}, f32[32,1024]{1,0:T(8,128)}, u32[]{:S(2)}, u32[]{:S(2)}) collective-permute-start(f32[32,1024]{1,0:T(8,128)S(1)} %add.332), channel_id=1, source_target_pairs={{0,16},{16,0},{1,17},{17,1},{2,18},{18,2},{3,19},{19,3},{4,20},{20... | collective-permute-start | bytes 393224 | tf_op jit(solution)/shard_map/ppermute | solution.py:469
  386.5 12.1 %collective-permute-start.42 = (bf16[2048,128]{0,1:T(8,128)(2,1)}, bf16[2048,128]{0,1:T(8,128)(2,1)}, u32[]{:S(2)}, u32[]{:S(2)}) collective-permute-start(bf16[2048,128]{0,1:T(8,128)(2,1)} %pad_maximum_fusion.7), channel_id=1, source_target_pairs={{0,4},{4,0},{1,5},{5,1},{2,6},{6,2},{3,7},{7,3},{8,12},{12,8},{9,1... | collective-permute-start | bytes 1572872 | tf_op jit(solution)/shard_map/ppermute | solution.py:469
  389.8 13.8 %collective-permute-start.39 = (bf16[2048,128]{0,1:T(8,128)(2,1)}, bf16[2048,128]{0,1:T(8,128)(2,1)S(1)}, u32[]{:S(2)}, u32[]{:S(2)}) collective-permute-start(bf16[2048,128]{0,1:T(8,128)(2,1)} %pad_maximum_fusion.6), channel_id=1, source_target_pairs={{0,16},{16,0},{1,17},{17,1},{2,18},{18,2},{3,19},{19,3},{4,20},{20... | collective-permute-start | bytes 1572872 | tf_op jit(solution)/shard_map/ppermute | solution.py:469
  391.9 32.2 %all-to-all-start = ((bf16[4,704,128]{2,1,0:T(8,128)(2,1)}), bf16[4,704,128]{2,1,0:T(8,128)(2,1)S(1)}, u32[]{:S(2)}, u32[]{:S(2)}) async-start(bf16[4,704,128]{2,1,0:T(8,128)(2,1)} %pad_maximum_fusion.2), calls=%async_computation.1 | async-start | bytes 1441792 | tf_op jit(solution)/shard_map/all_to_all | solution.py:1102
  404.0 21.4 %collective-permute-start.45 = (bf16[1280,128]{0,1:T(8,128)(2,1)S(1)}, bf16[1280,128]{0,1:T(8,128)(2,1)S(1)}, u32[]{:S(2)}, u32[]{:S(2)}) collective-permute-start(bf16[1280,128]{0,1:T(8,128)(2,1)S(1)} %get-tuple-element.236), channel_id=1, source_target_pairs={{0,1},{1,2},{2,3},{3,0},{4,5},{5,6},{6,7},{7,4},{8,9},{9,10},{10,1... | collective-permute-start | bytes 983048 | tf_op jit(solution)/shard_map/ppermute | solution.py:465
  404.1 44.8 %collective-permute-start.44 = (bf16[1280,128]{0,1:T(8,128)(2,1)S(1)}, bf16[1280,128]{0,1:T(8,128)(2,1)S(1)}, u32[]{:S(2)}, u32[]{:S(2)}) collective-permute-start(bf16[1280,128]{0,1:T(8,128)(2,1)S(1)} %get-tuple-element.237), channel_id=1, source_target_pairs={{0,2},{1,3},{2,0},{3,1},{4,6},{5,7},{6,4},{7,5},{8,10},{9,11},{10,... | collective-permute-start | bytes 983048 | tf_op jit(solution)/shard_map/ppermute | solution.py:465
  408.4 41.3 %collective-permute-start.43 = (bf16[1280,128]{0,1:T(8,128)(2,1)S(1)}, bf16[1280,128]{0,1:T(8,128)(2,1)S(1)}, u32[]{:S(2)}, u32[]{:S(2)}) collective-permute-start(bf16[1280,128]{0,1:T(8,128)(2,1)S(1)} %get-tuple-element.238), channel_id=1, source_target_pairs={{0,3},{1,0},{2,1},{3,2},{4,7},{5,4},{6,5},{7,6},{8,11},{9,8},{10,9... | collective-permute-start | bytes 983048 | tf_op jit(solution)/shard_map/ppermute | solution.py:465
  (44 other events, 193.7 us)
Sparse Core Ops, SparseCore 0:
  10.8 150.0 all-gather.2
  247.0 171.7 reduce-scatter.1

commit v3 on v2

--- a/solution.py
+++ b/solution.py
@@ -517,10 +517,7 @@
 ):
     take_columns(gain_one_ref, order_ref, new_one_ref)
     take_columns(gain_two_ref, order_ref, new_two_ref)
-    for j in range(8):
-        new_rank_in_ref[j * 128 : (j + 1) * 128, :] = rank_in_ref[
-            pl.ds(pl.multiple_of(order_ref[j] * 128, 128), 128), :
-        ]
+    take_columns(rank_in_ref, order_ref, new_rank_in_ref)
     for k in range(heads):
         lanes = pl.ds(pl.multiple_of(order_ref[16 + k] * DK, DK), DK)
         new_rank_out_ref[:, k * DK : (k + 1) * DK] = rank_out_ref[:, lanes]
@@ -544,6 +541,34 @@
         compiler_params=params(),
         name=name,
     )(*smem_args, *args)
+
+
+def pack_kernel(q_ref, k_ref, v_ref, g_ref, o_ref, gate_ref, up_ref, down_ref, mixer_ref, ffn_ref):
+    at = 0
+    for ref in (q_ref, k_ref, g_ref, v_ref):
+        for i in range(ref.shape[1] // 128):
+            mixer_ref[at : at + 128, :] = ref[:, i * 128 : (i + 1) * 128].T
+            at += 128
+    mixer_ref[at:, :] = o_ref[...]
+    units = down_ref.shape[0]
+    for i, ref in enumerate((gate_ref, up_ref)):
+        ffn_ref[i * units : (i + 1) * units, :] = ref[...]
+    ffn_ref[2 * units :, :] = down_ref[...]
+
+
+def pack_weights(w_query, w_key, w_value, w_outgate, w_output, w_gate, w_up, w_down):
+    if not split_axes():
+        mixer = [w_query.T, w_key.T, w_outgate.T, w_value.T, w_output]
+        return jnp.concatenate(mixer, axis=0), jnp.concatenate([w_gate.T, w_up.T, w_down], axis=0)
+    args = (w_query, w_key, w_value, w_outgate, w_output, w_gate.T, w_up.T, w_down)
+    rows = 2 * DK + 3 * DV
+    return call_whole(
+        pack_kernel,
+        [],
+        args,
+        [shaped((rows, 128), BF16), shaped((3 * w_down.shape[0], 128), BF16)],
+        "pack",
+    )
 
 
 def output_kernel(back_ref, resid_ref, feed_ref, out_ref):
@@ -576,15 +601,51 @@
     scratch[25:26, :] = ffn_ref[...]
     for j in range(8):
         lanes = pl.ds(pl.multiple_of(back_ref[8 + j] * 128, 128), 128)
-        small_ref[0:16, j * 128 : (j + 1) * 128] = scratch[0:16, lanes]
-        small_ref[24:26, j * 128 : (j + 1) * 128] = scratch[24:26, lanes]
-    width = heads * DK
+        small_ref[j * 32 : j * 32 + 16, :] = scratch[0:16, lanes]
+        small_ref[j * 32 + 24 : j * 32 + 26, :] = scratch[24:26, lanes]
     for k in range(heads):
         lanes = pl.ds(pl.multiple_of(back_ref[16 + k] * DK, DK), DK)
-        small_ref[16:24, k * DK : (k + 1) * DK] = rank_out_ref[0:8, lanes]
-        small_ref[16:24, width + k * DK : width + (k + 1) * DK] = rank_out_ref[8:16, lanes]
-        small_ref[26:27, k * DK : (k + 1) * DK] = bias_ref[:, lanes]
-    small_ref[26:27, width : width + DV] = group_ref[...]
+        small_ref[k * 32 + 16 : k * 32 + 24, :] = rank_out_ref[0:8, lanes]
+        small_ref[(heads + k) * 32 + 16 : (heads + k) * 32 + 24, :] = rank_out_ref[8:16, lanes]
+        small_ref[k * 32 + 26 : k * 32 + 27, :] = bias_ref[:, lanes]
+    for k in range(DV // 128):
+        small_ref[(heads + k) * 32 + 26 : (heads + k) * 32 + 27, :] = group_ref[:, k * 128 : (k + 1) * 128]
+
+
+def last_kernel(heads, count, order_ref, *refs):
+    parts, outs, scratch = refs[:count], refs[count:-1], refs[-1]
+    q_ref, k_ref, v_ref, g_ref, o_ref, mixer_ref, in_ref, out_ref, bias_ref, group_ref, ffn_ref = outs
+    small = 4 * DV
+
+    def summed(at, rows):
+        total = parts[0][at : at + rows, :].astype(F32)
+        for part in parts[1:]:
+            total = total + part[at : at + rows, :].astype(F32)
+        return total
+
+    o_ref[...] = summed(0, DV)
+    at = DV
+    for ref in (g_ref, q_ref, k_ref, v_ref):
+        for i in range(ref.shape[1] // 128):
+            ref[:, i * 128 : (i + 1) * 128] = summed(at, 128).T
+            at += 128
+    for k in range(count):
+        scratch[k] = parts[k][small:, :].astype(F32)
+    total = scratch[order_ref[16]]
+    for z in range(1, count):
+        total = total + scratch[order_ref[16 + z]]
+    for j in range(8):
+        lanes = slice(j * 128, (j + 1) * 128)
+        block = total[j * 32 : (j + 1) * 32]
+        in_ref[:, lanes] = block[0:16]
+        mixer_ref[:, lanes] = block[24:25]
+        ffn_ref[:, lanes] = block[25:26]
+        k = j % heads
+        out_ref[(j // heads) * 8 : (j // heads) * 8 + 8, k * DK : (k + 1) * DK] = block[16:24]
+        if j < heads:
+            bias_ref[:, lanes] = block[26:27]
+        elif j < heads + DV // 128:
+            group_ref[:, k * 128 : (k + 1) * 128] = block[26:27]
 
 
 def split_axes():
@@ -622,13 +683,14 @@
             out[:, block * 128 : (block + 1) * 128] = refs[2 * i + half][...]
 
 
-def join_columns(pieces, swap):
-    rows = pieces[0].shape[0] // 2
+def join_columns(pieces, swap, part):
+    rows = pieces[0].shape[0] // 4
     tile = 512
     specs, args = [], []
     for piece in pieces:
         for half in range(2):
-            specs.append(pl.BlockSpec((tile, 128), functools.partial(lambda at, i: (at + i, 0), half * (rows // tile))))
+            start = (2 * half + part) * (rows // tile)
+            specs.append(pl.BlockSpec((tile, 128), functools.partial(lambda at, i: (at + i, 0), start)))
             args.append(piece)
     return pl.pallas_call(
         functools.partial(join_kernel, swap),
@@ -733,9 +795,8 @@
     )(order, every, rows, upstream)
 
 
-def gather_units(parts):
+def gather_units(shard):
     count = lax.axis_size("tp")
-    shard = jnp.concatenate(parts, axis=0)
     rows = shard.shape[0]
     if not split_axes():
         wide = lax.all_gather(shard, ("dpo", "core", "ctx"), axis=1, tiled=True)
@@ -756,14 +817,13 @@
     )
 
 
-def gather_slots(shards):
+def gather_slots(shard, sizes):
     count = lax.axis_size("tp")
-    shard = jnp.concatenate(shards, axis=0)
     slots = [shard] + [shifted(shard, "tp", k) for k in range(1, count)]
     stacks, at = [], 0
-    for part in shards:
-        stacks.append([slot[at : at + part.shape[0]] for slot in slots])
-        at += part.shape[0]
+    for size in sizes:
+        stacks.append([slot[at : at + size] for slot in slots])
+        at += size
     return stacks
 
 
@@ -788,12 +848,18 @@
         self.far = swapped(self.pair, self.first[1])
         return self.far
 
-    def hop_core(self, *hold):
+    def hop_core(self):
+        if split_axes():
+            self.pieces = [
+                self.pair, self.far, swapped(self.pair, "core"), swapped(self.far, "core")
+            ]
+
+    def join(self, part, *hold):
         if not split_axes():
-            return self.whole
-        far = tie(self.far, *hold)
-        pieces = [self.pair, far, swapped(self.pair, "core"), swapped(far, "core")]
-        return join_columns(pieces, self.first[0] == "dpo")
+            rows = self.whole.shape[0] // 2
+            return self.whole[part * rows : (part + 1) * rows]
+        pieces = [tie(self.pieces[0], *hold)] + self.pieces[1:]
+        return join_columns(pieces, self.first[0] == "dpo", part)
 
 
 class Scatter:
@@ -806,19 +872,24 @@
             self.received = swapped(far, "core")
         return far
 
-    def one(self, near):
+    def one(self, nears):
         if not split_axes():
+            near = jnp.concatenate(nears, axis=0)
             self.kept = jnp.concatenate([near, self.sent.astype(F32)], axis=-1)
             return None
-        near = near + self.received.astype(F32)
-        quarter = near.shape[-1] // 4
-        blocks = [near[..., i * quarter : (i + 1) * quarter] for i in range(4)]
-        if self.first[0] == "ctx":
-            kept, sent = (blocks[0], blocks[2]), (blocks[1], blocks[3])
-        else:
-            kept, sent = (blocks[0], blocks[1]), (blocks[2], blocks[3])
-        self.kept = jnp.concatenate(kept, axis=-1).astype(BF16)
-        self.sent = jnp.concatenate(sent, axis=-1).astype(BF16)
+        kept, sent, at = [], [], 0
+        for near in nears:
+            near = near + self.received[at : at + near.shape[0]].astype(F32)
+            at += near.shape[0]
+            quarter = near.shape[-1] // 4
+            blocks = [near[:, i * quarter : (i + 1) * quarter] for i in range(4)]
+            if self.first[0] == "ctx":
+                mine, other = (blocks[0], blocks[2]), (blocks[1], blocks[3])
+            else:
+                mine, other = (blocks[0], blocks[1]), (blocks[2], blocks[3])
+            kept.append(jnp.concatenate(mine, axis=-1).astype(BF16))
+            sent.append(jnp.concatenate(other, axis=-1).astype(BF16))
+        self.kept, self.sent = jnp.concatenate(kept, axis=0), jnp.concatenate(sent, axis=0)
         self.received = swapped(self.sent, self.first[0])
         return self.sent
 
@@ -857,24 +928,6 @@
         return self.sent
 
 
-def hop_two_together(ones, *hold):
-    if not split_axes():
-        return None
-    kept, sent = [], []
-    for one in ones:
-        quarter = one.kept.shape[-1] // 2
-        sums = tie(one.kept, *hold).astype(F32) + one.received.astype(F32)
-        kept.append(sums[..., :quarter].astype(BF16))
-        sent.append(sums[..., quarter:].astype(BF16))
-    received = swapped(jnp.concatenate(sent, axis=0), ones[0].first[1])
-    at = 0
-    for i, one in enumerate(ones):
-        rows = kept[i].shape[0]
-        one.kept, one.received = kept[i], received[at : at + rows]
-        at += rows
-    return received
-
-
 def send_slots(slots):
     count = lax.axis_size("tp")
     return [slots[0]] + [shifted(slots[k], "tp", -k) for k in range(1, count)]
@@ -891,34 +944,10 @@
     return total
 
 
-def ordered_sum_kernel(count, order_ref, *refs):
-    scratch, out_ref = refs[-1], refs[-2]
-    for k in range(count):
-        scratch[k] = refs[k][...].astype(F32)
-    total = scratch[order_ref[16]]
-    for z in range(1, count):
-        total = total + scratch[order_ref[16 + z]]
-    out_ref[...] = total
-
-
 def sum_here(values):
     for axis in ("core", "ctx", "dpo"):
         values = values + swapped(values, axis)
     return values
-
-
-def sum_slots(parts, order):
-    vmem = pl.BlockSpec(memory_space=pltpu.VMEM)
-    shape = parts[0].shape
-    return pl.pallas_call(
-        functools.partial(ordered_sum_kernel, len(parts)),
-        in_specs=[smem()] + [vmem] * len(parts),
-        out_specs=vmem,
-        out_shape=shaped(shape, F32),
-        scratch_shapes=[pltpu.VMEM((len(parts), *shape), F32)],
-        compiler_params=params(),
-        name="ordered_sum",
-    )(order, *parts)
 
 
 def rms_scale(values):
@@ -958,26 +987,20 @@
     chunks = length // CHUNK
     units = w_down.shape[0]
 
-    stacks = gather_slots(
-        [jnp.concatenate([w_query.T, w_key.T], axis=0), w_outgate.T, w_value.T, w_output]
-    )
+    mixer_shard, ffn_shard = pack_weights(
+        w_query, w_key, w_value, w_outgate, w_output, w_gate, w_up, w_down
+    )
+    stacks = gather_slots(mixer_shard, [2 * DK, DV, DV, DV])
     takes = [Gather(stacks[:2], "dpo"), Gather(stacks[2:], "ctx")]
     order = column_order()
-    ffn_all = gather_units([w_gate.T, w_up.T, w_down])
-    first_hops = [take.hop_one() for take in takes]
-    for take in takes:
-        take.hop_two(*first_hops)
-    w_one, w_two = (take.hop_core() for take in takes)
-    w_qk, w_og_all = w_one[: heads * 2 * DK], w_one[heads * 2 * DK :]
-    w_val, w_out_all = w_two[: heads * DV], w_two[heads * DV :]
-
+    ffn_all = gather_units(ffn_shard)
     kinds = [
         shaped((length, width), BF16),
         shaped((length, width), BF16),
         shaped((length, width), BF16),
         shaped((1, width), F32),
         shaped((1, width), F32),
-        shaped((width, RANK), BF16),
+        shaped((RANK, width), BF16),
         shaped((RANK, heads * DK), BF16),
         shaped((1, heads * DK), F32),
     ]
@@ -989,7 +1012,7 @@
             cotangent[0],
             norm_mixer.astype(F32)[None],
             norm_ffn.astype(F32)[None],
-            w_rank_in,
+            w_rank_in.T,
             w_rank_out,
             gate_bias.astype(F32)[None],
         ],
@@ -1007,11 +1030,19 @@
     first_half = (starts % PIECE) == 0
     flags = jnp.stack([in_piece, in_piece & first_half]).astype(jnp.int32)
 
-    rank_low = nn(normed, rank_in).astype(BF16)
+    rank_low = nt(normed, rank_in).astype(BF16)
     gate_in = nn(rank_low, rank_out) + bias
+    first_hops = [take.hop_one() for take in takes]
+    for take in takes:
+        take.hop_two(*first_hops, gate_in)
+    for take in takes:
+        take.hop_core()
+    w_qk, w_val = (take.join(0) for take in takes)
+
     qk = nt(normed, w_qk).astype(BF16)
     values = nt(normed, w_val).astype(BF16)
     sums, local, future, ends = chunk_states(qk, values, gate_in, heads)
+    w_og_all, w_out_all = (take.join(1, ends) for take in takes)
     later = neighbour_future(future[:, 0], True)
     incoming = exchange_states(ends, False)
     outgate = nt(normed, w_og_all)
@@ -1037,50 +1068,52 @@
     grad_ffn_term = jnp.sum(d_norm_two * resid * scale_two, axis=0, keepdims=True)
     d_resid = upstream.astype(F32) + norm_back(d_norm_two, resid, scale_two, gain_two)
     d_branch = d_resid.astype(BF16)
-    give_out, give_gate = Scatter("ctx"), Scatter("dpo")
     d_gated = nt(d_branch, w_out_all)
-    if fast:
-        sent_down = [
-            give_down[i].one(
-                near_down[:, i * pairs : (i + 1) * pairs], received_down[:, i * pairs : (i + 1) * pairs]
-            )
-            for i in range(2)
-        ]
-        d_gated = tie(d_gated, *sent_down)
     d_outgate, d_mixed, gain_terms, back_local, back_ends, earlier = gate_back(
         flags, d_gated, outgate, mixed, gain_group, qk, sums, heads
     )
     grad_group_term = jnp.sum(gain_terms, axis=0)
+    if fast:
+        near_late = tie(near_down, d_outgate)
+        for i in range(2):
+            cut = slice(i * pairs, (i + 1) * pairs)
+            give_down[i].one(near_late[:, cut], received_down[:, cut])
     earlier = neighbour_future(earlier, False)
     back_incoming = exchange_states(back_ends, True)
-    give_out.core(tn(gated, d_branch[:, side:]).astype(BF16))
-    give_gate.core(tn(d_outgate, normed[:, side:]).astype(BF16))
-    near_out = give_out.one(tn(gated, d_branch[:, :side]))
-    near_gate = give_gate.one(tn(d_outgate, normed[:, :side]))
-    d_mixed = tie(d_mixed, near_out, near_gate)
+    far_out, far_gate = (
+        tn(left, right[:, side:]).astype(BF16) for left, right in ((gated, d_branch), (d_outgate, normed))
+    )
+    near_out, near_gate = tn(gated, d_branch[:, :side]), tn(d_outgate, normed[:, :side])
+    d_mixed = tie(
+        d_mixed, far_out, far_gate, near_out, near_gate, *[one.sent for one in give_down if fast]
+    )
     d_qk, d_val, d_gate_in = mix_back(
         flags, d_mixed, qk, values, sums, local, incoming, future, later, back_local, back_incoming, earlier, gate_in
     )
-    give_qk, give_val = Scatter("dpo"), Scatter("ctx")
+    give = [Scatter("ctx"), Scatter("dpo")]
+    far_in = [tn(left, normed[:, side:]).astype(BF16) for left in (d_val, d_qk)]
     far_in = [
-        give_qk.core(tn(d_qk, normed[:, side:]).astype(BF16)),
-        give_val.core(tn(d_val, normed[:, side:]).astype(BF16)),
+        give[0].core(jnp.concatenate([far_out, far_in[0]], axis=0)),
+        give[1].core(jnp.concatenate([far_gate, far_in[1]], axis=0)),
     ]
     second_down = step_down("two", *far_in)
+    d_gate_in = tie(d_gate_in, *far_in)
     grad_bias_here = jnp.sum(d_gate_in.astype(F32), axis=0, keepdims=True)
     grad_rank_here = tn(rank_low, d_gate_in)
     d_rank_low = nt(d_gate_in, rank_out).astype(BF16)
-    d_low = tie(d_qk, *far_in, *second_down)
-    d_normed = nn(d_low, w_qk) + nn(d_val, w_val) + nn(d_outgate, w_og_all) + nt(d_rank_low, rank_in)
-    d_tied = tie((d_qk, d_val), d_normed)
-    near_in = [give_qk.one(tn(d_tied[0], normed[:, :side])), give_val.one(tn(d_tied[1], normed[:, :side]))]
-    d_normed = tie(d_normed, *near_in)
+    d_tied = tie((d_qk, d_val), *second_down, grad_rank_here, d_rank_low)
+    near_in = [
+        give[0].one([near_out, tn(d_tied[1], normed[:, :side])]),
+        give[1].one([near_gate, tn(d_tied[0], normed[:, :side])]),
+    ]
+    d_low = tie((d_qk, d_val, d_outgate), *near_in)
+    d_normed = nn(d_low[0], w_qk) + nn(d_low[1], w_val) + nn(d_low[2], w_og_all) + nn(d_rank_low, rank_in)
     grad_rank_in_term = tn(d_rank_low, normed)
     grad_in, small = pl.pallas_call(
         functools.partial(finish_kernel, heads),
         in_specs=[smem()] + [pl.BlockSpec(memory_space=pltpu.VMEM)] * 9,
         out_specs=[pl.BlockSpec(memory_space=pltpu.VMEM)] * 2,
-        out_shape=[shaped((length, width), F32), shaped((32, width), F32)],
+        out_shape=[shaped((length, width), F32), shaped((256, 128), F32)],
         scratch_shapes=[pltpu.VMEM((CHUNK, width), F32)],
         compiler_params=params(),
         name="finish",
@@ -1102,49 +1135,85 @@
         parts_down = lax.all_to_all(slots_down, "tp", 0, 0, tiled=True)
         grad_down = add_slots([parts_down[k] for k in range(heads)])
     else:
+        parts_down = ()
         slots_down = jnp.concatenate([near_down, far_down], axis=0)
         slots_down = jnp.transpose(slots_down, (1, 2, 0, 3)).reshape(heads, units, width)
         grad_down = lax.psum_scatter(slots_down.astype(F32), "tp", scatter_dimension=0, tiled=True)
         grad_down = add_slots([grad_down[0]])
-    hop_two_together([give_out, give_val])
-    hop_two_together([give_gate, give_qk])
-    slots_in = [
-        one.sums().reshape(heads, DV, -1) for one in (give_out, give_gate, give_qk, give_val)
-    ]
-    slots_in = [[part[k] for part in slots_in] for k in range(heads)]
-    if fast:
-        small = sum_here(small).astype(BF16)
-        parts_in = send_slots(
-            [jnp.concatenate(slot + [small.reshape(-1, DK)], axis=0) for slot in slots_in]
-        )
-        rows = parts_in[0].shape[0] - small.size // DK
-        small = sum_slots([part[rows:].reshape(small.shape) for part in parts_in], order)
-        mixer_grads = add_slots([part[:rows] for part in parts_in])
-    else:
-        small = lax.psum(small, ("dpo", "core", "ctx", "tp"))
-        mixer_grads = add_slots(send_slots([jnp.concatenate(slot, axis=0) for slot in slots_in]))
+    hops = [one.two() for one in give]
+    parts = [one.sums(parts_down).reshape(2, heads, DV, -1) for one in give]
+    slots_in = [[parts[0][0, k], parts[1][0, k], parts[1][1, k], parts[0][1, k]] for k in range(heads)]
     hidden_out = call_whole(
         output_kernel, [order], [resid, feed], [shaped((length, width), BF16)], "output"
     )[0][None]
-    grad_output, grad_outgate, grad_heads = mixer_grads[:DV], mixer_grads[DV : 2 * DV], mixer_grads[2 * DV :]
     grads_ffn = grads_ffn.astype(F32)
-    grad_gate, grad_up = grads_ffn[:units], grads_ffn[units : 2 * units]
+    grad_gate, grad_up = grads_ffn[:units].T, grads_ffn[units : 2 * units].T
+    if not fast:
+        small = lax.psum(small, ("dpo", "core", "ctx", "tp"))
+        mixer = add_slots(send_slots([jnp.concatenate(slot, axis=0) for slot in slots_in]))
+        small = small.reshape(8, 32, 128)
+        flat = lambda row: small[:, row].reshape(width)
+        return (
+            hidden_out,
+            grad_in[None],
+            flat(24),
+            mixer[2 * DV : 2 * DV + DK].T,
+            mixer[2 * DV + DK : 3 * DV].T,
+            mixer[3 * DV :].T,
+            mixer[DV : 2 * DV].T,
+            jnp.swapaxes(small[:, :RANK], 1, 2).reshape(width, RANK),
+            jnp.transpose(small[:, 16:24].reshape(2, heads, 8, DK), (0, 2, 1, 3)).reshape(RANK, -1),
+            flat(26)[: heads * DK],
+            flat(26)[heads * DK : heads * DK + DV],
+            mixer[:DV],
+            flat(25),
+            grad_gate,
+            grad_up,
+            grad_down,
+        )
+    small = sum_here(tie(small, *hops)).astype(BF16)
+    parts_in = send_slots([jnp.concatenate([*slot, small], axis=0) for slot in slots_in])
+    parts_in[0] = tie(parts_in[0], grad_gate, grad_up, grad_down, hidden_out)
+    vmem = pl.BlockSpec(memory_space=pltpu.VMEM)
+    shapes = [
+        (128, DK),
+        (128, DK),
+        (128, DV),
+        (128, DV),
+        (DV, 128),
+        (1, width),
+        (RANK, width),
+        (RANK, heads * DK),
+        (1, heads * DK),
+        (1, DV),
+        (1, width),
+    ]
+    last = pl.pallas_call(
+        functools.partial(last_kernel, heads, heads),
+        in_specs=[smem()] + [vmem] * heads,
+        out_specs=[vmem] * len(shapes),
+        out_shape=[shaped(shape, F32) for shape in shapes],
+        scratch_shapes=[pltpu.VMEM((heads, 256, 128), F32)],
+        compiler_params=params(),
+        name="last",
+    )(order, *parts_in)
+    grad_query, grad_key, grad_value, grad_outgate, grad_output = last[:5]
     return (
         hidden_out,
         grad_in[None],
-        small[24],
-        grad_heads[:DK].T,
-        grad_heads[DK : 2 * DK].T,
-        grad_heads[2 * DK :].T,
-        grad_outgate.T,
-        small[:RANK].T,
-        jnp.concatenate([small[16:24, : heads * DK], small[16:24, heads * DK :]], axis=0),
-        small[26, : heads * DK],
-        small[26, heads * DK : heads * DK + DV],
+        last[5][0],
+        grad_query,
+        grad_key,
+        grad_value,
+        grad_outgate,
+        last[6].T,
+        last[7],
+        last[8][0],
+        last[9][0],
         grad_output,
-        small[25],
-        grad_gate.T,
-        grad_up.T,
+        last[10][0],
+        grad_gate,
+        grad_up,
         grad_down,
     )
 

time: 477 us -> 451 us (0.945)
  the two profiles are of different devices: /device:TPU:24 before, /device:TPU:12 now
where the time goes in v3:
time: 451 us; the launch traced here: 442 us
  Pallas kernels  131 us (29%)
  waiting for transfers between devices  128 us (28%)
  starting transfers between devices  52.9 us (12%)
  matrix products  49.4 us (11%)
  other arithmetic  38.1 us (8%)
  local copies, waits for them, and re-layouts  26.7 us (6%)
  between operations  15.3 us (3%)
    ppermute x24, waiting for transfers between devices, swapped(): return lax.ppermute(array, axis, [(0, 1), (1, 0)])  72 us
    ppermute x18, waiting for transfers between devices, shifted(): lax.ppermute(array, axis, [(i, (i + by) % size) for i in range(size)])  56.4 us
    pallas_call x1, Pallas kernels, feed_forward(): pl.pallas_call(functools.partial(ffn_kernel, units), grid_spec=pltpu.Pref...  53.7 us
    ppermute x18, starting transfers between devices, shifted(): lax.ppermute(array, axis, [(i, (i + by) % size) for i in range(size)])  29.5 us
    dot_general x10, matrix products, tn(): lax.dot_general(left, right, (((0,), (0,)), ((), ())), preferred_element_...  19.3 us
    dot_general x6, matrix products, nn(): lax.dot_general(left, right, (((1,), (0,)), ((), ())), preferred_element_...  15.1 us
    ppermute x24, starting transfers between devices, swapped(): return lax.ppermute(array, axis, [(0, 1), (1, 0)])  15 us
    dot_general x6, matrix products, nt(): lax.dot_general(left, right, (((1,), (1,)), ((), ())), preferred_element_...  15 us
  transfers between devices with their start and end apart: 47, of which 15 were waited for; matrix products, arithmetic and copies ran while one was open for 24% of the time, Pallas kernels for 17%

profile of v3, /device:TPU:12, one launch (start us, length us, event | category | flops | bytes accessed | tf_op | source)
XLA Modules:
  0.0 442.1 jit_solution(4108396684066804295)
XLA Ops:
  7.2 2.2 pack.1
  10.0 2.6 collective-permute-start.1
  12.6 2.5 collective-permute-start
  19.4 5.0 %begin.1 = (bf16[640,1024]{1,0:T(8,128)(2,1)}, bf16[640,1024]{1,0:T(8,128)(2,1)}, bf16[640,1024]{1,0:T(8,128)(2,1)}, f32[1,1024]{1,0:T(1,128)}, f32[1,1024]{1,0:...) custom-call(s32[20]{0:T(128)} %stack.162.order_ref.back_ref, ...), custom_call_target="tpu_custom_call" | custom-call | tf_op jit(solution)/shard_map/begin/pallas_call | solution.py:536
  24.4 1.8 convolution_convert_fusion.6
  26.2 2.2 convolution_add_fusion.gate_ref
  28.5 18.2 %collective-permute-done = bf16[1024,128]{1,0:T(8,128)(2,1)S(1)} collective-permute-done((bf16[1024,128]{1,0:T(8,128)(2,1)}, bf16[1024,128]{1,0:T(8,128)(2,1)S(1)}, u32[]{:S(2)}, u32[]{:S(2)}) %collective-permute-start) | collective-permute-done | bytes 262176 | tf_op jit(solution)/shard_map/ppermute | solution.py:465
  49.2 18.5 %collective-permute-done.4 = bf16[2048,128]{1,0:T(8,128)(2,1)S(1)} collective-permute-done((bf16[2048,128]{1,0:T(8,128)(2,1)S(1)}, bf16[2048,128]{1,0:T(8,128)(2,1)S(1)}, u32[]{:S(2)}, u32[]{:S(2)}) %collective-permute-start.4) | collective-permute-done | bytes 524320 | tf_op jit(solution)/shard_map/ppermute | solution.py:469
  67.8 2.5 collective-permute-done.3
  70.9 20.0 %collective-permute-done.8.refs_2_.refs_3_ = bf16[4096,128]{1,0:T(8,128)(2,1)S(1)} collective-permute-done((bf16[4096,128]{1,0:T(8,128)(2,1)S(1)}, bf16[4096,128]{1,0:T(8,128)(2,1)S(1)}, u32[]{:S(2)}, u32[]{:S(2)}) %collective-permute-start.8) | collective-permute-done | bytes 1048608 | tf_op jit(solution)/shard_map/ppermute | solution.py:469
  91.5 6.1 %collective-permute-done.5.refs_2_.refs_3_ = bf16[4096,128]{1,0:T(8,128)(2,1)} collective-permute-done((bf16[4096,128]{1,0:T(8,128)(2,1)S(1)}, bf16[4096,128]{1,0:T(8,128)(2,1)}, u32[]{:S(2)}, u32[]{:S(2)}) %collective-permute-start.5) | collective-permute-done | bytes 1048608 | tf_op jit(solution)/shard_map/ppermute | solution.py:469
  100.1 3.5 join.5
  103.7 3.2 join.4
  107.0 2.6 convolution_convert_fusion.value_ref
  109.6 2.6 convolution_convert_fusion.1.qk_ref
  112.2 6.6 %chunk_states.1 = (f32[640,512]{1,0:T(8,128)}, f32[4,5,256,128]{3,2,1,0:T(8,128)}, bf16[4,5,256,128]{3,2,1,0:T(8,128)(2,1)}, bf16[4,272,128]{2,1,0:T(8,128)(2,1)}) custom-call(bf16[640,1024]{1,0:T(8,128)(2,1)} %convolution_convert_fusion.1.qk_ref, bf16[640,1024]{1,0:T(8,128)(2,1)} %convolution_convert_fusion.value_ref, f32[640,512]{1,0:T(8,128)} %convolution_add_fusion.gate_ref), custom_call_target="tpu_custom_call" | custom-call | tf_op jit(solution)/shard_map/chunk_states/pallas_call | solution.py:313
  118.8 1.6 slice_bitcast_fusion.7
  120.4 2.8 collective-permute-start.13
  125.3 6.3 %collective-permute-done.13.refs_3_ = bf16[272,128]{1,0:T(8,128)(2,1)S(1)} collective-permute-done((bf16[272,128]{1,0:T(8,128)(2,1)S(1)}, bf16[272,128]{1,0:T(8,128)(2,1)S(1)}, u32[]{:S(2)}, u32[]{:S(2)}) %collective-permute-start.13) | collective-permute-done | bytes 69664 | tf_op jit(solution)/shard_map/ppermute | solution.py:465
  131.6 5.3 %collective-permute-done.12.refs_2_ = bf16[272,128]{1,0:T(8,128)(2,1)S(1)} collective-permute-done((bf16[272,128]{1,0:T(8,128)(2,1)S(1)}, bf16[272,128]{1,0:T(8,128)(2,1)S(1)}, u32[]{:S(2)}, u32[]{:S(2)}) %collective-permute-start.12) | collective-permute-done | bytes 69664 | tf_op jit(solution)/shard_map/ppermute | solution.py:465
  138.6 1.8 chain.4
  144.3 2.9 join.6
  147.8 1.8 chain.5
  149.7 4.5 %collective-permute-start.16 = (bf16[256,128]{1,0:T(8,128)(2,1)}, bf16[256,128]{1,0:T(8,128)(2,1)S(1)}, u32[]{:S(2)}, u32[]{:S(2)}) collective-permute-start(bf16[256,128]{1,0:T(8,128)(2,1)} %get-tuple-element.103), channel_id=1, source_target_pairs={{0,2},{1,3},{2,0},{3,1},{4,6},{5,7},{6,4},{7,5},{8,10},{9,11},{10,... | collective-permute-start | bytes 196616 | tf_op jit(solution)/shard_map/ppermute | solution.py:465
  154.1 2.4 collective-permute-start.17
  156.5 4.7 %fusion.30.outgate_ref = f32[640,1024]{1,0:T(8,128)} fusion(bf16[640,1024]{1,0:T(8,128)(2,1)S(1)} %copy-done.9, bf16[1024,1024]{1,0:T(8,128)(2,1)} %join.6), kind=kOutput, calls=%fused_computation.167 | convolution fusion | flops 1342177280 | bytes 6029312 | tf_op jit(solution)/shard_map/dot_general | solution.py:27
  161.2 2.9 join.7
  165.7 8.2 %mix.1 = (f32[640,1024]{1,0:T(8,128)}, bf16[640,1024]{1,0:T(8,128)(2,1)}) custom-call(s32[2,5]{1,0:T(2,128)} %add_convert_fusion.17.flags_ref, bf16[640,1024]{1,0:T(8,128)(2,1)} %convolution_convert_fusion.1.qk_ref, bf16[640,1024]{1,0:T(8,128)(2,1)} %convolution_convert_fusion.value_ref, f32[640,512]{1,0:T(8,128)} %get-tuple-element.97.sums_ref, ...), custom_call_target="tpu_custom_call" | custom-call | tf_op jit(solution)/shard_map/mix/pallas_call | solution.py:337
  173.9 4.0 multiply_reduce_fusion.2
  177.9 1.6 multiply_convert_fusion.rows_ref
  179.5 53.7 %feed_forward.1 = (f32[640,1024]{1,0:T(8,128)}, f32[640,1024]{1,0:T(8,128)}, bf16[8,4,1440,128]{3,2,1,0:T(8,128)(2,1)}, bf16[4,4,704,128]{3,2,1,0:T(8,128)(2,1)}, bf16[4,4,704,128]{3,2,1,0:T(8,128)(2,1)}) custom-call(s32[20]{0:T(128)} %stack.162.order_ref.back_ref, bf16[8,4,2112,128]{3,2,1,0:T(8,128)(2,1)} %bitcast.197, ...), custom_call_target="tpu_custom_call" | custom-call | tf_op jit(solution)/shard_map/feed_forward/pallas_call | solution.py:767
  233.3 3.1 multiply_reduce_fusion
  236.5 2.3 fusion.21
  238.8 3.1 fusion.31.d_gated_ref
  241.8 8.6 %gate_back.1 = (bf16[640,1024]{1,0:T(8,128)(2,1)}, bf16[640,1024]{1,0:T(8,128)(2,1)}, f32[4,1,256]{2,1,0:T(1,128)}, f32[4,5,256,128]{3,2,1,0:T(8,128)}, bf16[4,2...) custom-call(s32[2,5]{1,0:T(2,128)} %add_convert_fusion.17.flags_ref, f32[640,1024]{1,0:T(8,128)} %fusion.31.d_gated_ref, ...), custom_call_target="tpu_custom_call" | custom-call | tf_op jit(solution)/shard_map/gate_back/pallas_call | solution.py:362
  250.5 1.7 slice_bitcast_fusion.3
  254.9 2.8 fusion
  257.7 2.4 fusion.7
  260.1 1.8 collective-permute-done.20.refs_1_
  262.5 1.8 chain.6
  265.2 3.4 convolution_convert_fusion.4
  270.6 1.8 chain.7
  272.4 3.8 collective-permute-start.24
  276.3 1.9 collective-permute-start.25
  278.1 3.5 convolution_convert_fusion.5
  281.6 2.0 copy.37
  284.2 1.6 pad_maximum_fusion.8.back_incoming_ref
  288.4 3.4 add_convert_fusion
  295.0 14.2 %mix_back.1 = (bf16[640,1024]{1,0:T(8,128)(2,1)}, bf16[640,1024]{1,0:T(8,128)(2,1)}, bf16[640,512]{1,0:T(8,128)(2,1)}) custom-call(s32[2,5]{1,0:T(2,128)} %add_convert_fusion.17.flags_ref, bf16[640,1024]{1,0:T(8,128)(2,1)} %get-tuple-element.120.d_mixed_ref, bf16[640,1024]{1,0:T(8,128)(2,1)} %convolution_convert_fusion.1.qk_ref, ...), custom_call_target="tpu_custom_call" | custom-call | tf_op jit(solution)/shard_map/mix_back/pallas_call | solution.py:400
  309.3 2.5 convolution_convert_fusion.3
  337.4 5.7 %all-to-all-start = ((bf16[4,704,128]{2,1,0:T(8,128)(2,1)}), bf16[4,704,128]{2,1,0:T(8,128)(2,1)S(1)}, u32[]{:S(2)}, u32[]{:S(2)}) async-start(bf16[4,704,128]{2,1,0:T(8,128)(2,1)} %pad_maximum_fusion.5), calls=%async_computation | async-start | bytes 1441792 | tf_op jit(solution)/shard_map/all_to_all | solution.py:1135
  343.2 3.7 fusion.33
  348.8 3.2 add_add_fusion.d_normed_ref
  352.0 6.3 %finish.1 = (f32[640,1024]{1,0:T(8,128)}, f32[256,128]{1,0:T(8,128)}) custom-call(s32[20]{0:T(128)} %stack.162.order_ref.back_ref, f32[640,1024]{1,0:T(8,128)} %get-tuple-element.167.d_resid_ref, f32[640,1024]{1,0:T(8,128)} %add_add_fusion.d_normed_ref, bf16[640,1024]{1,0:T(8,128)(2,1)} %get-tuple-element.89.inputs_ref, ...), custom_call_target="tpu_custom_call" | custom-call | tf_op jit(solution)/shard_map/finish/pallas_call | solution.py:1112
  358.3 2.6 collective-permute-done.32
  360.9 1.6 add_convert_fusion.3
  363.2 9.5 %collective-permute-done.36 = bf16[2048,256]{1,0:T(8,128)(2,1)} collective-permute-done((bf16[2048,256]{1,0:T(8,128)(2,1)}, bf16[2048,256]{1,0:T(8,128)(2,1)}, u32[]{:S(2)}, u32[]{:S(2)}) %collective-permute-start.36) | collective-permute-done | bytes 1048608 | tf_op jit(solution)/shard_map/ppermute | solution.py:469
  372.7 1.6 add_convert_fusion.2
  377.5 4.3 output.1
  385.3 11.4 %collective-permute-done.37 = bf16[2048,128]{1,0:T(8,128)(2,1)S(1)} collective-permute-done((bf16[2048,128]{1,0:T(8,128)(2,1)}, bf16[2048,128]{1,0:T(8,128)(2,1)S(1)}, u32[]{:S(2)}, u32[]{:S(2)}) %collective-permute-start.37) | collective-permute-done | bytes 524320 | tf_op jit(solution)/shard_map/ppermute | solution.py:469
  400.2 2.4 collective-permute-start.42
  407.4 16.1 %collective-permute-done.42.refs_2_ = bf16[1280,128]{1,0:T(8,128)(2,1)S(1)} collective-permute-done((bf16[1280,128]{1,0:T(8,128)(2,1)S(1)}, bf16[1280,128]{1,0:T(8,128)(2,1)S(1)}, u32[]{:S(2)}, u32[]{:S(2)}) %collective-permute-start.42) | collective-permute-done | bytes 327712 | tf_op jit(solution)/shard_map/ppermute | solution.py:465
  423.5 7.7 %collective-permute-done.41.refs_1_ = bf16[1280,128]{1,0:T(8,128)(2,1)S(1)} collective-permute-done((bf16[1280,128]{1,0:T(8,128)(2,1)}, bf16[1280,128]{1,0:T(8,128)(2,1)S(1)}, u32[]{:S(2)}, u32[]{:S(2)}) %collective-permute-start.41) | collective-permute-done | bytes 327712 | tf_op jit(solution)/shard_map/ppermute | solution.py:465
  432.6 2.2 last.1
  (263 shorter events, 78.3 us)
Async XLA Ops:
  7.2 172.3 %all-gather.3.cloned.1.call-start = ((), (), s32[]{:S(2)}) async-start(), calls=%async_computation.3 | async-start | bytes 17842176 | tf_op jit(solution)/shard_map/all_gather | solution.py:805
  9.4 396.0 %reduce-scatter.2.cloned.1.call-start = ((), (), s32[]{:S(2)}) async-start(), calls=%async_computation.2 | async-start | bytes 12165120 | tf_op jit(solution)/shard_map/reduce_scatter | solution.py:815
  9.5 37.3 %collective-permute-start.2 = (bf16[1024,128]{1,0:T(8,128)(2,1)}, bf16[1024,128]{1,0:T(8,128)(2,1)S(1)}, u32[]{:S(2)}, u32[]{:S(2)}) collective-permute-start(bf16[1024,128]{1,0:T(8,128)(2,1)} %get-tuple-element.91), channel_id=1, source_target_pairs={{0,3},{1,0},{2,1},{3,2},{4,7},{5,4},{6,5},{7,6},{8,11},{9,8},{10,9... | collective-permute-start | bytes 786440 | tf_op jit(solution)/shard_map/ppermute | solution.py:465
  10.0 36.7 %collective-permute-start.1 = (bf16[1024,128]{1,0:T(8,128)(2,1)}, bf16[1024,128]{1,0:T(8,128)(2,1)S(1)}, u32[]{:S(2)}, u32[]{:S(2)}) collective-permute-start(bf16[1024,128]{1,0:T(8,128)(2,1)} %get-tuple-element.91), channel_id=1, source_target_pairs={{0,2},{1,3},{2,0},{3,1},{4,6},{5,7},{6,4},{7,5},{8,10},{9,11},{10,... | collective-permute-start | bytes 786440 | tf_op jit(solution)/shard_map/ppermute | solution.py:465
  12.6 34.1 %collective-permute-start = (bf16[1024,128]{1,0:T(8,128)(2,1)}, bf16[1024,128]{1,0:T(8,128)(2,1)S(1)}, u32[]{:S(2)}, u32[]{:S(2)}) collective-permute-start(bf16[1024,128]{1,0:T(8,128)(2,1)} %get-tuple-element.91), channel_id=1, source_target_pairs={{0,1},{1,2},{2,3},{3,0},{4,5},{5,6},{6,7},{7,4},{8,9},{9,10},{10,1... | collective-permute-start | bytes 786440 | tf_op jit(solution)/shard_map/ppermute | solution.py:465
  19.4 9.0 %copy-start.29 = (bf16[1024,128]{1,0:T(8,128)(2,1)S(1)}, bf16[1024,128]{1,0:T(8,128)(2,1)}, u32[]{:S(2)}) copy-start(bf16[1024,128]{1,0:T(8,128)(2,1)} %get-tuple-element.91) | copy-start | bytes 786436
  46.9 50.7 %copy-start.53 = (bf16[256]{0:T(256)(128)(2,1)S(1)}, bf16[256]{0:T(256)(128)(2,1)}, u32[]{:S(2)}) copy-start(bf16[256]{0:T(256)(128)(2,1)} %param.28) | copy-start | bytes 1540
  46.9 52.5 %copy-start.49 = (s32[1,4]{1,0:T(1,128)S(1)}, s32[1,4]{1,0:T(1,128)}, u32[]{:S(2)}) copy-start(s32[1,4]{1,0:T(1,128)} %param.19) | copy-start | bytes 52
  47.0 20.7 %collective-permute-start.4 = (bf16[2048,128]{1,0:T(8,128)(2,1)S(1)}, bf16[2048,128]{1,0:T(8,128)(2,1)S(1)}, u32[]{:S(2)}, u32[]{:S(2)}) collective-permute-start(bf16[2048,128]{1,0:T(8,128)(2,1)S(1)} %get-tuple-element.224), channel_id=1, source_target_pairs={{0,4},{4,0},{1,5},{5,1},{2,6},{6,2},{3,7},{7,3},{8,12},{12,8},{9,1... | collective-permute-start | bytes 1572872 | tf_op jit(solution)/shard_map/ppermute | solution.py:469
  48.6 21.7 %collective-permute-start.3 = (bf16[2048,128]{1,0:T(8,128)(2,1)S(1)}, bf16[2048,128]{1,0:T(8,128)(2,1)S(1)}, u32[]{:S(2)}, u32[]{:S(2)}) collective-permute-start(bf16[2048,128]{1,0:T(8,128)(2,1)S(1)} %get-tuple-element.225), channel_id=1, source_target_pairs={{0,16},{16,0},{1,17},{17,1},{2,18},{18,2},{3,19},{19,3},{4,20},{20... | collective-permute-start | bytes 1572872 | tf_op jit(solution)/shard_map/ppermute | solution.py:469
  67.8 32.3 %copy-start.2 = (bf16[4096,128]{1,0:T(8,128)(2,1)}, bf16[4096,128]{1,0:T(8,128)(2,1)S(1)}, u32[]{:S(2)}) copy-start(bf16[4096,128]{1,0:T(8,128)(2,1)S(1)} %constant_dynamic-update-slice_fusion.25.refs_0_.refs_1_) | copy-start | bytes 3145732
  70.3 20.7 %collective-permute-start.8 = (bf16[4096,128]{1,0:T(8,128)(2,1)S(1)}, bf16[4096,128]{1,0:T(8,128)(2,1)S(1)}, u32[]{:S(2)}, u32[]{:S(2)}) collective-permute-start(bf16[4096,128]{1,0:T(8,128)(2,1)S(1)} %constant_dynamic-update-slice_fusion.25.refs_0_.refs_1_), channel_id=1, source_target_pairs={{0,16},{16,0},{1,17},{17,1},{2,18},{18,2},{3,19},{19,3},{4,20},{20... | collective-permute-start | bytes 3145736 | tf_op jit(solution)/shard_map/ppermute | solution.py:469
  70.6 33.1 %copy-start.1 = (bf16[4096,128]{1,0:T(8,128)(2,1)}, bf16[4096,128]{1,0:T(8,128)(2,1)S(1)}, u32[]{:S(2)}) copy-start(bf16[4096,128]{1,0:T(8,128)(2,1)S(1)} %constant_dynamic-update-slice_fusion.8.refs_0_.refs_1_) | copy-start | bytes 3145732
  70.6 27.0 %collective-permute-start.5 = (bf16[4096,128]{1,0:T(8,128)(2,1)S(1)}, bf16[4096,128]{1,0:T(8,128)(2,1)}, u32[]{:S(2)}, u32[]{:S(2)}) collective-permute-start(bf16[4096,128]{1,0:T(8,128)(2,1)S(1)} %constant_dynamic-update-slice_fusion.8.refs_0_.refs_1_), channel_id=1, source_target_pairs={{0,4},{4,0},{1,5},{5,1},{2,6},{6,2},{3,7},{7,3},{8,12},{12,8},{9,1... | collective-permute-start | bytes 3145736 | tf_op jit(solution)/shard_map/ppermute | solution.py:469
  70.9 29.2 %collective-permute-start.9 = (bf16[4096,128]{1,0:T(8,128)(2,1)S(1)}, bf16[4096,128]{1,0:T(8,128)(2,1)}, u32[]{:S(2)}, u32[]{:S(2)}) collective-permute-start(bf16[4096,128]{1,0:T(8,128)(2,1)S(1)} %constant_dynamic-update-slice_fusion.25.refs_0_.refs_1_), channel_id=1, source_target_pairs={{0,8},{8,0},{1,9},{9,1},{2,10},{10,2},{3,11},{11,3},{4,12},{12,4},... | collective-permute-start | bytes 3145736 | tf_op jit(solution)/shard_map/ppermute | solution.py:469
  91.0 9.2 %copy-start.3 = (bf16[4096,128]{1,0:T(8,128)(2,1)}, bf16[4096,128]{1,0:T(8,128)(2,1)S(1)}, u32[]{:S(2)}) copy-start(bf16[4096,128]{1,0:T(8,128)(2,1)S(1)} %collective-permute-done.8.refs_2_.refs_3_) | copy-start | bytes 3145732
  91.0 9.1 %collective-permute-start.10 = (bf16[4096,128]{1,0:T(8,128)(2,1)S(1)}, bf16[4096,128]{1,0:T(8,128)(2,1)}, u32[]{:S(2)}, u32[]{:S(2)}) collective-permute-start(bf16[4096,128]{1,0:T(8,128)(2,1)S(1)} %collective-permute-done.8.refs_2_.refs_3_), channel_id=1, source_target_pairs={{0,8},{8,0},{1,9},{9,1},{2,10},{10,2},{3,11},{11,3},{4,12},{12,4},... | collective-permute-start | bytes 3145736 | tf_op jit(solution)/shard_map/ppermute | solution.py:469
  91.0 12.7 %collective-permute-start.6 = (bf16[4096,128]{1,0:T(8,128)(2,1)S(1)}, bf16[4096,128]{1,0:T(8,128)(2,1)}, u32[]{:S(2)}, u32[]{:S(2)}) collective-permute-start(bf16[4096,128]{1,0:T(8,128)(2,1)S(1)} %constant_dynamic-update-slice_fusion.8.refs_0_.refs_1_), channel_id=1, source_target_pairs={{0,8},{8,0},{1,9},{9,1},{2,10},{10,2},{3,11},{11,3},{4,12},{12,4},... | collective-permute-start | bytes 3145736 | tf_op jit(solution)/shard_map/ppermute | solution.py:469
  97.6 6.1 %collective-permute-start.7 = (bf16[4096,128]{1,0:T(8,128)(2,1)}, bf16[4096,128]{1,0:T(8,128)(2,1)}, u32[]{:S(2)}, u32[]{:S(2)}) collective-permute-start(bf16[4096,128]{1,0:T(8,128)(2,1)} %collective-permute-done.5.refs_2_.refs_3_), channel_id=1, source_target_pairs={{0,8},{8,0},{1,9},{9,1},{2,10},{10,2},{3,11},{11,3},{4,12},{12,4},... | collective-permute-start | bytes 3145736 | tf_op jit(solution)/shard_map/ppermute | solution.py:469
  120.4 11.1 %collective-permute-start.13 = (bf16[272,128]{1,0:T(8,128)(2,1)S(1)}, bf16[272,128]{1,0:T(8,128)(2,1)S(1)}, u32[]{:S(2)}, u32[]{:S(2)}) collective-permute-start(bf16[272,128]{1,0:T(8,128)(2,1)S(1)} %get-tuple-element.218), channel_id=1, source_target_pairs={{0,1},{1,2},{2,3},{3,0},{4,5},{5,6},{6,7},{7,4},{8,9},{9,10},{10,1... | collective-permute-start | bytes 208904 | tf_op jit(solution)/shard_map/ppermute | solution.py:465
  123.2 13.7 %collective-permute-start.12 = (bf16[272,128]{1,0:T(8,128)(2,1)S(1)}, bf16[272,128]{1,0:T(8,128)(2,1)S(1)}, u32[]{:S(2)}, u32[]{:S(2)}) collective-permute-start(bf16[272,128]{1,0:T(8,128)(2,1)S(1)} %get-tuple-element.219), channel_id=1, source_target_pairs={{0,2},{1,3},{2,0},{3,1},{4,6},{5,7},{6,4},{7,5},{8,10},{9,11},{10,... | collective-permute-start | bytes 208904 | tf_op jit(solution)/shard_map/ppermute | solution.py:465
  123.2 14.8 %collective-permute-start.11 = (bf16[272,128]{1,0:T(8,128)(2,1)S(1)}, bf16[272,128]{1,0:T(8,128)(2,1)S(1)}, u32[]{:S(2)}, u32[]{:S(2)}) collective-permute-start(bf16[272,128]{1,0:T(8,128)(2,1)S(1)} %get-tuple-element.220), channel_id=1, source_target_pairs={{0,3},{1,0},{2,1},{3,2},{4,7},{5,4},{6,5},{7,6},{8,11},{9,8},{10,9... | collective-permute-start | bytes 208904 | tf_op jit(solution)/shard_map/ppermute | solution.py:465
  131.6 7.0 %copy-start.34 = (bf16[272,128]{1,0:T(8,128)(2,1)}, bf16[272,128]{1,0:T(8,128)(2,1)S(1)}, u32[]{:S(2)}) copy-start(bf16[272,128]{1,0:T(8,128)(2,1)S(1)} %collective-permute-done.13.refs_3_) | copy-start | bytes 208900
  140.5 6.8 %collective-permute-start.14 = (bf16[256,128]{1,0:T(8,128)(2,1)}, bf16[256,128]{1,0:T(8,128)(2,1)S(1)}, u32[]{:S(2)}, u32[]{:S(2)}) collective-permute-start(bf16[256,128]{1,0:T(8,128)(2,1)} %get-tuple-element.100), channel_id=1, source_target_pairs={{0,4},{4,0},{1,5},{5,1},{2,6},{6,2},{3,7},{7,3},{8,12},{12,8},{9,1... | collective-permute-start | bytes 196616 | tf_op jit(solution)/shard_map/ppermute | solution.py:469
  143.0 21.9 %collective-permute-start.18 = (bf16[4,256,128]{2,1,0:T(8,128)(2,1)S(1)}, bf16[4,256,128]{2,1,0:T(8,128)(2,1)S(1)}, u32[]{:S(2)}, u32[]{:S(2)}) collective-permute-start(bf16[4,256,128]{2,1,0:T(8,128)(2,1)S(1)} %slice_bitcast_fusion.2), channel_id=1, source_target_pairs={{1,0},{3,2},{5,4},{7,6},{9,8},{11,10},{13,12},{15,14},{17,16},{19,... | collective-permute-start | bytes 786440 | tf_op jit(solution)/shard_map/ppermute | solution.py:488
  149.7 14.5 %collective-permute-start.15 = (bf16[256,128]{1,0:T(8,128)(2,1)}, bf16[256,128]{1,0:T(8,128)(2,1)S(1)}, u32[]{:S(2)}, u32[]{:S(2)}) collective-permute-start(bf16[256,128]{1,0:T(8,128)(2,1)} %get-tuple-element.102), channel_id=1, source_target_pairs={{0,1},{1,2},{2,3},{3,0},{4,5},{5,6},{6,7},{7,4},{8,9},{9,10},{10,1... | collective-permute-start | bytes 196616 | tf_op jit(solution)/shard_map/ppermute | solution.py:465
  149.7 14.5 %collective-permute-start.16 = (bf16[256,128]{1,0:T(8,128)(2,1)}, bf16[256,128]{1,0:T(8,128)(2,1)S(1)}, u32[]{:S(2)}, u32[]{:S(2)}) collective-permute-start(bf16[256,128]{1,0:T(8,128)(2,1)} %get-tuple-element.103), channel_id=1, source_target_pairs={{0,2},{1,3},{2,0},{3,1},{4,6},{5,7},{6,4},{7,5},{8,10},{9,11},{10,... | collective-permute-start | bytes 196616 | tf_op jit(solution)/shard_map/ppermute | solution.py:465
  154.1 10.0 %collective-permute-start.17 = (bf16[256,128]{1,0:T(8,128)(2,1)}, bf16[256,128]{1,0:T(8,128)(2,1)S(1)}, u32[]{:S(2)}, u32[]{:S(2)}) collective-permute-start(bf16[256,128]{1,0:T(8,128)(2,1)} %get-tuple-element.104), channel_id=1, source_target_pairs={{0,3},{1,0},{2,1},{3,2},{4,7},{5,4},{6,5},{7,6},{8,11},{9,8},{10,9... | collective-permute-start | bytes 196616 | tf_op jit(solution)/shard_map/ppermute | solution.py:465
  177.8 58.6 %copy-start = (f32[640,1024]{1,0:T(8,128)}, f32[640,1024]{1,0:T(8,128)S(1)}, u32[]{:S(2)}) copy-start(f32[640,1024]{1,0:T(8,128)S(1)} %get-tuple-element.256.resid_ref) | copy-start | bytes 7864324
  233.2 55.2 %collective-permute-start.19 = (bf16[4,4,704,128]{3,2,1,0:T(8,128)(2,1)}, bf16[4,4,704,128]{3,2,1,0:T(8,128)(2,1)}, u32[]{:S(2)}, u32[]{:S(2)}) collective-permute-start(bf16[4,4,704,128]{3,2,1,0:T(8,128)(2,1)} %get-tuple-element.119), channel_id=1, source_target_pairs={{0,8},{8,0},{1,9},{9,1},{2,10},{10,2},{3,11},{11,3},{4,12},{12,4},... | collective-permute-start | bytes 8650760 | tf_op jit(solution)/shard_map/ppermute | solution.py:469
  252.2 7.9 %collective-permute-start.22 = (bf16[272,128]{1,0:T(8,128)(2,1)S(1)}, bf16[272,128]{1,0:T(8,128)(2,1)S(1)}, u32[]{:S(2)}, u32[]{:S(2)}) collective-permute-start(bf16[272,128]{1,0:T(8,128)(2,1)S(1)} %get-tuple-element.214), channel_id=1, source_target_pairs={{0,1},{1,2},{2,3},{3,0},{4,5},{5,6},{6,7},{7,4},{8,9},{9,10},{10,1... | collective-permute-start | bytes 208904 | tf_op jit(solution)/shard_map/ppermute | solution.py:465
  253.3 6.7 %collective-permute-start.21 = (bf16[272,128]{1,0:T(8,128)(2,1)S(1)}, bf16[272,128]{1,0:T(8,128)(2,1)S(1)}, u32[]{:S(2)}, u32[]{:S(2)}) collective-permute-start(bf16[272,128]{1,0:T(8,128)(2,1)S(1)} %get-tuple-element.215), channel_id=1, source_target_pairs={{0,2},{1,3},{2,0},{3,1},{4,6},{5,7},{6,4},{7,5},{8,10},{9,11},{10,... | collective-permute-start | bytes 208904 | tf_op jit(solution)/shard_map/ppermute | solution.py:465
  254.9 7.0 %collective-permute-start.20 = (bf16[272,128]{1,0:T(8,128)(2,1)S(1)}, bf16[272,128]{1,0:T(8,128)(2,1)S(1)}, u32[]{:S(2)}, u32[]{:S(2)}) collective-permute-start(bf16[272,128]{1,0:T(8,128)(2,1)S(1)} %get-tuple-element.216), channel_id=1, source_target_pairs={{0,3},{1,0},{2,1},{3,2},{4,7},{5,4},{6,5},{7,6},{8,11},{9,8},{10,9... | collective-permute-start | bytes 208904 | tf_op jit(solution)/shard_map/ppermute | solution.py:465
  264.3 5.6 %collective-permute-start.23 = (bf16[256,128]{1,0:T(8,128)(2,1)}, bf16[256,128]{1,0:T(8,128)(2,1)S(1)}, u32[]{:S(2)}, u32[]{:S(2)}) collective-permute-start(bf16[256,128]{1,0:T(8,128)(2,1)} %get-tuple-element.123), channel_id=1, source_target_pairs={{0,4},{4,0},{1,5},{5,1},{2,6},{6,2},{3,7},{7,3},{8,12},{12,8},{9,1... | collective-permute-start | bytes 196616 | tf_op jit(solution)/shard_map/ppermute | solution.py:469
  268.7 17.2 %collective-permute-start.27 = (bf16[4,256,128]{2,1,0:T(8,128)(2,1)}, bf16[4,256,128]{2,1,0:T(8,128)(2,1)}, u32[]{:S(2)}, u32[]{:S(2)}) collective-permute-start(bf16[4,256,128]{2,1,0:T(8,128)(2,1)} %get-tuple-element.128), channel_id=1, source_target_pairs={{0,1},{2,3},{4,5},{6,7},{8,9},{10,11},{12,13},{14,15},{16,17},{18,... | collective-permute-start | bytes 786440 | tf_op jit(solution)/shard_map/ppermute | solution.py:490
  272.4 11.8 %collective-permute-start.24 = (bf16[256,128]{1,0:T(8,128)(2,1)}, bf16[256,128]{1,0:T(8,128)(2,1)}, u32[]{:S(2)}, u32[]{:S(2)}) collective-permute-start(bf16[256,128]{1,0:T(8,128)(2,1)} %get-tuple-element.125), channel_id=1, source_target_pairs={{0,1},{1,2},{2,3},{3,0},{4,5},{5,6},{6,7},{7,4},{8,9},{9,10},{10,1... | collective-permute-start | bytes 196616 | tf_op jit(solution)/shard_map/ppermute | solution.py:465
  276.3 7.9 %collective-permute-start.25 = (bf16[256,128]{1,0:T(8,128)(2,1)}, bf16[256,128]{1,0:T(8,128)(2,1)}, u32[]{:S(2)}, u32[]{:S(2)}) collective-permute-start(bf16[256,128]{1,0:T(8,128)(2,1)} %get-tuple-element.126), channel_id=1, source_target_pairs={{0,2},{1,3},{2,0},{3,1},{4,6},{5,7},{6,4},{7,5},{8,10},{9,11},{10,... | collective-permute-start | bytes 196616 | tf_op jit(solution)/shard_map/ppermute | solution.py:465
  278.1 6.1 %collective-permute-start.26 = (bf16[256,128]{1,0:T(8,128)(2,1)}, bf16[256,128]{1,0:T(8,128)(2,1)}, u32[]{:S(2)}, u32[]{:S(2)}) collective-permute-start(bf16[256,128]{1,0:T(8,128)(2,1)} %get-tuple-element.127), channel_id=1, source_target_pairs={{0,3},{1,0},{2,1},{3,2},{4,7},{5,4},{6,5},{7,6},{8,11},{9,8},{10,9... | collective-permute-start | bytes 196616 | tf_op jit(solution)/shard_map/ppermute | solution.py:465
  293.4 28.4 %collective-permute-start.30 = (bf16[2,2,704,128]{3,2,1,0:T(8,128)(2,1)}, bf16[2,2,704,128]{3,2,1,0:T(8,128)(2,1)}, u32[]{:S(2)}, u32[]{:S(2)}) collective-permute-start(bf16[2,2,704,128]{3,2,1,0:T(8,128)(2,1)} %get-tuple-element.175), channel_id=1, source_target_pairs={{0,16},{16,0},{1,17},{17,1},{2,18},{18,2},{3,19},{19,3},{4,20},{20... | collective-permute-start | bytes 2162696 | tf_op jit(solution)/shard_map/ppermute | solution.py:469
  294.4 24.4 %collective-permute-start.29 = (bf16[2,2,704,128]{3,2,1,0:T(8,128)(2,1)}, bf16[2,2,704,128]{3,2,1,0:T(8,128)(2,1)}, u32[]{:S(2)}, u32[]{:S(2)}) collective-permute-start(bf16[2,2,704,128]{3,2,1,0:T(8,128)(2,1)} %get-tuple-element.257), channel_id=1, source_target_pairs={{0,4},{4,0},{1,5},{5,1},{2,6},{6,2},{3,7},{7,3},{8,12},{12,8},{9,1... | collective-permute-start | bytes 2162696 | tf_op jit(solution)/shard_map/ppermute | solution.py:469
  311.9 12.2 %collective-permute-start.28 = (bf16[2048,512]{1,0:T(8,128)(2,1)S(1)}, bf16[2048,512]{1,0:T(8,128)(2,1)S(1)}, u32[]{:S(2)}, u32[]{:S(2)}) collective-permute-start(bf16[2048,512]{1,0:T(8,128)(2,1)S(1)} %pad_maximum_fusion), channel_id=1, source_target_pairs={{0,8},{8,0},{1,9},{9,1},{2,10},{10,2},{3,11},{11,3},{4,12},{12,4},... | collective-permute-start | bytes 6291464 | tf_op jit(solution)/shard_map/ppermute | solution.py:469
  314.5 16.0 %collective-permute-start.31 = (bf16[2048,512]{1,0:T(8,128)(2,1)S(1)}, bf16[2048,512]{1,0:T(8,128)(2,1)S(1)}, u32[]{:S(2)}, u32[]{:S(2)}) collective-permute-start(bf16[2048,512]{1,0:T(8,128)(2,1)S(1)} %pad_maximum_fusion.1), channel_id=1, source_target_pairs={{0,8},{8,0},{1,9},{9,1},{2,10},{10,2},{3,11},{11,3},{4,12},{12,4},... | collective-permute-start | bytes 6291464 | tf_op jit(solution)/shard_map/ppermute | solution.py:469
  318.8 5.3 %copy-start.50 = (bf16[640,1024]{1,0:T(8,128)(2,1)S(1)}, bf16[640,1024]{1,0:T(8,128)(2,1)}, u32[]{:S(2)}) copy-start(bf16[640,1024]{1,0:T(8,128)(2,1)} %get-tuple-element.138) | copy-start | bytes 3932164
  320.3 16.2 %collective-permute-start.33 = (bf16[2,704,128]{2,1,0:T(8,128)(2,1)S(1)}, bf16[2,704,128]{2,1,0:T(8,128)(2,1)S(1)}, u32[]{:S(2)}, u32[]{:S(2)}) collective-permute-start(bf16[2,704,128]{2,1,0:T(8,128)(2,1)S(1)} %get-tuple-element.171), channel_id=1, source_target_pairs={{0,16},{16,0},{1,17},{17,1},{2,18},{18,2},{3,19},{19,3},{4,20},{20... | collective-permute-start | bytes 1081352 | tf_op jit(solution)/shard_map/ppermute | solution.py:469
  323.1 13.2 %collective-permute-start.34 = (bf16[2,704,128]{2,1,0:T(8,128)(2,1)S(1)}, bf16[2,704,128]{2,1,0:T(8,128)(2,1)S(1)}, u32[]{:S(2)}, u32[]{:S(2)}) collective-permute-start(bf16[2,704,128]{2,1,0:T(8,128)(2,1)S(1)} %get-tuple-element.173), channel_id=1, source_target_pairs={{0,4},{4,0},{1,5},{5,1},{2,6},{6,2},{3,7},{7,3},{8,12},{12,8},{9,1... | collective-permute-start | bytes 1081352 | tf_op jit(solution)/shard_map/ppermute | solution.py:469
  329.4 31.5 %collective-permute-start.32 = (bf16[2048,256]{1,0:T(8,128)(2,1)}, bf16[2048,256]{1,0:T(8,128)(2,1)}, u32[]{:S(2)}, u32[]{:S(2)}) collective-permute-start(bf16[2048,256]{1,0:T(8,128)(2,1)} %maximum_maximum_fusion), channel_id=1, source_target_pairs={{0,4},{4,0},{1,5},{5,1},{2,6},{6,2},{3,7},{7,3},{8,12},{12,8},{9,1... | collective-permute-start | bytes 3145736 | tf_op jit(solution)/shard_map/ppermute | solution.py:469
  335.8 36.9 %collective-permute-start.36 = (bf16[2048,256]{1,0:T(8,128)(2,1)}, bf16[2048,256]{1,0:T(8,128)(2,1)}, u32[]{:S(2)}, u32[]{:S(2)}) collective-permute-start(bf16[2048,256]{1,0:T(8,128)(2,1)} %pad_maximum_fusion.2), channel_id=1, source_target_pairs={{0,16},{16,0},{1,17},{17,1},{2,18},{18,2},{3,19},{19,3},{4,20},{20... | collective-permute-start | bytes 3145736 | tf_op jit(solution)/shard_map/ppermute | solution.py:469
  337.4 45.5 %all-to-all-start = ((bf16[4,704,128]{2,1,0:T(8,128)(2,1)}), bf16[4,704,128]{2,1,0:T(8,128)(2,1)S(1)}, u32[]{:S(2)}, u32[]{:S(2)}) async-start(bf16[4,704,128]{2,1,0:T(8,128)(2,1)} %pad_maximum_fusion.5), calls=%async_computation | async-start | bytes 1441792 | tf_op jit(solution)/shard_map/all_to_all | solution.py:1135
  352.0 8.9 %copy-start.25 = (bf16[1024,128]{1,0:T(8,128)(2,1)S(1)}, bf16[1024,128]{1,0:T(8,128)(2,1)}, u32[]{:S(2)}) copy-start(bf16[1024,128]{1,0:T(8,128)(2,1)} %get-tuple-element.192) | copy-start | bytes 786436
  352.0 8.9 %copy-start.26 = (bf16[1024,128]{1,0:T(8,128)(2,1)S(1)}, bf16[1024,128]{1,0:T(8,128)(2,1)}, u32[]{:S(2)}) copy-start(bf16[1024,128]{1,0:T(8,128)(2,1)} %get-tuple-element.193) | copy-start | bytes 786436
  352.0 8.9 %copy-start.27 = (bf16[1024,128]{1,0:T(8,128)(2,1)S(1)}, bf16[1024,128]{1,0:T(8,128)(2,1)}, u32[]{:S(2)}) copy-start(bf16[1024,128]{1,0:T(8,128)(2,1)} %get-tuple-element.188) | copy-start | bytes 786436
  352.0 8.9 %copy-start.28 = (bf16[1024,128]{1,0:T(8,128)(2,1)S(1)}, bf16[1024,128]{1,0:T(8,128)(2,1)}, u32[]{:S(2)}) copy-start(bf16[1024,128]{1,0:T(8,128)(2,1)} %get-tuple-element.189) | copy-start | bytes 786436
  360.9 11.8 %copy-start.18 = (bf16[1024,256]{1,0:T(8,128)(2,1)S(1)}, bf16[1024,256]{1,0:T(8,128)(2,1)}, u32[]{:S(2)}) copy-start(bf16[1024,256]{1,0:T(8,128)(2,1)} %get-tuple-element.184) | copy-start | bytes 1572868
  360.9 11.8 %copy-start.19 = (bf16[1024,256]{1,0:T(8,128)(2,1)S(1)}, bf16[1024,256]{1,0:T(8,128)(2,1)}, u32[]{:S(2)}) copy-start(bf16[1024,256]{1,0:T(8,128)(2,1)} %get-tuple-element.182) | copy-start | bytes 1572868
  362.6 21.9 %collective-permute-start.35 = (bf16[2048,128]{1,0:T(8,128)(2,1)S(1)}, bf16[2048,128]{1,0:T(8,128)(2,1)S(1)}, u32[]{:S(2)}, u32[]{:S(2)}) collective-permute-start(bf16[2048,128]{1,0:T(8,128)(2,1)S(1)} %get-tuple-element.187), channel_id=1, source_target_pairs={{0,16},{16,0},{1,17},{17,1},{2,18},{18,2},{3,19},{19,3},{4,20},{20... | collective-permute-start | bytes 1572872 | tf_op jit(solution)/shard_map/ppermute | solution.py:469
  375.2 1.3 collective-permute-start.38
  376.5 6.4 %collective-permute-start.39 = (f32[256,128]{1,0:T(8,128)S(1)}, f32[256,128]{1,0:T(8,128)}, u32[]{:S(2)}, u32[]{:S(2)}) collective-permute-start(f32[256,128]{1,0:T(8,128)S(1)} %add.318), channel_id=1, source_target_pairs={{0,4},{4,0},{1,5},{5,1},{2,6},{6,2},{3,7},{7,3},{8,12},{12,8},{9,1... | collective-permute-start | bytes 393224 | tf_op jit(solution)/shard_map/ppermute | solution.py:469
  381.7 15.0 %collective-permute-start.37 = (bf16[2048,128]{1,0:T(8,128)(2,1)}, bf16[2048,128]{1,0:T(8,128)(2,1)S(1)}, u32[]{:S(2)}, u32[]{:S(2)}) collective-permute-start(bf16[2048,128]{1,0:T(8,128)(2,1)} %get-tuple-element.181), channel_id=1, source_target_pairs={{0,4},{4,0},{1,5},{5,1},{2,6},{6,2},{3,7},{7,3},{8,12},{12,8},{9,1... | collective-permute-start | bytes 1572872 | tf_op jit(solution)/shard_map/ppermute | solution.py:469
  383.8 15.0 %collective-permute-start.40 = (f32[256,128]{1,0:T(8,128)S(1)}, f32[256,128]{1,0:T(8,128)S(1)}, u32[]{:S(2)}, u32[]{:S(2)}) collective-permute-start(f32[256,128]{1,0:T(8,128)S(1)} %add.319), channel_id=1, source_target_pairs={{0,16},{16,0},{1,17},{17,1},{2,18},{18,2},{3,19},{19,3},{4,20},{20... | collective-permute-start | bytes 393224 | tf_op jit(solution)/shard_map/ppermute | solution.py:469
  400.2 31.0 %copy-start.30 = (bf16[1280,128]{1,0:T(8,128)(2,1)}, bf16[1280,128]{1,0:T(8,128)(2,1)S(1)}, u32[]{:S(2)}) copy-start(bf16[1280,128]{1,0:T(8,128)(2,1)S(1)} %get-tuple-element.150.refs_0_) | copy-start | bytes 983044
  400.2 23.3 %collective-permute-start.42 = (bf16[1280,128]{1,0:T(8,128)(2,1)S(1)}, bf16[1280,128]{1,0:T(8,128)(2,1)S(1)}, u32[]{:S(2)}, u32[]{:S(2)}) collective-permute-start(bf16[1280,128]{1,0:T(8,128)(2,1)S(1)} %get-tuple-element.250), channel_id=1, source_target_pairs={{0,2},{1,3},{2,0},{3,1},{4,6},{5,7},{6,4},{7,5},{8,10},{9,11},{10,... | collective-permute-start | bytes 983048 | tf_op jit(solution)/shard_map/ppermute | solution.py:465
  402.6 28.6 %collective-permute-start.41 = (bf16[1280,128]{1,0:T(8,128)(2,1)}, bf16[1280,128]{1,0:T(8,128)(2,1)S(1)}, u32[]{:S(2)}, u32[]{:S(2)}) collective-permute-start(bf16[1280,128]{1,0:T(8,128)(2,1)} %get-tuple-element.251), channel_id=1, source_target_pairs={{0,3},{1,0},{2,1},{3,2},{4,7},{5,4},{6,5},{7,6},{8,11},{9,8},{10,9... | collective-permute-start | bytes 983048 | tf_op jit(solution)/shard_map/ppermute | solution.py:465
  403.1 28.0 %collective-permute-start.43 = (bf16[1280,128]{1,0:T(8,128)(2,1)}, bf16[1280,128]{1,0:T(8,128)(2,1)S(1)}, u32[]{:S(2)}, u32[]{:S(2)}) collective-permute-start(bf16[1280,128]{1,0:T(8,128)(2,1)} %get-tuple-element.164), channel_id=1, source_target_pairs={{0,1},{1,2},{2,3},{3,0},{4,5},{5,6},{6,7},{7,4},{8,9},{9,10},{10,1... | collective-permute-start | bytes 983048 | tf_op jit(solution)/shard_map/ppermute | solution.py:465
  423.5 7.7 %copy-start.31 = (bf16[1280,128]{1,0:T(8,128)(2,1)}, bf16[1280,128]{1,0:T(8,128)(2,1)S(1)}, u32[]{:S(2)}) copy-start(bf16[1280,128]{1,0:T(8,128)(2,1)S(1)} %collective-permute-done.42.refs_2_) | copy-start | bytes 983044
  (37 other events, 83.1 us)
Sparse Core Ops, SparseCore 0:
  10.8 149.0 all-gather.2
  233.4 162.2 reduce-scatter.1

commit v4 on v3

--- a/solution.py
+++ b/solution.py
@@ -1083,9 +1083,8 @@
     far_out, far_gate = (
         tn(left, right[:, side:]).astype(BF16) for left, right in ((gated, d_branch), (d_outgate, normed))
     )
-    near_out, near_gate = tn(gated, d_branch[:, :side]), tn(d_outgate, normed[:, :side])
     d_mixed = tie(
-        d_mixed, far_out, far_gate, near_out, near_gate, *[one.sent for one in give_down if fast]
+        d_mixed, far_out, far_gate, *[one.sent for one in give_down if fast]
     )
     d_qk, d_val, d_gate_in = mix_back(
         flags, d_mixed, qk, values, sums, local, incoming, future, later, back_local, back_incoming, earlier, gate_in
@@ -1102,6 +1101,8 @@
     grad_rank_here = tn(rank_low, d_gate_in)
     d_rank_low = nt(d_gate_in, rank_out).astype(BF16)
     d_tied = tie((d_qk, d_val), *second_down, grad_rank_here, d_rank_low)
+    late = tie((gated, d_outgate), *far_in)
+    near_out, near_gate = tn(late[0], d_branch[:, :side]), tn(late[1], normed[:, :side])
     near_in = [
         give[0].one([near_out, tn(d_tied[1], normed[:, :side])]),
         give[1].one([near_gate, tn(d_tied[0], normed[:, :side])]),

time: 451 us -> 447 us (level)
  waiting for transfers between devices: 128 us -> 133 us
  local copies, waits for them, and re-layouts: 26.7 us -> 22.1 us
    reduce_scatter x1, waiting for transfers between devices: 0.01 us -> 15.3 us  [scatter_units(): lax.psum_scatter(grads.reshape(blocks * count, rows, lanes), ('dpo', 'cor...]
    ppermute x24, waiting for transfers between devices: 72 us -> 64.6 us  [swapped(): return lax.ppermute(array, axis, [(0, 1), (1, 0)])]
    unnamed x124 -> x126, local copies, waits for them, and re-layouts: 10.9 us -> 10 us
  transfers between devices with their start and end apart: 47 -> 47, of which waited for: 15 -> 23; matrix products, arithmetic and copies ran while one was open for 24% -> 22% of each run, Pallas kernels for 17% -> 17%
where the time goes in v4:
time: 447 us; the launch traced here: 438 us
  waiting for transfers between devices  133 us (30%)
  Pallas kernels  132 us (30%)
  starting transfers between devices  53.8 us (12%)
  matrix products  45 us (10%)
  other arithmetic  36.6 us (8%)
  local copies, waits for them, and re-layouts  22.1 us (5%)
  between operations  15.1 us (3%)
    ppermute x24, waiting for transfers between devices, swapped(): return lax.ppermute(array, axis, [(0, 1), (1, 0)])  64.6 us
    pallas_call x1, Pallas kernels, feed_forward(): pl.pallas_call(functools.partial(ffn_kernel, units), grid_spec=pltpu.Pref...  53.7 us
    ppermute x18, waiting for transfers between devices, shifted(): lax.ppermute(array, axis, [(i, (i + by) % size) for i in range(size)])  53.1 us
    ppermute x18, starting transfers between devices, shifted(): lax.ppermute(array, axis, [(i, (i + by) % size) for i in range(size)])  28 us
    ppermute x24, starting transfers between devices, swapped(): return lax.ppermute(array, axis, [(0, 1), (1, 0)])  17.2 us
    reduce_scatter x1, waiting for transfers between devices, scatter_units(): lax.psum_scatter(grads.reshape(blocks * count, rows, lanes), ('dpo', 'cor...  15.3 us
    dot_general x6, matrix products, nn(): lax.dot_general(left, right, (((1,), (0,)), ((), ())), preferred_element_...  15.1 us
    dot_general x10, matrix products, tn(): lax.dot_general(left, right, (((0,), (0,)), ((), ())), preferred_element_...  15 us
  transfers between devices with their start and end apart: 47, of which 23 were waited for; matrix products, arithmetic and copies ran while one was open for 22% of the time, Pallas kernels for 17%

profile of v4, /device:TPU:12, one launch (start us, length us, event | category | flops | bytes accessed | tf_op | source)
XLA Modules:
  0.0 438.1 jit_solution(629818676654732575)
XLA Ops:
  7.2 2.2 pack.1
  10.0 2.6 collective-permute-start.1
  12.6 2.5 collective-permute-start
  19.6 5.0 %begin.1 = (bf16[640,1024]{1,0:T(8,128)(2,1)}, bf16[640,1024]{1,0:T(8,128)(2,1)}, bf16[640,1024]{1,0:T(8,128)(2,1)}, f32[1,1024]{1,0:T(1,128)}, f32[1,1024]{1,0:...) custom-call(s32[20]{0:T(128)} %stack.162.order_ref.back_ref, ...), custom_call_target="tpu_custom_call" | custom-call | tf_op jit(solution)/shard_map/begin/pallas_call | solution.py:536
  24.5 1.8 convolution_convert_fusion.6
  26.3 2.2 convolution_add_fusion.gate_ref
  28.6 18.1 %collective-permute-done = bf16[1024,128]{1,0:T(8,128)(2,1)S(1)} collective-permute-done((bf16[1024,128]{1,0:T(8,128)(2,1)}, bf16[1024,128]{1,0:T(8,128)(2,1)S(1)}, u32[]{:S(2)}, u32[]{:S(2)}) %collective-permute-start) | collective-permute-done | bytes 262176 | tf_op jit(solution)/shard_map/ppermute | solution.py:465
  49.2 18.5 %collective-permute-done.4 = bf16[2048,128]{1,0:T(8,128)(2,1)S(1)} collective-permute-done((bf16[2048,128]{1,0:T(8,128)(2,1)S(1)}, bf16[2048,128]{1,0:T(8,128)(2,1)S(1)}, u32[]{:S(2)}, u32[]{:S(2)}) %collective-permute-start.4) | collective-permute-done | bytes 524320 | tf_op jit(solution)/shard_map/ppermute | solution.py:469
  67.8 2.5 collective-permute-done.3
  70.9 20.0 %collective-permute-done.8.refs_2_.refs_3_ = bf16[4096,128]{1,0:T(8,128)(2,1)S(1)} collective-permute-done((bf16[4096,128]{1,0:T(8,128)(2,1)S(1)}, bf16[4096,128]{1,0:T(8,128)(2,1)S(1)}, u32[]{:S(2)}, u32[]{:S(2)}) %collective-permute-start.8) | collective-permute-done | bytes 1048608 | tf_op jit(solution)/shard_map/ppermute | solution.py:469
  91.5 6.1 %collective-permute-done.5.refs_2_.refs_3_ = bf16[4096,128]{1,0:T(8,128)(2,1)} collective-permute-done((bf16[4096,128]{1,0:T(8,128)(2,1)S(1)}, bf16[4096,128]{1,0:T(8,128)(2,1)}, u32[]{:S(2)}, u32[]{:S(2)}) %collective-permute-start.5) | collective-permute-done | bytes 1048608 | tf_op jit(solution)/shard_map/ppermute | solution.py:469
  99.5 3.0 join.5
  102.5 3.8 join.4
  106.7 2.6 convolution_convert_fusion.value_ref
  109.3 2.6 convolution_convert_fusion.1.qk_ref
  111.9 6.6 %chunk_states.1 = (f32[640,512]{1,0:T(8,128)}, f32[4,5,256,128]{3,2,1,0:T(8,128)}, bf16[4,5,256,128]{3,2,1,0:T(8,128)(2,1)}, bf16[4,272,128]{2,1,0:T(8,128)(2,1)}) custom-call(bf16[640,1024]{1,0:T(8,128)(2,1)} %convolution_convert_fusion.1.qk_ref, bf16[640,1024]{1,0:T(8,128)(2,1)} %convolution_convert_fusion.value_ref, f32[640,512]{1,0:T(8,128)} %convolution_add_fusion.gate_ref), custom_call_target="tpu_custom_call" | custom-call | tf_op jit(solution)/shard_map/chunk_states/pallas_call | solution.py:313
  118.5 1.6 slice_bitcast_fusion.7
  120.1 2.4 collective-permute-start.13
  124.7 6.1 %collective-permute-done.13.refs_3_ = bf16[272,128]{1,0:T(8,128)(2,1)S(1)} collective-permute-done((bf16[272,128]{1,0:T(8,128)(2,1)S(1)}, bf16[272,128]{1,0:T(8,128)(2,1)S(1)}, u32[]{:S(2)}, u32[]{:S(2)}) %collective-permute-start.13) | collective-permute-done | bytes 69664 | tf_op jit(solution)/shard_map/ppermute | solution.py:465
  130.8 5.6 %collective-permute-done.12.refs_2_ = bf16[272,128]{1,0:T(8,128)(2,1)S(1)} collective-permute-done((bf16[272,128]{1,0:T(8,128)(2,1)S(1)}, bf16[272,128]{1,0:T(8,128)(2,1)S(1)}, u32[]{:S(2)}, u32[]{:S(2)}) %collective-permute-start.12) | collective-permute-done | bytes 69664 | tf_op jit(solution)/shard_map/ppermute | solution.py:465
  138.6 1.8 chain.4
  144.2 2.9 join.6
  147.7 1.8 chain.5
  149.5 2.0 collective-permute-start.16
  151.6 2.4 collective-permute-start.17
  154.0 4.6 %fusion.34.outgate_ref = f32[640,1024]{1,0:T(8,128)} fusion(bf16[640,1024]{1,0:T(8,128)(2,1)S(1)} %copy-done.8, bf16[1024,1024]{1,0:T(8,128)(2,1)} %join.6), kind=kOutput, calls=%fused_computation.167 | convolution fusion | flops 1342177280 | bytes 6029312 | tf_op jit(solution)/shard_map/dot_general | solution.py:27
  158.6 2.9 join.7
  161.6 2.1 collective-permute-done.16
  165.2 8.2 %mix.1 = (f32[640,1024]{1,0:T(8,128)}, bf16[640,1024]{1,0:T(8,128)(2,1)}) custom-call(s32[2,5]{1,0:T(2,128)} %add_convert_fusion.17.flags_ref, bf16[640,1024]{1,0:T(8,128)(2,1)} %convolution_convert_fusion.1.qk_ref, bf16[640,1024]{1,0:T(8,128)(2,1)} %convolution_convert_fusion.value_ref, f32[640,512]{1,0:T(8,128)} %get-tuple-element.99.sums_ref, ...), custom_call_target="tpu_custom_call" | custom-call | tf_op jit(solution)/shard_map/mix/pallas_call | solution.py:337
  173.4 4.0 multiply_reduce_fusion.2
  179.0 53.7 %feed_forward.1 = (f32[640,1024]{1,0:T(8,128)}, f32[640,1024]{1,0:T(8,128)}, bf16[8,4,1440,128]{3,2,1,0:T(8,128)(2,1)}, bf16[4,4,704,128]{3,2,1,0:T(8,128)(2,1)}, bf16[4,4,704,128]{3,2,1,0:T(8,128)(2,1)}) custom-call(s32[20]{0:T(128)} %stack.162.order_ref.back_ref, bf16[8,4,2112,128]{3,2,1,0:T(8,128)(2,1)} %bitcast.197, ...), custom_call_target="tpu_custom_call" | custom-call | tf_op jit(solution)/shard_map/feed_forward/pallas_call | solution.py:767
  232.9 3.1 multiply_reduce_fusion
  236.0 2.3 fusion.25
  238.3 3.1 fusion.35.d_gated_ref
  241.4 8.7 %gate_back.1 = (bf16[640,1024]{1,0:T(8,128)(2,1)}, bf16[640,1024]{1,0:T(8,128)(2,1)}, f32[4,1,256]{2,1,0:T(1,128)}, f32[4,5,256,128]{3,2,1,0:T(8,128)}, bf16[4,2...) custom-call(s32[2,5]{1,0:T(2,128)} %add_convert_fusion.17.flags_ref, f32[640,1024]{1,0:T(8,128)} %fusion.35.d_gated_ref, ...), custom_call_target="tpu_custom_call" | custom-call | tf_op jit(solution)/shard_map/gate_back/pallas_call | solution.py:362
  250.1 1.7 slice_bitcast_fusion.3
  253.3 1.7 collective-permute-start.21
  256.7 3.2 collective-permute-done.21.refs_2_
  259.9 2.1 collective-permute-done.20.refs_1_
  262.6 1.8 chain.6
  265.4 3.4 convolution_convert_fusion.5
  270.8 1.8 chain.7
  272.6 3.1 collective-permute-start.24
  275.7 2.0 collective-permute-start.25
  277.6 2.4 convolution_convert_fusion.4
  284.4 3.8 add_convert_fusion
  290.8 14.4 %mix_back.1 = (bf16[640,1024]{1,0:T(8,128)(2,1)}, bf16[640,1024]{1,0:T(8,128)(2,1)}, bf16[640,512]{1,0:T(8,128)(2,1)}) custom-call(s32[2,5]{1,0:T(2,128)} %add_convert_fusion.17.flags_ref, bf16[640,1024]{1,0:T(8,128)(2,1)} %get-tuple-element.122.d_mixed_ref, bf16[640,1024]{1,0:T(8,128)(2,1)} %convolution_convert_fusion.1.qk_ref, ...), custom_call_target="tpu_custom_call" | custom-call | tf_op jit(solution)/shard_map/mix_back/pallas_call | solution.py:400
  305.3 2.4 convolution_convert_fusion.3
  332.1 2.7 collective-permute-done.34
  335.9 5.9 %all-to-all-start = ((bf16[4,704,128]{2,1,0:T(8,128)(2,1)}), bf16[4,704,128]{2,1,0:T(8,128)(2,1)S(1)}, u32[]{:S(2)}, u32[]{:S(2)}) async-start(bf16[4,704,128]{2,1,0:T(8,128)(2,1)} %pad_maximum_fusion.5), calls=%async_computation | async-start | bytes 1441792 | tf_op jit(solution)/shard_map/all_to_all | solution.py:1136
  341.9 3.7 fusion.37
  347.5 3.2 add_add_fusion.d_normed_ref
  350.7 6.9 %finish.1 = (f32[640,1024]{1,0:T(8,128)}, f32[256,128]{1,0:T(8,128)}) custom-call(s32[20]{0:T(128)} %stack.162.order_ref.back_ref, f32[640,1024]{1,0:T(8,128)} %get-tuple-element.171.d_resid_ref, f32[640,1024]{1,0:T(8,128)} %add_add_fusion.d_normed_ref, bf16[640,1024]{1,0:T(8,128)(2,1)} %get-tuple-element.91.inputs_ref, ...), custom_call_target="tpu_custom_call" | custom-call | tf_op jit(solution)/shard_map/finish/pallas_call | solution.py:1113
  357.6 3.1 collective-permute-done.32
  362.4 3.9 collective-permute-start.35
  370.2 4.5 %output.1 = bf16[640,1024]{1,0:T(8,128)(2,1)} custom-call(s32[20]{0:T(128)} %stack.162.order_ref.back_ref, f32[640,1024]{1,0:T(8,128)} %copy-done, f32[640,1024]{1,0:T(8,128)} %get-tuple-element.114.feed_ref), custom_call_target="tpu_custom_call" | custom-call | tf_op jit(solution)/shard_map/output/pallas_call | solution.py:536
  374.7 1.8 collective-permute-start.37
  379.7 9.2 %collective-permute-done.37 = bf16[2048,128]{1,0:T(8,128)(2,1)S(1)} collective-permute-done((bf16[2048,128]{1,0:T(8,128)(2,1)}, bf16[2048,128]{1,0:T(8,128)(2,1)S(1)}, u32[]{:S(2)}, u32[]{:S(2)}) %collective-permute-start.37) | collective-permute-done | bytes 524320 | tf_op jit(solution)/shard_map/ppermute | solution.py:469
  392.3 2.8 collective-permute-start.42
  395.1 1.7 collective-permute-start.41
  399.0 15.3 %reduce-scatter.2.cloned.1.call-done = bf16[1,1440,128]{2,1,0:T(8,128)(2,1)} async-done(((bf16[32,1440,128]{2,1,0:T(8,128)(2,1)}), bf16[1,1440,128]{2,1,0:T(8,128)(2,1)}) %reduce-scatter.2.cloned.1.call-update) | async-done | bytes 368656 | tf_op jit(solution)/shard_map/reduce_scatter | solution.py:815
  416.3 2.7 collective-permute-done.42.refs_2_
  419.0 8.3 %collective-permute-done.41.refs_1_ = bf16[1280,128]{1,0:T(8,128)(2,1)S(1)} collective-permute-done((bf16[1280,128]{1,0:T(8,128)(2,1)}, bf16[1280,128]{1,0:T(8,128)(2,1)S(1)}, u32[]{:S(2)}, u32[]{:S(2)}) %collective-permute-start.41) | collective-permute-done | bytes 327712 | tf_op jit(solution)/shard_map/ppermute | solution.py:465
  428.7 2.2 last.1
  (262 shorter events, 81.9 us)
Async XLA Ops:
  7.2 171.8 %all-gather.3.cloned.1.call-start = ((), (), s32[]{:S(2)}) async-start(), calls=%async_computation.3 | async-start | bytes 17842176 | tf_op jit(solution)/shard_map/all_gather | solution.py:805
  9.4 404.9 %reduce-scatter.2.cloned.1.call-start = ((), (), s32[]{:S(2)}) async-start(), calls=%async_computation.2 | async-start | bytes 12165120 | tf_op jit(solution)/shard_map/reduce_scatter | solution.py:815
  9.5 37.3 %collective-permute-start.2 = (bf16[1024,128]{1,0:T(8,128)(2,1)}, bf16[1024,128]{1,0:T(8,128)(2,1)S(1)}, u32[]{:S(2)}, u32[]{:S(2)}) collective-permute-start(bf16[1024,128]{1,0:T(8,128)(2,1)} %get-tuple-element.93), channel_id=1, source_target_pairs={{0,3},{1,0},{2,1},{3,2},{4,7},{5,4},{6,5},{7,6},{8,11},{9,8},{10,9... | collective-permute-start | bytes 786440 | tf_op jit(solution)/shard_map/ppermute | solution.py:465
  10.0 36.7 %collective-permute-start.1 = (bf16[1024,128]{1,0:T(8,128)(2,1)}, bf16[1024,128]{1,0:T(8,128)(2,1)S(1)}, u32[]{:S(2)}, u32[]{:S(2)}) collective-permute-start(bf16[1024,128]{1,0:T(8,128)(2,1)} %get-tuple-element.93), channel_id=1, source_target_pairs={{0,2},{1,3},{2,0},{3,1},{4,6},{5,7},{6,4},{7,5},{8,10},{9,11},{10,... | collective-permute-start | bytes 786440 | tf_op jit(solution)/shard_map/ppermute | solution.py:465
  12.6 34.1 %collective-permute-start = (bf16[1024,128]{1,0:T(8,128)(2,1)}, bf16[1024,128]{1,0:T(8,128)(2,1)S(1)}, u32[]{:S(2)}, u32[]{:S(2)}) collective-permute-start(bf16[1024,128]{1,0:T(8,128)(2,1)} %get-tuple-element.93), channel_id=1, source_target_pairs={{0,1},{1,2},{2,3},{3,0},{4,5},{5,6},{6,7},{7,4},{8,9},{9,10},{10,1... | collective-permute-start | bytes 786440 | tf_op jit(solution)/shard_map/ppermute | solution.py:465
  19.6 9.0 %copy-start.28 = (bf16[1024,128]{1,0:T(8,128)(2,1)S(1)}, bf16[1024,128]{1,0:T(8,128)(2,1)}, u32[]{:S(2)}) copy-start(bf16[1024,128]{1,0:T(8,128)(2,1)} %get-tuple-element.93) | copy-start | bytes 786436
  46.9 50.7 %copy-start.54 = (bf16[256]{0:T(256)(128)(2,1)S(1)}, bf16[256]{0:T(256)(128)(2,1)}, u32[]{:S(2)}) copy-start(bf16[256]{0:T(256)(128)(2,1)} %param.28) | copy-start | bytes 1540
  46.9 51.9 %copy-start.48 = (s32[1,4]{1,0:T(1,128)S(1)}, s32[1,4]{1,0:T(1,128)}, u32[]{:S(2)}) copy-start(s32[1,4]{1,0:T(1,128)} %param.19) | copy-start | bytes 52
  47.0 20.7 %collective-permute-start.4 = (bf16[2048,128]{1,0:T(8,128)(2,1)S(1)}, bf16[2048,128]{1,0:T(8,128)(2,1)S(1)}, u32[]{:S(2)}, u32[]{:S(2)}) collective-permute-start(bf16[2048,128]{1,0:T(8,128)(2,1)S(1)} %get-tuple-element.228), channel_id=1, source_target_pairs={{0,4},{4,0},{1,5},{5,1},{2,6},{6,2},{3,7},{7,3},{8,12},{12,8},{9,1... | collective-permute-start | bytes 1572872 | tf_op jit(solution)/shard_map/ppermute | solution.py:469
  48.6 21.7 %collective-permute-start.3 = (bf16[2048,128]{1,0:T(8,128)(2,1)S(1)}, bf16[2048,128]{1,0:T(8,128)(2,1)S(1)}, u32[]{:S(2)}, u32[]{:S(2)}) collective-permute-start(bf16[2048,128]{1,0:T(8,128)(2,1)S(1)} %get-tuple-element.229), channel_id=1, source_target_pairs={{0,16},{16,0},{1,17},{17,1},{2,18},{18,2},{3,19},{19,3},{4,20},{20... | collective-permute-start | bytes 1572872 | tf_op jit(solution)/shard_map/ppermute | solution.py:469
  67.8 31.6 %copy-start.2 = (bf16[4096,128]{1,0:T(8,128)(2,1)}, bf16[4096,128]{1,0:T(8,128)(2,1)S(1)}, u32[]{:S(2)}) copy-start(bf16[4096,128]{1,0:T(8,128)(2,1)S(1)} %constant_dynamic-update-slice_fusion.25.refs_0_.refs_1_) | copy-start | bytes 3145732
  70.3 20.7 %collective-permute-start.8 = (bf16[4096,128]{1,0:T(8,128)(2,1)S(1)}, bf16[4096,128]{1,0:T(8,128)(2,1)S(1)}, u32[]{:S(2)}, u32[]{:S(2)}) collective-permute-start(bf16[4096,128]{1,0:T(8,128)(2,1)S(1)} %constant_dynamic-update-slice_fusion.25.refs_0_.refs_1_), channel_id=1, source_target_pairs={{0,16},{16,0},{1,17},{17,1},{2,18},{18,2},{3,19},{19,3},{4,20},{20... | collective-permute-start | bytes 3145736 | tf_op jit(solution)/shard_map/ppermute | solution.py:469
  70.6 31.9 %copy-start.1 = (bf16[4096,128]{1,0:T(8,128)(2,1)}, bf16[4096,128]{1,0:T(8,128)(2,1)S(1)}, u32[]{:S(2)}) copy-start(bf16[4096,128]{1,0:T(8,128)(2,1)S(1)} %constant_dynamic-update-slice_fusion.8.refs_0_.refs_1_) | copy-start | bytes 3145732
  70.6 27.0 %collective-permute-start.5 = (bf16[4096,128]{1,0:T(8,128)(2,1)S(1)}, bf16[4096,128]{1,0:T(8,128)(2,1)}, u32[]{:S(2)}, u32[]{:S(2)}) collective-permute-start(bf16[4096,128]{1,0:T(8,128)(2,1)S(1)} %constant_dynamic-update-slice_fusion.8.refs_0_.refs_1_), channel_id=1, source_target_pairs={{0,4},{4,0},{1,5},{5,1},{2,6},{6,2},{3,7},{7,3},{8,12},{12,8},{9,1... | collective-permute-start | bytes 3145736 | tf_op jit(solution)/shard_map/ppermute | solution.py:469
  70.9 28.5 %collective-permute-start.9 = (bf16[4096,128]{1,0:T(8,128)(2,1)S(1)}, bf16[4096,128]{1,0:T(8,128)(2,1)}, u32[]{:S(2)}, u32[]{:S(2)}) collective-permute-start(bf16[4096,128]{1,0:T(8,128)(2,1)S(1)} %constant_dynamic-update-slice_fusion.25.refs_0_.refs_1_), channel_id=1, source_target_pairs={{0,8},{8,0},{1,9},{9,1},{2,10},{10,2},{3,11},{11,3},{4,12},{12,4},... | collective-permute-start | bytes 3145736 | tf_op jit(solution)/shard_map/ppermute | solution.py:469
  91.0 8.5 %copy-start.3 = (bf16[4096,128]{1,0:T(8,128)(2,1)}, bf16[4096,128]{1,0:T(8,128)(2,1)S(1)}, u32[]{:S(2)}) copy-start(bf16[4096,128]{1,0:T(8,128)(2,1)S(1)} %collective-permute-done.8.refs_2_.refs_3_) | copy-start | bytes 3145732
  91.0 8.5 %collective-permute-start.10 = (bf16[4096,128]{1,0:T(8,128)(2,1)S(1)}, bf16[4096,128]{1,0:T(8,128)(2,1)}, u32[]{:S(2)}, u32[]{:S(2)}) collective-permute-start(bf16[4096,128]{1,0:T(8,128)(2,1)S(1)} %collective-permute-done.8.refs_2_.refs_3_), channel_id=1, source_target_pairs={{0,8},{8,0},{1,9},{9,1},{2,10},{10,2},{3,11},{11,3},{4,12},{12,4},... | collective-permute-start | bytes 3145736 | tf_op jit(solution)/shard_map/ppermute | solution.py:469
  91.0 11.5 %collective-permute-start.6 = (bf16[4096,128]{1,0:T(8,128)(2,1)S(1)}, bf16[4096,128]{1,0:T(8,128)(2,1)}, u32[]{:S(2)}, u32[]{:S(2)}) collective-permute-start(bf16[4096,128]{1,0:T(8,128)(2,1)S(1)} %constant_dynamic-update-slice_fusion.8.refs_0_.refs_1_), channel_id=1, source_target_pairs={{0,8},{8,0},{1,9},{9,1},{2,10},{10,2},{3,11},{11,3},{4,12},{12,4},... | collective-permute-start | bytes 3145736 | tf_op jit(solution)/shard_map/ppermute | solution.py:469
  97.6 4.9 %collective-permute-start.7 = (bf16[4096,128]{1,0:T(8,128)(2,1)}, bf16[4096,128]{1,0:T(8,128)(2,1)}, u32[]{:S(2)}, u32[]{:S(2)}) collective-permute-start(bf16[4096,128]{1,0:T(8,128)(2,1)} %collective-permute-done.5.refs_2_.refs_3_), channel_id=1, source_target_pairs={{0,8},{8,0},{1,9},{9,1},{2,10},{10,2},{3,11},{11,3},{4,12},{12,4},... | collective-permute-start | bytes 3145736 | tf_op jit(solution)/shard_map/ppermute | solution.py:469
  120.1 10.7 %collective-permute-start.13 = (bf16[272,128]{1,0:T(8,128)(2,1)S(1)}, bf16[272,128]{1,0:T(8,128)(2,1)S(1)}, u32[]{:S(2)}, u32[]{:S(2)}) collective-permute-start(bf16[272,128]{1,0:T(8,128)(2,1)S(1)} %get-tuple-element.222), channel_id=1, source_target_pairs={{0,1},{1,2},{2,3},{3,0},{4,5},{5,6},{6,7},{7,4},{8,9},{9,10},{10,1... | collective-permute-start | bytes 208904 | tf_op jit(solution)/shard_map/ppermute | solution.py:465
  122.6 13.8 %collective-permute-start.12 = (bf16[272,128]{1,0:T(8,128)(2,1)S(1)}, bf16[272,128]{1,0:T(8,128)(2,1)S(1)}, u32[]{:S(2)}, u32[]{:S(2)}) collective-permute-start(bf16[272,128]{1,0:T(8,128)(2,1)S(1)} %get-tuple-element.223), channel_id=1, source_target_pairs={{0,2},{1,3},{2,0},{3,1},{4,6},{5,7},{6,4},{7,5},{8,10},{9,11},{10,... | collective-permute-start | bytes 208904 | tf_op jit(solution)/shard_map/ppermute | solution.py:465
  122.6 15.3 %collective-permute-start.11 = (bf16[272,128]{1,0:T(8,128)(2,1)S(1)}, bf16[272,128]{1,0:T(8,128)(2,1)S(1)}, u32[]{:S(2)}, u32[]{:S(2)}) collective-permute-start(bf16[272,128]{1,0:T(8,128)(2,1)S(1)} %get-tuple-element.224), channel_id=1, source_target_pairs={{0,3},{1,0},{2,1},{3,2},{4,7},{5,4},{6,5},{7,6},{8,11},{9,8},{10,9... | collective-permute-start | bytes 208904 | tf_op jit(solution)/shard_map/ppermute | solution.py:465
  130.8 7.7 %copy-start.33 = (bf16[272,128]{1,0:T(8,128)(2,1)}, bf16[272,128]{1,0:T(8,128)(2,1)S(1)}, u32[]{:S(2)}) copy-start(bf16[272,128]{1,0:T(8,128)(2,1)S(1)} %collective-permute-done.13.refs_3_) | copy-start | bytes 208900
  140.4 6.7 %collective-permute-start.14 = (bf16[256,128]{1,0:T(8,128)(2,1)}, bf16[256,128]{1,0:T(8,128)(2,1)S(1)}, u32[]{:S(2)}, u32[]{:S(2)}) collective-permute-start(bf16[256,128]{1,0:T(8,128)(2,1)} %get-tuple-element.102), channel_id=1, source_target_pairs={{0,4},{4,0},{1,5},{5,1},{2,6},{6,2},{3,7},{7,3},{8,12},{12,8},{9,1... | collective-permute-start | bytes 196616 | tf_op jit(solution)/shard_map/ppermute | solution.py:469
  142.8 21.6 %collective-permute-start.18 = (bf16[4,256,128]{2,1,0:T(8,128)(2,1)S(1)}, bf16[4,256,128]{2,1,0:T(8,128)(2,1)S(1)}, u32[]{:S(2)}, u32[]{:S(2)}) collective-permute-start(bf16[4,256,128]{2,1,0:T(8,128)(2,1)S(1)} %slice_bitcast_fusion.2), channel_id=1, source_target_pairs={{1,0},{3,2},{5,4},{7,6},{9,8},{11,10},{13,12},{15,14},{17,16},{19,... | collective-permute-start | bytes 786440 | tf_op jit(solution)/shard_map/ppermute | solution.py:488
  149.5 12.0 %collective-permute-start.15 = (bf16[256,128]{1,0:T(8,128)(2,1)}, bf16[256,128]{1,0:T(8,128)(2,1)S(1)}, u32[]{:S(2)}, u32[]{:S(2)}) collective-permute-start(bf16[256,128]{1,0:T(8,128)(2,1)} %get-tuple-element.104), channel_id=1, source_target_pairs={{0,1},{1,2},{2,3},{3,0},{4,5},{5,6},{6,7},{7,4},{8,9},{9,10},{10,1... | collective-permute-start | bytes 196616 | tf_op jit(solution)/shard_map/ppermute | solution.py:465
  149.5 14.2 %collective-permute-start.16 = (bf16[256,128]{1,0:T(8,128)(2,1)}, bf16[256,128]{1,0:T(8,128)(2,1)S(1)}, u32[]{:S(2)}, u32[]{:S(2)}) collective-permute-start(bf16[256,128]{1,0:T(8,128)(2,1)} %get-tuple-element.105), channel_id=1, source_target_pairs={{0,2},{1,3},{2,0},{3,1},{4,6},{5,7},{6,4},{7,5},{8,10},{9,11},{10,... | collective-permute-start | bytes 196616 | tf_op jit(solution)/shard_map/ppermute | solution.py:465
  151.6 12.1 %collective-permute-start.17 = (bf16[256,128]{1,0:T(8,128)(2,1)}, bf16[256,128]{1,0:T(8,128)(2,1)S(1)}, u32[]{:S(2)}, u32[]{:S(2)}) collective-permute-start(bf16[256,128]{1,0:T(8,128)(2,1)} %get-tuple-element.106), channel_id=1, source_target_pairs={{0,3},{1,0},{2,1},{3,2},{4,7},{5,4},{6,5},{7,6},{8,11},{9,8},{10,9... | collective-permute-start | bytes 196616 | tf_op jit(solution)/shard_map/ppermute | solution.py:465
  177.4 58.6 %copy-start = (f32[640,1024]{1,0:T(8,128)}, f32[640,1024]{1,0:T(8,128)S(1)}, u32[]{:S(2)}) copy-start(f32[640,1024]{1,0:T(8,128)S(1)} %get-tuple-element.260.resid_ref) | copy-start | bytes 7864324
  232.7 51.6 %collective-permute-start.19 = (bf16[4,4,704,128]{3,2,1,0:T(8,128)(2,1)}, bf16[4,4,704,128]{3,2,1,0:T(8,128)(2,1)}, u32[]{:S(2)}, u32[]{:S(2)}) collective-permute-start(bf16[4,4,704,128]{3,2,1,0:T(8,128)(2,1)} %get-tuple-element.121), channel_id=1, source_target_pairs={{0,8},{8,0},{1,9},{9,1},{2,10},{10,2},{3,11},{11,3},{4,12},{12,4},... | collective-permute-start | bytes 8650760 | tf_op jit(solution)/shard_map/ppermute | solution.py:469
  241.4 24.1 %copy-start.19 = (bf16[640,1024]{1,0:T(8,128)(2,1)S(1)}, bf16[640,1024]{1,0:T(8,128)(2,1)}, u32[]{:S(2)}) copy-start(bf16[640,1024]{1,0:T(8,128)(2,1)} %copy-done.18) | copy-start | bytes 3932164
  251.8 5.0 %collective-permute-start.22 = (bf16[272,128]{1,0:T(8,128)(2,1)S(1)}, bf16[272,128]{1,0:T(8,128)(2,1)S(1)}, u32[]{:S(2)}, u32[]{:S(2)}) collective-permute-start(bf16[272,128]{1,0:T(8,128)(2,1)S(1)} %get-tuple-element.218), channel_id=1, source_target_pairs={{0,1},{1,2},{2,3},{3,0},{4,5},{5,6},{6,7},{7,4},{8,9},{9,10},{10,1... | collective-permute-start | bytes 208904 | tf_op jit(solution)/shard_map/ppermute | solution.py:465
  253.3 6.6 %collective-permute-start.21 = (bf16[272,128]{1,0:T(8,128)(2,1)S(1)}, bf16[272,128]{1,0:T(8,128)(2,1)S(1)}, u32[]{:S(2)}, u32[]{:S(2)}) collective-permute-start(bf16[272,128]{1,0:T(8,128)(2,1)S(1)} %get-tuple-element.219), channel_id=1, source_target_pairs={{0,2},{1,3},{2,0},{3,1},{4,6},{5,7},{6,4},{7,5},{8,10},{9,11},{10,... | collective-permute-start | bytes 208904 | tf_op jit(solution)/shard_map/ppermute | solution.py:465
  255.0 7.0 %collective-permute-start.20 = (bf16[272,128]{1,0:T(8,128)(2,1)S(1)}, bf16[272,128]{1,0:T(8,128)(2,1)S(1)}, u32[]{:S(2)}, u32[]{:S(2)}) collective-permute-start(bf16[272,128]{1,0:T(8,128)(2,1)S(1)} %get-tuple-element.220), channel_id=1, source_target_pairs={{0,3},{1,0},{2,1},{3,2},{4,7},{5,4},{6,5},{7,6},{8,11},{9,8},{10,9... | collective-permute-start | bytes 208904 | tf_op jit(solution)/shard_map/ppermute | solution.py:465
  264.4 13.2 %copy-start.9 = (bf16[640,1024]{1,0:T(8,128)(2,1)S(1)}, bf16[640,1024]{1,0:T(8,128)(2,1)}, u32[]{:S(2)}) copy-start(bf16[640,1024]{1,0:T(8,128)(2,1)} %get-tuple-element.92) | copy-start | bytes 3932164
  264.4 5.7 %collective-permute-start.23 = (bf16[256,128]{1,0:T(8,128)(2,1)}, bf16[256,128]{1,0:T(8,128)(2,1)S(1)}, u32[]{:S(2)}, u32[]{:S(2)}) collective-permute-start(bf16[256,128]{1,0:T(8,128)(2,1)} %get-tuple-element.125), channel_id=1, source_target_pairs={{0,4},{4,0},{1,5},{5,1},{2,6},{6,2},{3,7},{7,3},{8,12},{12,8},{9,1... | collective-permute-start | bytes 196616 | tf_op jit(solution)/shard_map/ppermute | solution.py:469
  268.8 14.8 %collective-permute-start.27 = (bf16[4,256,128]{2,1,0:T(8,128)(2,1)S(1)}, bf16[4,256,128]{2,1,0:T(8,128)(2,1)S(1)}, u32[]{:S(2)}, u32[]{:S(2)}) collective-permute-start(bf16[4,256,128]{2,1,0:T(8,128)(2,1)S(1)} %copy-done.53), channel_id=1, source_target_pairs={{0,1},{2,3},{4,5},{6,7},{8,9},{10,11},{12,13},{14,15},{16,17},{18,... | collective-permute-start | bytes 786440 | tf_op jit(solution)/shard_map/ppermute | solution.py:490
  272.6 8.7 %collective-permute-start.24 = (bf16[256,128]{1,0:T(8,128)(2,1)}, bf16[256,128]{1,0:T(8,128)(2,1)S(1)}, u32[]{:S(2)}, u32[]{:S(2)}) collective-permute-start(bf16[256,128]{1,0:T(8,128)(2,1)} %get-tuple-element.127), channel_id=1, source_target_pairs={{0,1},{1,2},{2,3},{3,0},{4,5},{5,6},{6,7},{7,4},{8,9},{9,10},{10,1... | collective-permute-start | bytes 196616 | tf_op jit(solution)/shard_map/ppermute | solution.py:465
  275.7 5.8 %collective-permute-start.25 = (bf16[256,128]{1,0:T(8,128)(2,1)}, bf16[256,128]{1,0:T(8,128)(2,1)S(1)}, u32[]{:S(2)}, u32[]{:S(2)}) collective-permute-start(bf16[256,128]{1,0:T(8,128)(2,1)} %get-tuple-element.128), channel_id=1, source_target_pairs={{0,2},{1,3},{2,0},{3,1},{4,6},{5,7},{6,4},{7,5},{8,10},{9,11},{10,... | collective-permute-start | bytes 196616 | tf_op jit(solution)/shard_map/ppermute | solution.py:465
  277.6 5.2 %collective-permute-start.26 = (bf16[256,128]{1,0:T(8,128)(2,1)}, bf16[256,128]{1,0:T(8,128)(2,1)S(1)}, u32[]{:S(2)}, u32[]{:S(2)}) collective-permute-start(bf16[256,128]{1,0:T(8,128)(2,1)} %get-tuple-element.129), channel_id=1, source_target_pairs={{0,3},{1,0},{2,1},{3,2},{4,7},{5,4},{6,5},{7,6},{8,11},{9,8},{10,9... | collective-permute-start | bytes 196616 | tf_op jit(solution)/shard_map/ppermute | solution.py:465
  289.7 28.0 %collective-permute-start.30 = (bf16[2,2,704,128]{3,2,1,0:T(8,128)(2,1)}, bf16[2,2,704,128]{3,2,1,0:T(8,128)(2,1)}, u32[]{:S(2)}, u32[]{:S(2)}) collective-permute-start(bf16[2,2,704,128]{3,2,1,0:T(8,128)(2,1)} %get-tuple-element.179), channel_id=1, source_target_pairs={{0,16},{16,0},{1,17},{17,1},{2,18},{18,2},{3,19},{19,3},{4,20},{20... | collective-permute-start | bytes 2162696 | tf_op jit(solution)/shard_map/ppermute | solution.py:469
  290.2 24.4 %collective-permute-start.29 = (bf16[2,2,704,128]{3,2,1,0:T(8,128)(2,1)}, bf16[2,2,704,128]{3,2,1,0:T(8,128)(2,1)}, u32[]{:S(2)}, u32[]{:S(2)}) collective-permute-start(bf16[2,2,704,128]{3,2,1,0:T(8,128)(2,1)} %get-tuple-element.261), channel_id=1, source_target_pairs={{0,4},{4,0},{1,5},{5,1},{2,6},{6,2},{3,7},{7,3},{8,12},{12,8},{9,1... | collective-permute-start | bytes 2162696 | tf_op jit(solution)/shard_map/ppermute | solution.py:469
  307.8 12.6 %collective-permute-start.28 = (bf16[2048,512]{1,0:T(8,128)(2,1)S(1)}, bf16[2048,512]{1,0:T(8,128)(2,1)S(1)}, u32[]{:S(2)}, u32[]{:S(2)}) collective-permute-start(bf16[2048,512]{1,0:T(8,128)(2,1)S(1)} %pad_maximum_fusion), channel_id=1, source_target_pairs={{0,8},{8,0},{1,9},{9,1},{2,10},{10,2},{3,11},{11,3},{4,12},{12,4},... | collective-permute-start | bytes 6291464 | tf_op jit(solution)/shard_map/ppermute | solution.py:469
  310.3 16.5 %collective-permute-start.31 = (bf16[2048,512]{1,0:T(8,128)(2,1)S(1)}, bf16[2048,512]{1,0:T(8,128)(2,1)S(1)}, u32[]{:S(2)}, u32[]{:S(2)}) collective-permute-start(bf16[2048,512]{1,0:T(8,128)(2,1)S(1)} %pad_maximum_fusion.1), channel_id=1, source_target_pairs={{0,8},{8,0},{1,9},{9,1},{2,10},{10,2},{3,11},{11,3},{4,12},{12,4},... | collective-permute-start | bytes 6291464 | tf_op jit(solution)/shard_map/ppermute | solution.py:469
  314.6 5.9 %copy-start.50 = (bf16[640,1024]{1,0:T(8,128)(2,1)S(1)}, bf16[640,1024]{1,0:T(8,128)(2,1)}, u32[]{:S(2)}) copy-start(bf16[640,1024]{1,0:T(8,128)(2,1)} %get-tuple-element.142) | copy-start | bytes 3932164
  316.0 18.8 %collective-permute-start.33 = (bf16[2,704,128]{2,1,0:T(8,128)(2,1)S(1)}, bf16[2,704,128]{2,1,0:T(8,128)(2,1)S(1)}, u32[]{:S(2)}, u32[]{:S(2)}) collective-permute-start(bf16[2,704,128]{2,1,0:T(8,128)(2,1)S(1)} %get-tuple-element.175), channel_id=1, source_target_pairs={{0,16},{16,0},{1,17},{17,1},{2,18},{18,2},{3,19},{19,3},{4,20},{20... | collective-permute-start | bytes 1081352 | tf_op jit(solution)/shard_map/ppermute | solution.py:469
  318.9 15.8 %collective-permute-start.34 = (bf16[2,704,128]{2,1,0:T(8,128)(2,1)S(1)}, bf16[2,704,128]{2,1,0:T(8,128)(2,1)S(1)}, u32[]{:S(2)}, u32[]{:S(2)}) collective-permute-start(bf16[2,704,128]{2,1,0:T(8,128)(2,1)S(1)} %get-tuple-element.177), channel_id=1, source_target_pairs={{0,4},{4,0},{1,5},{5,1},{2,6},{6,2},{3,7},{7,3},{8,12},{12,8},{9,1... | collective-permute-start | bytes 1081352 | tf_op jit(solution)/shard_map/ppermute | solution.py:469
  326.2 34.4 %collective-permute-start.32 = (bf16[2048,256]{1,0:T(8,128)(2,1)}, bf16[2048,256]{1,0:T(8,128)(2,1)}, u32[]{:S(2)}, u32[]{:S(2)}) collective-permute-start(bf16[2048,256]{1,0:T(8,128)(2,1)} %maximum_maximum_fusion), channel_id=1, source_target_pairs={{0,4},{4,0},{1,5},{5,1},{2,6},{6,2},{3,7},{7,3},{8,12},{12,8},{9,1... | collective-permute-start | bytes 3145736 | tf_op jit(solution)/shard_map/ppermute | solution.py:469
  331.6 34.6 %collective-permute-start.36 = (bf16[2048,256]{1,0:T(8,128)(2,1)}, bf16[2048,256]{1,0:T(8,128)(2,1)}, u32[]{:S(2)}, u32[]{:S(2)}) collective-permute-start(bf16[2048,256]{1,0:T(8,128)(2,1)} %pad_maximum_fusion.2), channel_id=1, source_target_pairs={{0,16},{16,0},{1,17},{17,1},{2,18},{18,2},{3,19},{19,3},{4,20},{20... | collective-permute-start | bytes 3145736 | tf_op jit(solution)/shard_map/ppermute | solution.py:469
  335.9 40.5 %all-to-all-start = ((bf16[4,704,128]{2,1,0:T(8,128)(2,1)}), bf16[4,704,128]{2,1,0:T(8,128)(2,1)S(1)}, u32[]{:S(2)}, u32[]{:S(2)}) async-start(bf16[4,704,128]{2,1,0:T(8,128)(2,1)} %pad_maximum_fusion.5), calls=%async_computation | async-start | bytes 1441792 | tf_op jit(solution)/shard_map/all_to_all | solution.py:1136
  350.7 10.0 %copy-start.24 = (bf16[1024,128]{1,0:T(8,128)(2,1)S(1)}, bf16[1024,128]{1,0:T(8,128)(2,1)}, u32[]{:S(2)}) copy-start(bf16[1024,128]{1,0:T(8,128)(2,1)} %get-tuple-element.196) | copy-start | bytes 786436
  350.7 10.0 %copy-start.25 = (bf16[1024,128]{1,0:T(8,128)(2,1)S(1)}, bf16[1024,128]{1,0:T(8,128)(2,1)}, u32[]{:S(2)}) copy-start(bf16[1024,128]{1,0:T(8,128)(2,1)} %get-tuple-element.197) | copy-start | bytes 786436
  350.7 10.0 %copy-start.26 = (bf16[1024,128]{1,0:T(8,128)(2,1)S(1)}, bf16[1024,128]{1,0:T(8,128)(2,1)}, u32[]{:S(2)}) copy-start(bf16[1024,128]{1,0:T(8,128)(2,1)} %get-tuple-element.192) | copy-start | bytes 786436
  350.7 10.0 %copy-start.27 = (bf16[1024,128]{1,0:T(8,128)(2,1)S(1)}, bf16[1024,128]{1,0:T(8,128)(2,1)}, u32[]{:S(2)}) copy-start(bf16[1024,128]{1,0:T(8,128)(2,1)} %get-tuple-element.193) | copy-start | bytes 786436
  362.4 16.5 %collective-permute-start.35 = (bf16[2048,128]{1,0:T(8,128)(2,1)S(1)}, bf16[2048,128]{1,0:T(8,128)(2,1)S(1)}, u32[]{:S(2)}, u32[]{:S(2)}) collective-permute-start(bf16[2048,128]{1,0:T(8,128)(2,1)S(1)} %get-tuple-element.191), channel_id=1, source_target_pairs={{0,16},{16,0},{1,17},{17,1},{2,18},{18,2},{3,19},{19,3},{4,20},{20... | collective-permute-start | bytes 1572872 | tf_op jit(solution)/shard_map/ppermute | solution.py:469
  368.7 1.3 collective-permute-start.38
  370.1 6.4 %collective-permute-start.39 = (f32[256,128]{1,0:T(8,128)S(1)}, f32[256,128]{1,0:T(8,128)}, u32[]{:S(2)}, u32[]{:S(2)}) collective-permute-start(f32[256,128]{1,0:T(8,128)S(1)} %add.318), channel_id=1, source_target_pairs={{0,4},{4,0},{1,5},{5,1},{2,6},{6,2},{3,7},{7,3},{8,12},{12,8},{9,1... | collective-permute-start | bytes 393224 | tf_op jit(solution)/shard_map/ppermute | solution.py:469
  374.7 14.2 %collective-permute-start.37 = (bf16[2048,128]{1,0:T(8,128)(2,1)}, bf16[2048,128]{1,0:T(8,128)(2,1)S(1)}, u32[]{:S(2)}, u32[]{:S(2)}) collective-permute-start(bf16[2048,128]{1,0:T(8,128)(2,1)} %get-tuple-element.185), channel_id=1, source_target_pairs={{0,4},{4,0},{1,5},{5,1},{2,6},{6,2},{3,7},{7,3},{8,12},{12,8},{9,1... | collective-permute-start | bytes 1572872 | tf_op jit(solution)/shard_map/ppermute | solution.py:469
  377.4 13.6 %collective-permute-start.40 = (f32[256,128]{1,0:T(8,128)S(1)}, f32[256,128]{1,0:T(8,128)S(1)}, u32[]{:S(2)}, u32[]{:S(2)}) collective-permute-start(f32[256,128]{1,0:T(8,128)S(1)} %add.319), channel_id=1, source_target_pairs={{0,16},{16,0},{1,17},{17,1},{2,18},{18,2},{3,19},{19,3},{4,20},{20... | collective-permute-start | bytes 393224 | tf_op jit(solution)/shard_map/ppermute | solution.py:469
  392.3 35.0 %copy-start.29 = (bf16[1280,128]{1,0:T(8,128)(2,1)}, bf16[1280,128]{1,0:T(8,128)(2,1)S(1)}, u32[]{:S(2)}) copy-start(bf16[1280,128]{1,0:T(8,128)(2,1)S(1)} %get-tuple-element.154.refs_0_) | copy-start | bytes 983044
  392.3 26.7 %collective-permute-start.42 = (bf16[1280,128]{1,0:T(8,128)(2,1)S(1)}, bf16[1280,128]{1,0:T(8,128)(2,1)S(1)}, u32[]{:S(2)}, u32[]{:S(2)}) collective-permute-start(bf16[1280,128]{1,0:T(8,128)(2,1)S(1)} %get-tuple-element.254), channel_id=1, source_target_pairs={{0,2},{1,3},{2,0},{3,1},{4,6},{5,7},{6,4},{7,5},{8,10},{9,11},{10,... | collective-permute-start | bytes 983048 | tf_op jit(solution)/shard_map/ppermute | solution.py:465
  395.1 32.2 %collective-permute-start.41 = (bf16[1280,128]{1,0:T(8,128)(2,1)}, bf16[1280,128]{1,0:T(8,128)(2,1)S(1)}, u32[]{:S(2)}, u32[]{:S(2)}) collective-permute-start(bf16[1280,128]{1,0:T(8,128)(2,1)} %get-tuple-element.255), channel_id=1, source_target_pairs={{0,3},{1,0},{2,1},{3,2},{4,7},{5,4},{6,5},{7,6},{8,11},{9,8},{10,9... | collective-permute-start | bytes 983048 | tf_op jit(solution)/shard_map/ppermute | solution.py:465
  396.7 30.5 %collective-permute-start.43 = (bf16[1280,128]{1,0:T(8,128)(2,1)}, bf16[1280,128]{1,0:T(8,128)(2,1)S(1)}, u32[]{:S(2)}, u32[]{:S(2)}) collective-permute-start(bf16[1280,128]{1,0:T(8,128)(2,1)} %get-tuple-element.168), channel_id=1, source_target_pairs={{0,1},{1,2},{2,3},{3,0},{4,5},{5,6},{6,7},{7,4},{8,9},{9,10},{10,1... | collective-permute-start | bytes 983048 | tf_op jit(solution)/shard_map/ppermute | solution.py:465
  419.0 8.3 %copy-start.30 = (bf16[1280,128]{1,0:T(8,128)(2,1)}, bf16[1280,128]{1,0:T(8,128)(2,1)S(1)}, u32[]{:S(2)}) copy-start(bf16[1280,128]{1,0:T(8,128)(2,1)S(1)} %collective-permute-done.42.refs_2_) | copy-start | bytes 983044
  (38 other events, 106.0 us)
Sparse Core Ops, SparseCore 0:
  10.8 151.4 all-gather.2
  233.0 181.3 reduce-scatter.1
